TPU v7x, 32 devices: a whole 2x2x4 slice. The times are simulated.
32 devices in a mesh: ep: 8 (over z, x), et: 4 (over y, core).
Axes of the slice: x: 2, y: 2, z: 4, core: 2. Of those that a mesh axis runs over, the one named last changes fastest.
Arguments:
- out_grad: bfloat16 [1024, 7168], P('ep', 'et'), may hold values from -0.1796875 to 0.1796875
- gate_weights: bfloat16 [1024, 8], P('ep'), may hold values from 0.049804688 to 1
- routes: int32 [1024, 8], P('ep'), may hold values from 0 to 7, as said below
- gate_pre: bfloat16 [8, 1024, 1024], P('ep', None, 'et'), may hold values from -6 to 6
- up_pre: bfloat16 [8, 1024, 1024], P('ep', None, 'et'), may hold values from -6 to 6
- down_weight: bfloat16 [8, 1024, 7168], P('ep', None, 'et'), may hold values from -0.1875 to 0.1875
Outputs:
- d_down_weight: bfloat16 [8, 1024, 7168], P('ep', None, 'et')
- d_gate: float32 [1024, 8], P('ep')
Inputs may be any that keep to these rules, and one draw needn't show every extreme that they name: The experts in one row of routes differ. Among the rows of one source (one index of ep), at most 128 pairs name the same expert, and one expert is named by exactly 128 pairs of every source.
All inputs are finite; a program needn't handle non-finite values.
Results may differ from a plain program's by a relative error of at most 0.0057.
Values may be sent and summed in bfloat16 or wider, within the bound.
No kernel may reach another device: no remote copies, remote signals or barrier semaphores. Data moves between devices by JAX's collectives and lax.ppermute only.
A program may use at most 64 MiB of HBM per device.

v0:
```python
import jax
import jax.numpy as jnp
from jax import lax
from jax.sharding import PartitionSpec as P


def local(out_grad, gate_weights, routes, gate_pre, up_pre, down_weight):
    tok_rows, topk = routes.shape
    experts = lax.axis_size("ep")
    slot_total = gate_pre.shape[1]
    capacity = slot_total // experts
    flat_route = routes.reshape(-1)
    pair_count = tok_rows * topk
    onehot = (flat_route[:, None] == jnp.arange(experts, dtype=jnp.int32)[None, :]).astype(
        jnp.int32
    )
    ranks = jnp.sum(jnp.cumsum(onehot, axis=0) * onehot, axis=1) - 1
    slot_of = flat_route * capacity + ranks
    pair_ids = jnp.arange(pair_count, dtype=jnp.int32)
    slot_pair = jnp.zeros((experts * capacity,), jnp.int32).at[slot_of].set(pair_ids)
    filled = jnp.zeros((experts * capacity,), jnp.bool_).at[slot_of].set(True)
    send_rows = jnp.where(filled[:, None], out_grad[slot_pair // topk], 0.0)
    send_rows = send_rows.reshape(experts, capacity, out_grad.shape[1])
    send_gates = jnp.where(filled, gate_weights.reshape(-1)[slot_pair], 0.0)
    send_gates = send_gates.reshape(experts, capacity)
    rows_in, gates_in = (
        lax.all_to_all(send_rows, "ep", split_axis=0, concat_axis=0, tiled=True),
        lax.all_to_all(send_gates, "ep", split_axis=0, concat_axis=0, tiled=True),
    )
    rows_in = rows_in.reshape(slot_total, out_grad.shape[1])
    gates_in = gates_in.reshape(slot_total)
    weight = down_weight[0]
    hidden_part = (
        jax.nn.silu(gate_pre[0].astype(jnp.float32)) * up_pre[0].astype(jnp.float32)
    ).astype(jnp.bfloat16)
    scaled = (gates_in.astype(jnp.float32)[:, None] * rows_in.astype(jnp.float32)).astype(
        jnp.bfloat16
    )
    piece = lax.all_gather(hidden_part, "et", axis=1, tiled=True)
    expert_out = jnp.dot(piece, weight, preferred_element_type=jnp.float32)
    block = lax.dot_general(
        piece, scaled, (((0,), (0,)), ((), ())), preferred_element_type=jnp.float32
    )
    grad_weight = block
    expert_out, grad_weight = (expert_out, grad_weight)
    partial_grad = jnp.sum(rows_in.astype(jnp.float32) * expert_out, axis=1)
    slot_grad = lax.psum(partial_grad, "et")
    returned = lax.all_to_all(
        slot_grad.reshape(experts, capacity), "ep", split_axis=0, concat_axis=0, tiled=True
    )
    d_gate = returned.reshape(-1)[slot_of].reshape(tok_rows, topk)
    return (grad_weight.astype(jnp.bfloat16)[None], d_gate)


def solution(mesh):
    in_specs = (
        P("ep", "et"),
        P("ep", None),
        P("ep", None),
        P("ep", None, "et"),
        P("ep", None, "et"),
        P("ep", None, "et"),
    )
    out_specs = (P("ep", None, "et"), P("ep", None))
    return jax.shard_map(local, mesh=mesh, in_specs=in_specs, out_specs=out_specs, check_vma=False)
```

profile of v0, /device:TPU:0, one launch (start us, length us, event | category | flops | bytes accessed | tf_op | source)
XLA Modules:
  0.0 173.0 jit_solution(15346934507952092839)
XLA Ops:
  7.2 0.0 copy-start
  7.2 0.8 copy.14
  8.0 0.1 eq.29
  8.1 0.1 eq.25
  8.2 0.7 broadcast_multiply_fusion
  8.9 2.3 %reduce-window.6 = s32[8,8,128]{2,1,0:T(8,128)S(1)} reduce-window(s32[8,8,128]{2,1,0:T(8,128)S(1)} %fusion.15, s32[]{:T(128)} %constant.30.clone.1), window={size=1x1x128 pad=0_0x0_0x127_0}, to_apply=%region_0.0 | reduce-window | flops 1040384 | bytes 65540 | tf_op jit(solution)/shard_map/reduce-window
  11.2 0.3 slice_reduce_fusion
  11.4 0.2 reduce-window.9
  11.6 0.1 add_bitcast_fusion
  11.7 0.1 copy.13
  11.8 0.1 mul.37
  12.0 4.3 %scatter_custom_fusion.1 = s32[1024]{0:T(1024)S(1)} fusion(s32[1024]{0:T(1024)S(1)} %bitcast.41, s32[1024]{0:T(1024)S(1)} %iota.11, s32[]{:T(128)} %constant.30.clone.1), kind=kCustom, calls=%fused_computation.43 | custom fusion | bytes 4100 | tf_op jit(solution)/shard_map/scatter | solution.py:20
  16.3 0.8 copy.16
  17.1 0.1 reshape.98
  17.2 4.3 %scatter_custom_fusion = pred[1024]{0:T(1024)(128)(4,1)S(1)} fusion(s32[1024]{0:T(1024)S(1)} %bitcast.42, pred[1024]{0:T(1024)(128)(4,1)S(1)} %broadcast.83, pred[]{:T(512)} %constant.28.clone.1), kind=kCustom, calls=%fused_computation.47 | custom fusion | bytes 1025 | tf_op jit(solution)/shard_map/scatter | solution.py:21
  21.6 6.8 %gather_fusion = bf16[1024]{0:T(1024)(128)(2,1)S(1)} fusion(bf16[1024]{0:T(1024)(128)(2,1)S(1)} %reshape.98, s32[1024]{0:T(1024)S(1)} %get-tuple-element.6), kind=kCustom, calls=%fused_computation | custom fusion | bytes 8192 | tf_op jit(solution)/shard_map/gather | solution.py:24
  28.4 0.6 copy.17
  29.0 7.3 %all-to-all-start = ((bf16[8,1,128]{2,1,0:T(2,128)(2,1)}), bf16[8,1,128]{2,1,0:T(2,128)(2,1)S(1)}, u32[]{:S(2)}, u32[]{:S(2)}) async-start(bf16[8,1,128]{2,1,0:T(2,128)(2,1)} %copy.17), calls=%async_computation | async-start | bytes 8192 | tf_op jit(solution)/shard_map/all_to_all | solution.py:28
  36.2 0.0 copy-done
  36.2 5.8 %gather_fusion.1 = bf16[1024,1792]{1,0:T(8,128)(2,1)} fusion(bf16[128,1792]{1,0:T(8,128)(2,1)S(1)} %copy-done, s32[1024]{0:T(1024)S(1)} %get-tuple-element.7), kind=kCustom, calls=%fused_computation.1 | custom fusion | bytes 7344128 | tf_op jit(solution)/shard_map/gather | solution.py:22
  42.0 4.2 %broadcast_select_fusion = bf16[8,128,1792]{2,1,0:T(8,128)(2,1)} fusion(bf16[8,128,1792]{2,1,0:T(8,128)(2,1)} %bitcast.40, pred[8,128]{1,0:T(8,128)(4,1)S(1)} %bitcast.48), kind=kLoop, calls=%fused_computation.12 | loop fusion | flops 1835008 | bytes 7341056 | tf_op jit(solution)/shard_map/jit(_where)/select_n | solution.py:22
  46.2 0.0 copy-start.1
  46.2 0.0 copy-start.2
  46.2 0.0 all-to-all-done
  46.2 6.1 %all-to-all-start.1 = ((bf16[8,128,1792]{2,1,0:T(8,128)(2,1)}), bf16[8,128,1792]{2,1,0:T(8,128)(2,1)}, u32[]{:S(2)}, u32[]{:S(2)}) async-start(bf16[8,128,1792]{2,1,0:T(8,128)(2,1)} %broadcast_select_fusion), calls=%async_computation.1 | async-start | bytes 7340032 | tf_op jit(solution)/shard_map/all_to_all | solution.py:27
  52.4 0.0 all-gather.2.cloned.1.call-start
  52.4 0.0 copy-done.1
  52.4 0.0 copy-done.2
  52.4 1.1 fusion.12
  53.6 0.0 all-gather.2.cloned.1.call-update
  53.6 25.4 %all-gather.2.cloned.1.call-done = bf16[1024,1024]{1,0:T(8,128)(2,1)} async-done(((bf16[1024,256]{1,0:T(8,128)(2,1)}), bf16[1024,1024]{1,0:T(8,128)(2,1)}) %all-gather.2.cloned.1.call-update) | async-done | bytes 2097168 | tf_op jit(solution)/shard_map/all_gather | solution.py:39
  79.1 54.8 %all-to-all-done.1 = bf16[8,128,1792]{2,1,0:T(8,128)(2,1)} async-done(((bf16[8,128,1792]{2,1,0:T(8,128)(2,1)}), bf16[8,128,1792]{2,1,0:T(8,128)(2,1)}, u32[]{:S(2)}, u32[]{:S(2)}) %all-to-all-start.1) | async-done | bytes 3670048 | tf_op jit(solution)/shard_map/all_to_all | solution.py:27
  133.9 0.0 copy-start.3
  133.9 7.9 %fusion.1 = f32[1024]{0:T(1024)S(1)} fusion(bf16[1024,1792]{1,0:T(8,128)(2,1)} %bitcast.12, bf16[1024,1024]{1,0:T(8,128)(2,1)} %all-gather.2.cloned.1.call-done, bf16[1,1024,1792]{2,1,0:T(8,128)(2,1)} %param.11), kind=kOutput, calls=%fused_computation.8 | convolution fusion | flops 3763600384 | bytes 9441280 | tf_op jit(solution)/shard_map/dot_general | solution.py:40
  141.8 6.3 %psum.7 = f32[8,1,128]{2,1,0:T(1,128)} all-reduce(f32[8,1,128]{2,1,0:T(1,128)S(1)} %bitcast.47), channel_id=1, replica_groups=mesh['ep'=8,'et'=4] {'et'}, use_global_device_ids=true, to_apply=%region_6.7 | all-reduce | flops 1024 | bytes 8192 | tf_op jit(solution)/shard_map/psum | solution.py:47
  148.1 4.9 %all-to-all-start.2 = ((f32[8,1,128]{2,1,0:T(1,128)}), f32[8,1,128]{2,1,0:T(1,128)S(1)}, u32[]{:S(2)}, u32[]{:S(2)}) async-start(f32[8,1,128]{2,1,0:T(1,128)} %psum.7), calls=%async_computation.2 | async-start | bytes 8192 | tf_op jit(solution)/shard_map/all_to_all | solution.py:48
  152.9 0.0 copy-done.3
  152.9 8.0 %fusion.5 = bf16[1,1024,1792]{2,1,0:T(8,128)(2,1)} fusion(bf16[1024,1024]{1,0:T(8,128)(2,1)S(1)} %copy-done.3, bf16[1024,1792]{1,0:T(8,128)(2,1)} %bitcast.12, f32[1024]{0:T(1024)S(1)} %bitcast.46), kind=kOutput, calls=%fused_computation.13 | convolution fusion | flops 3765436416 | bytes 9441280 | tf_op jit(solution)/shard_map/dot_general | solution.py:41
  160.9 0.0 all-to-all-done.2
  160.9 4.5 %gather_fusion.2 = f32[1024]{0:T(1024)S(1)} fusion(f32[1024]{0:T(1024)S(1)} %bitcast.39, s32[1024]{0:T(1024)S(1)} %broadcast_clamp_fusion), kind=kCustom, calls=%fused_computation.2 | custom fusion | bytes 12288 | tf_op jit(solution)/shard_map/gather | solution.py:51
  165.4 0.1 reshape.100
  165.5 0.7 copy.18
  (10 shorter events, 0.1 us)
Async XLA Ops:
  7.2 29.1 %copy-start = (bf16[128,1792]{1,0:T(8,128)(2,1)S(1)}, bf16[128,1792]{1,0:T(8,128)(2,1)}, u32[]{:S(2)}) copy-start(bf16[128,1792]{1,0:T(8,128)(2,1)} %param.6) | copy-start | bytes 1376260
  29.0 17.3 %all-to-all-start = ((bf16[8,1,128]{2,1,0:T(2,128)(2,1)}), bf16[8,1,128]{2,1,0:T(2,128)(2,1)S(1)}, u32[]{:S(2)}, u32[]{:S(2)}) async-start(bf16[8,1,128]{2,1,0:T(2,128)(2,1)} %copy.17), calls=%async_computation | async-start | bytes 8192 | tf_op jit(solution)/shard_map/all_to_all | solution.py:28
  46.2 6.2 %copy-start.1 = (bf16[1,1024,256]{2,1,0:T(8,128)(2,1)S(1)}, bf16[1,1024,256]{2,1,0:T(8,128)(2,1)}, u32[]{:S(2)}) copy-start(bf16[1,1024,256]{2,1,0:T(8,128)(2,1)} %param.10) | copy-start | bytes 1572868
  46.2 6.2 %copy-start.2 = (bf16[1,1024,256]{2,1,0:T(8,128)(2,1)S(1)}, bf16[1,1024,256]{2,1,0:T(8,128)(2,1)}, u32[]{:S(2)}) copy-start(bf16[1,1024,256]{2,1,0:T(8,128)(2,1)} %param.9) | copy-start | bytes 1572868
  46.2 87.6 %all-to-all-start.1 = ((bf16[8,128,1792]{2,1,0:T(8,128)(2,1)}), bf16[8,128,1792]{2,1,0:T(8,128)(2,1)}, u32[]{:S(2)}, u32[]{:S(2)}) async-start(bf16[8,128,1792]{2,1,0:T(8,128)(2,1)} %broadcast_select_fusion), calls=%async_computation.1 | async-start | bytes 7340032 | tf_op jit(solution)/shard_map/all_to_all | solution.py:27
  52.4 26.7 %all-gather.2.cloned.1.call-start = ((), (), s32[]{:S(2)}) async-start(), calls=%async_computation.3 | async-start | bytes 2621440 | tf_op jit(solution)/shard_map/all_gather | solution.py:39
  133.9 19.1 %copy-start.3 = (bf16[1024,1024]{1,0:T(8,128)(2,1)S(1)}, bf16[1024,1024]{1,0:T(8,128)(2,1)}, u32[]{:S(2)}) copy-start(bf16[1024,1024]{1,0:T(8,128)(2,1)} %all-gather.2.cloned.1.call-done) | copy-start | bytes 6291460
  148.1 12.8 %all-to-all-start.2 = ((f32[8,1,128]{2,1,0:T(1,128)}), f32[8,1,128]{2,1,0:T(1,128)S(1)}, u32[]{:S(2)}, u32[]{:S(2)}) async-start(f32[8,1,128]{2,1,0:T(1,128)} %psum.7), calls=%async_computation.2 | async-start | bytes 8192 | tf_op jit(solution)/shard_map/all_to_all | solution.py:48
Sparse Core Ops, SparseCore 0:
  54.8 24.2 all-gather.1
where the time goes:
time: 173 us
  waiting for transfers between devices  80.3 us (46%)
  local copies, waits for them, and re-layouts  29.6 us (17%)
  starting transfers between devices  18.3 us (11%)
  matrix products  15.9 us (9%)
  between operations  14.2 us (8%)
  other arithmetic  8.6 us (5%)
  blocking collectives  6.26 us (4%)
    all_to_all x1, waiting for transfers between devices, local(): lax.all_to_all(send_rows, 'ep', split_axis=0, concat_axis=0, tiled=True)  54.8 us
    all_gather x1, waiting for transfers between devices, local(): piece = lax.all_gather(hidden_part, 'et', axis=1, tiled=True)  25.4 us
    dot_general x1, matrix products, local(): lax.dot_general(piece, scaled, (((0,), (0,)), ((), ())), preferred_elemen...  7.96 us
    dot_general x1, matrix products, local(): expert_out = jnp.dot(piece, weight, preferred_element_type=jnp.float32)  7.94 us
    all_to_all x1, starting transfers between devices, local(): lax.all_to_all(send_gates, 'ep', split_axis=0, concat_axis=0, tiled=True)  7.25 us
    gather x1, local copies, waits for them, and re-layouts, local(): send_gates = jnp.where(filled, gate_weights.reshape(-1)[slot_pair], 0.0)  6.8 us
    psum x1, blocking collectives, local(): slot_grad = lax.psum(partial_grad, 'et')  6.26 us
    all_to_all x1, starting transfers between devices, local(): lax.all_to_all(send_rows, 'ep', split_axis=0, concat_axis=0, tiled=True)  6.13 us
  transfers between devices with their start and end apart: 4, of which 2 were waited for; matrix products, arithmetic and copies ran while one was open for 11% of the time, Pallas kernels for 0%

commit v1 on v0

--- a/solution.py
+++ b/solution.py
@@ -1,10 +1,222 @@
+import functools
+
 import jax
 import jax.numpy as jnp
+import numpy as np
 from jax import lax
+from jax.experimental import pallas as pl
+from jax.experimental.pallas import tpu as pltpu
 from jax.sharding import PartitionSpec as P
 
-
-def local(out_grad, gate_weights, routes, gate_pre, up_pre, down_weight):
+MIB = 1024 * 1024
+BF16 = jnp.bfloat16
+F32 = jnp.float32
+
+
+def vmem_spec():
+    return pl.BlockSpec(memory_space=pltpu.VMEM)
+
+
+def smem_spec():
+    return pl.BlockSpec(memory_space=pltpu.SMEM)
+
+
+def params(mib):
+    return pltpu.CompilerParams(vmem_limit_bytes=mib * MIB)
+
+
+def cost(flops, moved):
+    return pl.CostEstimate(flops=int(flops), bytes_accessed=int(moved), transcendentals=0)
+
+
+def assemble(info, parts, weight, capacity):
+    slots, width = parts[0].shape
+    units, feats = weight.shape
+    cols = 256
+
+    def body(info_ref, *refs):
+        part_refs, (w_ref, ht_ref, eo_ref, h_scr) = refs[: len(parts)], refs[len(parts) :]
+
+        @pl.when(pl.program_id(0) == 0)
+        def _():
+            for m, ref in enumerate(part_refs):
+                at = pl.multiple_of(info_ref[m] * width, width)
+                value = ref[...]
+                h_scr[:, pl.ds(at, width)] = value
+                ht_ref[pl.ds(at, width), :] = value.T
+
+        eo_ref[...] = jnp.dot(h_scr[...], w_ref[...], preferred_element_type=F32)
+
+    return pl.pallas_call(
+        body,
+        grid=(feats // cols,),
+        in_specs=[smem_spec()]
+        + [vmem_spec()] * len(parts)
+        + [pl.BlockSpec((units, cols), lambda j: (0, j))],
+        out_specs=[
+            pl.BlockSpec((units, slots), lambda j: (0, 0)),
+            pl.BlockSpec((slots, cols), lambda j: (0, j)),
+        ],
+        out_shape=[
+            jax.ShapeDtypeStruct((units, slots), BF16),
+            jax.ShapeDtypeStruct((slots, feats), F32),
+        ],
+        scratch_shapes=[pltpu.VMEM((slots, units), BF16)],
+        compiler_params=params(40),
+        cost_estimate=cost(2 * slots * units * feats, 2 * units * feats + 4 * slots * feats),
+        name="expert_out",
+    )(info, *parts, weight)
+
+
+def slot_sums(info, pieces, expert_out, capacity, where):
+    rows, feats = pieces[0].shape
+
+    def body(info_ref, *refs):
+        piece_refs, (eo_ref, out_ref) = refs[: len(pieces)], refs[len(pieces) :]
+        for i, ref in enumerate(piece_refs):
+            at, first = where[i]
+            start = pl.multiple_of(info_ref[at] * capacity + first, rows)
+            total = jnp.sum(ref[...].astype(F32) * eo_ref[pl.ds(start, rows), :], axis=1)
+            out_ref[pl.ds(i, 1), :] = total[None, :]
+
+    return pl.pallas_call(
+        body,
+        in_specs=[smem_spec()] + [vmem_spec()] * (len(pieces) + 1),
+        out_specs=vmem_spec(),
+        out_shape=jax.ShapeDtypeStruct((len(pieces), rows), F32),
+        compiler_params=params(24),
+        cost_estimate=cost(2 * len(pieces) * rows * feats, 6 * len(pieces) * rows * feats),
+        name="slot_sums",
+    )(info, *pieces, expert_out)
+
+
+def weight_grad(info, pieces, gates, hidden_t, capacity, where):
+    rows, feats = pieces[0].shape
+    units, slots = hidden_t.shape
+    cols = 256
+
+    def body(info_ref, *refs):
+        piece_refs, (g_ref, ht_ref, out_ref, rows_scr) = refs[: len(pieces)], refs[len(pieces) :]
+
+        for i, ref in enumerate(piece_refs):
+            at, first = where[i]
+            start = pl.multiple_of(info_ref[at] * capacity + first, rows)
+            gate = g_ref[pl.ds(start, rows), :].astype(F32)
+            rows_scr[pl.ds(start, rows), :] = (ref[...].astype(F32) * gate).astype(BF16)
+        out_ref[...] = jnp.dot(ht_ref[...], rows_scr[...], preferred_element_type=F32).astype(BF16)
+
+    return pl.pallas_call(
+        body,
+        grid=(feats // cols,),
+        in_specs=[smem_spec()]
+        + [pl.BlockSpec((rows, cols), lambda j: (0, j))] * len(pieces)
+        + [vmem_spec(), vmem_spec()],
+        out_specs=pl.BlockSpec((units, cols), lambda j: (0, j)),
+        out_shape=jax.ShapeDtypeStruct((units, feats), BF16),
+        scratch_shapes=[pltpu.VMEM((slots, cols), BF16)],
+        compiler_params=params(24),
+        cost_estimate=cost(2 * slots * units * feats, 4 * units * feats),
+        name="weight_grad",
+    )(info, *pieces, gates, hidden_t)
+
+
+def pick(returned, routes_t):
+    topk, tokens = routes_t.shape
+    experts, groups, _ = returned.shape
+
+    def body(back_ref, routes_ref, out_ref):
+        routes = routes_ref[...]
+        total = jnp.zeros((topk, tokens), F32)
+        for e in range(experts):
+            value = back_ref[e, 0:1, :]
+            for f in range(1, groups):
+                value = value + back_ref[e, f : f + 1, :]
+            total = jnp.where(routes == e, jnp.broadcast_to(value, total.shape), total)
+        out_ref[...] = total
+
+    return pl.pallas_call(
+        body,
+        in_specs=[vmem_spec(), vmem_spec()],
+        out_specs=vmem_spec(),
+        out_shape=jax.ShapeDtypeStruct((topk, tokens), F32),
+        name="pick_gate_grad",
+    )(returned, routes_t)
+
+
+def ring_of(experts):
+    return list(range(0, experts, 2)) + list(range(experts - 1, 0, -2))
+
+
+def dense(out_grad, gate_weights, routes, gate_pre, up_pre, down_weight):
+    tokens, topk = routes.shape
+    experts, groups = lax.axis_size("ep"), lax.axis_size("et")
+    slots = gate_pre.shape[1]
+    half = tokens // 2
+    weight = down_weight[0]
+
+    ring = ring_of(experts)
+    forth = [(ring[i], ring[(i + 1) % experts]) for i in range(experts)]
+    back = [(b, a) for a, b in forth]
+    place = {device: i for i, device in enumerate(ring)}
+    far = experts // 2
+    steps = [0] + [s for k in range(1, far) for s in (-k, k)] + [far]
+    sources = np.array([[ring[(place[d] + s) % experts] for s in steps] for d in range(experts)], np.int32)
+    et = lax.axis_index("et").astype(jnp.int32)
+    info = jnp.concatenate(
+        [jnp.stack([et ^ m for m in range(groups)]), jnp.asarray(sources)[lax.axis_index("ep")]]
+    )
+
+    top, bottom = out_grad[:half], out_grad[half:]
+    up, down = [top, bottom], [bottom, top]
+    pieces, where = [top, bottom], [(groups, 0), (groups, half)]
+    for k in range(1, far):
+        for c in range(2):
+            up[c] = lax.ppermute(up[c], "ep", forth)
+            down[c] = lax.ppermute(down[c], "ep", back)
+        pieces += [up[0], up[1], down[1], down[0]]
+        a, b = groups + 2 * k - 1, groups + 2 * k
+        where += [(a, 0), (a, half), (b, 0), (b, half)]
+    last = [lax.ppermute(up[0], "ep", forth), lax.ppermute(down[0], "ep", back)]
+    where_last = [(groups + 2 * far - 1, 0), (groups + 2 * far - 1, half)]
+
+    routes_t, gates_t = routes.T, gate_weights.T
+    by_expert = jnp.sum(
+        jnp.where(
+            routes_t[None] == jnp.arange(experts, dtype=jnp.int32)[:, None, None],
+            gates_t[None].astype(F32),
+            0.0,
+        ),
+        axis=1,
+    ).astype(BF16)
+    gates = lax.all_to_all(by_expert, "ep", split_axis=0, concat_axis=0, tiled=True)
+    gates = gates.reshape(slots, 1)
+
+    hidden = (
+        jax.nn.silu(gate_pre[0].astype(F32)) * up_pre[0].astype(F32)
+    ).astype(BF16)
+    parts = [hidden]
+    bit = 1
+    order = [0]
+    for axis_bit in (2, 1):
+        swap = [(i, i ^ axis_bit) for i in range(groups)]
+        parts += [lax.ppermute(p, "et", swap) for p in parts]
+        order += [o ^ axis_bit for o in order]
+    parts = [parts[order.index(m)] for m in range(groups)]
+
+    hidden_t, expert_out = assemble(info, parts, weight, tokens)
+    sums = slot_sums(info, pieces, expert_out, tokens, where)
+    sums_last = slot_sums(info, last, expert_out, tokens, where_last)
+    sums = jnp.concatenate([sums.reshape(-1, tokens), sums_last.reshape(1, tokens)])
+    inverse = np.argsort(sources, axis=1).astype(np.int32)
+    sums = sums[jnp.asarray(inverse)[lax.axis_index("ep")]]
+    outgoing = jnp.broadcast_to(sums[:, None, :], (experts, groups, tokens)).reshape(experts * groups, tokens)
+    returned = lax.all_to_all(outgoing, ("ep", "et"), split_axis=0, concat_axis=0, tiled=True)
+    grad = weight_grad(info, pieces + last, gates, hidden_t, tokens, where + where_last)
+    d_gate = pick(returned.reshape(experts, groups, tokens), routes_t).T
+    return grad[None], d_gate
+
+
+def routed(out_grad, gate_weights, routes, gate_pre, up_pre, down_weight):
     tok_rows, topk = routes.shape
     experts = lax.axis_size("ep")
     slot_total = gate_pre.shape[1]
@@ -38,11 +250,9 @@
     )
     piece = lax.all_gather(hidden_part, "et", axis=1, tiled=True)
     expert_out = jnp.dot(piece, weight, preferred_element_type=jnp.float32)
-    block = lax.dot_general(
+    grad_weight = lax.dot_general(
         piece, scaled, (((0,), (0,)), ((), ())), preferred_element_type=jnp.float32
     )
-    grad_weight = block
-    expert_out, grad_weight = (expert_out, grad_weight)
     partial_grad = jnp.sum(rows_in.astype(jnp.float32) * expert_out, axis=1)
     slot_grad = lax.psum(partial_grad, "et")
     returned = lax.all_to_all(
@@ -53,6 +263,15 @@
 
 
 def solution(mesh):
+    sizes = dict(mesh.shape)
+
+    def local(out_grad, gate_weights, routes, gate_pre, up_pre, down_weight):
+        tokens, topk = routes.shape
+        whole = topk == sizes["ep"] and gate_pre.shape[1] == topk * tokens
+        if whole and sizes["ep"] % 2 == 0 and sizes["et"] == 4:
+            return dense(out_grad, gate_weights, routes, gate_pre, up_pre, down_weight)
+        return routed(out_grad, gate_weights, routes, gate_pre, up_pre, down_weight)
+
     in_specs = (
         P("ep", "et"),
         P("ep", None),

time: 173 us -> 85.9 us (0.50)
  waiting for transfers between devices: 80.3 us -> 12.4 us
  Pallas kernels: 0 us -> 21.8 us
  matrix products: 15.9 us -> 0 us
  between operations: 14.2 us -> 0.72 us
  local copies, waits for them, and re-layouts: 29.6 us -> 17.1 us
  starting transfers between devices: 18.3 us -> 29.6 us
  blocking collectives: 6.26 us -> 0 us
  other arithmetic: 8.6 us -> 3.62 us
    all_to_all x3 -> x2, waiting for transfers between devices: 54.8 us -> 0.86 us  [the longest x1 0.86 us: dense(): lax.all_to_all(by_expert, 'ep', split_axis=0, concat_axis=0, tiled=True)]
    all_gather x1 -> x0, waiting for transfers between devices: 25.4 us -> none  [local(): piece = lax.all_gather(hidden_part, 'et', axis=1, tiled=True)]
    pallas_call x0 -> x5, Pallas kernels: none -> 21.8 us  [the longest x1 9.15 us: assemble(): pl.pallas_call(body, grid=(feats // cols,), in_specs=[smem_spec()] + [vme...]
    ppermute x0 -> x17, starting transfers between devices: none -> 19.3 us  [the longest x6 7.54 us: dense(): down[c] = lax.ppermute(down[c], 'ep', back)]
    gather x3 -> x1, local copies, waits for them, and re-layouts: 17.1 us -> 0.55 us  [dense(): sums = sums[jnp.asarray(inverse)[lax.axis_index('ep')]]]
    dot_general x2 -> x0, matrix products: 15.9 us -> none  [the longest x1 7.96 us: local(): lax.dot_general(piece, scaled, (((0,), (0,)), ((), ())), preferred_elemen...]
    ppermute x0 -> x17, waiting for transfers between devices: none -> 11.5 us  [the longest x6 6.39 us: dense(): up[c] = lax.ppermute(up[c], 'ep', forth)]
    unnamed x11 -> x20, local copies, waits for them, and re-layouts: 2.33 us -> 13.1 us
  transfers between devices with their start and end apart: 4 -> 19, of which waited for: 2 -> 6; matrix products, arithmetic and copies ran while one was open for 11% -> 6% of each run, Pallas kernels for 0% -> 22%
where the time goes in v1:
time: 85.9 us; the launch traced here: 85.2 us
  starting transfers between devices  29.6 us (34%)
  Pallas kernels  21.8 us (25%)
  local copies, waits for them, and re-layouts  17.1 us (20%)
  waiting for transfers between devices  12.4 us (14%)
  other arithmetic  3.62 us (4%)
    unnamed x20, local copies, waits for them, and re-layouts  13.1 us
    pallas_call x1, Pallas kernels, assemble(): pl.pallas_call(body, grid=(feats // cols,), in_specs=[smem_spec()] + [vme...  9.15 us
    pallas_call x1, Pallas kernels, weight_grad(): pl.pallas_call(body, grid=(feats // cols,), in_specs=[smem_spec()] + [pl....  8.68 us
    ppermute x6, starting transfers between devices, dense(): down[c] = lax.ppermute(down[c], 'ep', back)  7.54 us
    ppermute x6, starting transfers between devices, dense(): up[c] = lax.ppermute(up[c], 'ep', forth)  6.73 us
    ppermute x6, waiting for transfers between devices, dense(): up[c] = lax.ppermute(up[c], 'ep', forth)  6.39 us
    all_to_all x1, starting transfers between devices, dense(): lax.all_to_all(by_expert, 'ep', split_axis=0, concat_axis=0, tiled=True)  5.32 us
    ppermute x6, waiting for transfers between devices, dense(): down[c] = lax.ppermute(down[c], 'ep', back)  5.13 us
  transfers between devices with their start and end apart: 19, of which 6 were waited for; matrix products, arithmetic and copies ran while one was open for 6% of the time, Pallas kernels for 22%

profile of v1, /device:TPU:0, one launch (start us, length us, event | category | flops | bytes accessed | tf_op | source)
XLA Modules:
  0.0 85.2 jit_solution(5160826751008973420)
XLA Ops:
  0.6 1.5 %fusion.4.refs_0_ = bf16[1024,256]{1,0:T(8,128)(2,1)S(1)} fusion(bf16[1,1024,256]{2,1,0:T(8,128)(2,1)} %param.12, bf16[1,1024,256]{2,1,0:T(8,128)(2,1)} %param.11), kind=kLoop, calls=%fused_computation.7 | loop fusion | flops 2097152 | bytes 1572864 | tf_op jit(solution)/shard_map/convert_element_type | solution.py:196
  2.2 3.0 %collective-permute-start.15 = (bf16[1024,256]{1,0:T(8,128)(2,1)S(1)}, bf16[1024,256]{1,0:T(8,128)(2,1)}, u32[]{:S(2)}, u32[]{:S(2)}) collective-permute-start(bf16[1024,256]{1,0:T(8,128)(2,1)S(1)} %fusion.4.refs_0_), channel_id=1, source_target_pairs={{0,2},{1,3},{2,0},{3,1},{4,6},{5,7},{6,4},{7,5},{8,10},{9,11},{10,... | collective-permute-start | bytes 1572872 | tf_op jit(solution)/shard_map/ppermute | solution.py:202
  5.2 1.1 %fusion.6 = (bf16[64,1792]{1,0:T(8,128)(2,1)S(1)}, bf16[64,1792]{1,0:T(8,128)(2,1)S(1)}) fusion(bf16[128,1792]{1,0:T(8,128)(2,1)} %param.8), kind=kLoop, calls=%fused_computation.17 | loop fusion | bytes 917504 | tf_op jit(solution)/shard_map/slice | solution.py:169
  6.3 1.5 %collective-permute-start.3 = (bf16[64,1792]{1,0:T(8,128)(2,1)S(1)}, bf16[64,1792]{1,0:T(8,128)(2,1)S(1)}, u32[]{:S(2)}, u32[]{:S(2)}) collective-permute-start(bf16[64,1792]{1,0:T(8,128)(2,1)S(1)} %get-tuple-element.6.refs_1_), channel_id=1, source_target_pairs={{8,0},{16,8},{24,16},{28,24},{20,28},{12,20},{4,12},{0,4},{9,1},{1... | collective-permute-start | bytes 688136 | tf_op jit(solution)/shard_map/ppermute | solution.py:175
  7.8 0.5 collective-permute-start
  8.3 1.5 %collective-permute-start.2 = (bf16[64,1792]{1,0:T(8,128)(2,1)S(1)}, bf16[64,1792]{1,0:T(8,128)(2,1)S(1)}, u32[]{:S(2)}, u32[]{:S(2)}) collective-permute-start(bf16[64,1792]{1,0:T(8,128)(2,1)S(1)} %get-tuple-element.7.refs_0_), channel_id=1, source_target_pairs={{8,0},{16,8},{24,16},{28,24},{20,28},{12,20},{4,12},{0,4},{9,1},{1... | collective-permute-start | bytes 688136 | tf_op jit(solution)/shard_map/ppermute | solution.py:175
  9.8 0.5 collective-permute-start.1
  10.4 4.5 %collective-permute-done.3.refs_5_ = bf16[64,1792]{1,0:T(8,128)(2,1)S(1)} collective-permute-done((bf16[64,1792]{1,0:T(8,128)(2,1)S(1)}, bf16[64,1792]{1,0:T(8,128)(2,1)S(1)}, u32[]{:S(2)}, u32[]{:S(2)}) %collective-permute-start.3) | collective-permute-done | bytes 229408 | tf_op jit(solution)/shard_map/ppermute | solution.py:175
  14.8 0.0 collective-permute-start.14
  14.9 1.5 %collective-permute-done.refs_2_ = bf16[64,1792]{1,0:T(8,128)(2,1)S(1)} collective-permute-done((bf16[64,1792]{1,0:T(8,128)(2,1)S(1)}, bf16[64,1792]{1,0:T(8,128)(2,1)S(1)}, u32[]{:S(2)}, u32[]{:S(2)}) %collective-permute-start) | collective-permute-done | bytes 229408 | tf_op jit(solution)/shard_map/ppermute | solution.py:174
  16.4 1.6 %collective-permute-start.7 = (bf16[64,1792]{1,0:T(8,128)(2,1)S(1)}, bf16[64,1792]{1,0:T(8,128)(2,1)S(1)}, u32[]{:S(2)}, u32[]{:S(2)}) collective-permute-start(bf16[64,1792]{1,0:T(8,128)(2,1)S(1)} %collective-permute-done.3.refs_5_), channel_id=1, source_target_pairs={{8,0},{16,8},{24,16},{28,24},{20,28},{12,20},{4,12},{0,4},{9,1},{1... | collective-permute-start | bytes 688136 | tf_op jit(solution)/shard_map/ppermute | solution.py:175
  17.9 0.6 collective-permute-done.2.refs_4_
  18.6 1.6 %collective-permute-start.4 = (bf16[64,1792]{1,0:T(8,128)(2,1)S(1)}, bf16[64,1792]{1,0:T(8,128)(2,1)S(1)}, u32[]{:S(2)}, u32[]{:S(2)}) collective-permute-start(bf16[64,1792]{1,0:T(8,128)(2,1)S(1)} %collective-permute-done.refs_2_), channel_id=1, source_target_pairs={{0,8},{8,16},{16,24},{24,28},{28,20},{20,12},{12,4},{4,0},{1,9},{9... | collective-permute-start | bytes 688136 | tf_op jit(solution)/shard_map/ppermute | solution.py:174
  20.1 0.0 collective-permute-done.1.refs_3_
  20.2 0.9 %collective-permute-start.6 = (bf16[64,1792]{1,0:T(8,128)(2,1)S(1)}, bf16[64,1792]{1,0:T(8,128)(2,1)S(1)}, u32[]{:S(2)}, u32[]{:S(2)}) collective-permute-start(bf16[64,1792]{1,0:T(8,128)(2,1)S(1)} %collective-permute-done.2.refs_4_), channel_id=1, source_target_pairs={{8,0},{16,8},{24,16},{28,24},{20,28},{12,20},{4,12},{0,4},{9,1},{1... | collective-permute-start | bytes 688136 | tf_op jit(solution)/shard_map/ppermute | solution.py:175
  21.1 0.0 collective-permute-done.15.refs_2_
  21.1 0.0 collective-permute-start.16
  21.1 0.7 convert_bitcast_fusion
  21.8 0.7 select_reduce_fusion
  22.5 0.6 copy.14
  23.1 5.3 %all-to-all-start = ((bf16[8,1,128]{2,1,0:T(2,128)(2,1)}), bf16[8,1,128]{2,1,0:T(2,128)(2,1)S(1)}, u32[]{:S(2)}, u32[]{:S(2)}) async-start(bf16[8,1,128]{2,1,0:T(2,128)(2,1)} %copy.14), calls=%async_computation | async-start | bytes 8192 | tf_op jit(solution)/shard_map/all_to_all | solution.py:191
  28.4 0.0 collective-permute-done.7.refs_9_
  28.4 2.0 %collective-permute-start.5 = (bf16[64,1792]{1,0:T(8,128)(2,1)S(1)}, bf16[64,1792]{1,0:T(8,128)(2,1)S(1)}, u32[]{:S(2)}, u32[]{:S(2)}) collective-permute-start(bf16[64,1792]{1,0:T(8,128)(2,1)S(1)} %collective-permute-done.1.refs_3_), channel_id=1, source_target_pairs={{0,8},{8,16},{16,24},{24,28},{28,20},{20,12},{12,4},{4,0},{1,9},{9... | collective-permute-start | bytes 688136 | tf_op jit(solution)/shard_map/ppermute | solution.py:174
  30.4 0.0 collective-permute-done.4.refs_6_
  30.4 0.1 collective-permute-start.11
  30.5 0.0 collective-permute-done.6.refs_8_
  30.5 2.0 %collective-permute-start.8 = (bf16[64,1792]{1,0:T(8,128)(2,1)S(1)}, bf16[64,1792]{1,0:T(8,128)(2,1)S(1)}, u32[]{:S(2)}, u32[]{:S(2)}) collective-permute-start(bf16[64,1792]{1,0:T(8,128)(2,1)S(1)} %collective-permute-done.4.refs_6_), channel_id=1, source_target_pairs={{0,8},{8,16},{16,24},{24,28},{28,20},{20,12},{12,4},{4,0},{1,9},{9... | collective-permute-start | bytes 688136 | tf_op jit(solution)/shard_map/ppermute | solution.py:174
  32.5 0.7 fusion.5
  33.2 0.7 dynamic-slice_bitcast_fusion
  33.9 0.1 concatenate.6.info_ref
  34.0 0.9 %all-to-all-done = bf16[8,1,128]{2,1,0:T(2,128)(2,1)S(1)} async-done(((bf16[8,1,128]{2,1,0:T(2,128)(2,1)}), bf16[8,1,128]{2,1,0:T(2,128)(2,1)S(1)}, u32[]{:S(2)}, u32[]{:S(2)}) %all-to-all-start) | async-done | bytes 2080 | tf_op jit(solution)/shard_map/all_to_all | solution.py:191
  34.8 0.2 copy.15.refs_16_
  35.0 2.0 %collective-permute-done.5.refs_7_ = bf16[64,1792]{1,0:T(8,128)(2,1)S(1)} collective-permute-done((bf16[64,1792]{1,0:T(8,128)(2,1)S(1)}, bf16[64,1792]{1,0:T(8,128)(2,1)S(1)}, u32[]{:S(2)}, u32[]{:S(2)}) %collective-permute-start.5) | collective-permute-done | bytes 229408 | tf_op jit(solution)/shard_map/ppermute | solution.py:174
  37.0 1.9 %collective-permute-start.10 = (bf16[64,1792]{1,0:T(8,128)(2,1)S(1)}, bf16[64,1792]{1,0:T(8,128)(2,1)S(1)}, u32[]{:S(2)}, u32[]{:S(2)}) collective-permute-start(bf16[64,1792]{1,0:T(8,128)(2,1)S(1)} %collective-permute-done.6.refs_8_), channel_id=1, source_target_pairs={{8,0},{16,8},{24,16},{28,24},{20,28},{12,20},{4,12},{0,4},{9,1},{1... | collective-permute-start | bytes 688136 | tf_op jit(solution)/shard_map/ppermute | solution.py:175
  38.9 0.0 collective-permute-done.14.refs_1_
  38.9 0.1 collective-permute-start.9
  39.0 2.9 %collective-permute-done.8.refs_10_ = bf16[64,1792]{1,0:T(8,128)(2,1)S(1)} collective-permute-done((bf16[64,1792]{1,0:T(8,128)(2,1)S(1)}, bf16[64,1792]{1,0:T(8,128)(2,1)S(1)}, u32[]{:S(2)}, u32[]{:S(2)}) %collective-permute-start.8) | collective-permute-done | bytes 229408 | tf_op jit(solution)/shard_map/ppermute | solution.py:174
  41.9 1.9 %collective-permute-start.12 = (bf16[64,1792]{1,0:T(8,128)(2,1)S(1)}, bf16[64,1792]{1,0:T(8,128)(2,1)}, u32[]{:S(2)}, u32[]{:S(2)}) collective-permute-start(bf16[64,1792]{1,0:T(8,128)(2,1)S(1)} %collective-permute-done.8.refs_10_), channel_id=1, source_target_pairs={{0,8},{8,16},{16,24},{24,28},{28,20},{20,12},{12,4},{4,0},{1,9},{9... | collective-permute-start | bytes 688136 | tf_op jit(solution)/shard_map/ppermute | solution.py:179
  43.8 0.0 collective-permute-done.11.refs_13_
  43.8 0.1 collective-permute-start.13
  44.0 0.0 collective-permute-done.16.refs_3_
  44.0 2.0 %copy-done.6 = bf16[1,1024,1792]{2,1,0:T(8,128)(2,1)S(1)} copy-done((bf16[1,1024,1792]{2,1,0:T(8,128)(2,1)S(1)}, bf16[1,1024,1792]{2,1,0:T(8,128)(2,1)}, u32[]{:S(2)}) %copy-start.6) | copy-done | bytes 3670040
  46.0 9.2 %expert_out.1 = (bf16[1024,1024]{1,0:T(8,128)(2,1)S(1)}, f32[1024,1792]{1,0:T(8,128)}) custom-call(s32[12]{0:T(128)S(1)} %concatenate.6.info_ref, bf16[1024,256]{1,0:T(8,128)(2,1)S(1)} %fusion.4.refs_0_, bf16[1024,256]{1,0:T(8,128)(2,1)} %collective-permute-done.14.refs_1_, bf16[1024,256]{1,0:T(8,128)(2,1)} %collective-permute-done.15.refs_2_, ...), custom_call_target="tpu_custom_call" | custom-call | flops 3758096384 | bytes 11010048 | tf_op jit(solution)/shard_map/expert_out/pallas_call | solution.py:50
  55.2 1.3 %copy-done.7 = bf16[1024,1024]{1,0:T(8,128)(2,1)} copy-done((bf16[1024,1024]{1,0:T(8,128)(2,1)}, bf16[1024,1024]{1,0:T(8,128)(2,1)S(1)}, u32[]{:S(2)}) %copy-start.7) | copy-done | bytes 2097176
  56.5 0.0 collective-permute-done.10.refs_12_
  56.5 0.0 collective-permute-done.9.refs_11_
  56.5 3.1 %copy-done = f32[1024,1792]{1,0:T(8,128)S(1)} copy-done((f32[1024,1792]{1,0:T(8,128)S(1)}, f32[1024,1792]{1,0:T(8,128)}, u32[]{:S(2)}) %copy-start) | copy-done | bytes 7340056
  59.6 1.3 %slot_sums.2 = f32[14,64]{1,0:T(8,128)S(1)} custom-call(s32[12]{0:T(128)S(1)} %concatenate.6.info_ref, bf16[64,1792]{1,0:T(8,128)(2,1)S(1)} %get-tuple-element.7.refs_0_, bf16[64,1792]{1,0:T(8,128)(2,1)S(1)} %get-tuple-element.6.refs_1_, bf16[64,1792]{1,0:T(8,128)(2,1)S(1)} %collective-permute-done.refs_2_, ...), custom_call_target="tpu_custom_call" | custom-call | flops 3211264 | bytes 9633792 | tf_op jit(solution)/shard_map/slot_sums/pallas_call | solution.py:82
  60.9 0.7 copy-done.2
  61.6 0.7 copy-done.4
  62.3 0.1 reshape.69
  62.3 0.0 collective-permute-done.12.refs_14_.refs_0_
  62.3 0.0 collective-permute-done.13.refs_15_.refs_1_
  62.4 3.1 %copy-done.1 = f32[1024,1792]{1,0:T(8,128)S(1)} copy-done((f32[1024,1792]{1,0:T(8,128)S(1)}, f32[1024,1792]{1,0:T(8,128)}, u32[]{:S(2)}) %copy-start.1) | copy-done | bytes 7340056
  65.4 1.3 %slot_sums.3 = f32[2,64]{1,0:T(2,128)S(1)} custom-call(s32[12]{0:T(128)S(1)} %concatenate.6.info_ref, bf16[64,1792]{1,0:T(8,128)(2,1)} %collective-permute-done.12.refs_14_.refs_0_, bf16[64,1792]{1,0:T(8,128)(2,1)} %collective-permute-done.13.refs_15_.refs_1_, f32[1024,1792]{1,0:T(8,128)S(1)} %copy-done.1), custom_call_target="tpu_custom_call" | custom-call | flops 458752 | bytes 1376256 | tf_op jit(solution)/shard_map/slot_sums/pallas_call | solution.py:82
  66.7 0.1 reshape.70
  66.8 0.6 gather_fusion
  67.4 0.6 broadcast_in_dim.28
  68.0 5.0 %all-to-all-start.1 = ((f32[32,1,128]{2,1,0:T(1,128)}), f32[32,1,128]{2,1,0:T(1,128)S(1)}, u32[]{:S(2)}, u32[]{:S(2)}) async-start(f32[32,1,128]{2,1,0:T(1,128)} %bitcast.16), calls=%async_computation.1 | async-start | bytes 32768 | tf_op jit(solution)/shard_map/all_to_all | solution.py:213
  73.0 0.0 copy-start.8
  73.0 1.6 %copy-done.8 = bf16[1024,1024]{1,0:T(8,128)(2,1)S(1)} copy-done((bf16[1024,1024]{1,0:T(8,128)(2,1)S(1)}, bf16[1024,1024]{1,0:T(8,128)(2,1)}, u32[]{:S(2)}) %copy-start.8) | copy-done | bytes 2097176
  74.6 8.7 %weight_grad.1 = bf16[1024,1792]{1,0:T(8,128)(2,1)} custom-call(s32[12]{0:T(128)S(1)} %concatenate.6.info_ref, bf16[64,1792]{1,0:T(8,128)(2,1)S(1)} %get-tuple-element.7.refs_0_, bf16[64,1792]{1,0:T(8,128)(2,1)S(1)} %get-tuple-element.6.refs_1_, bf16[64,1792]{1,0:T(8,128)(2,1)S(1)} %collective-permute-done.refs_2_, ...), custom_call_target="tpu_custom_call" | custom-call | flops 3758096384 | bytes 7340032 | tf_op jit(solution)/shard_map/weight_grad/pallas_call | solution.py:108
  83.3 0.6 copy-done.9
  83.9 1.3 %pick_gate_grad.1 = f32[8,128]{1,0:T(8,128)} custom-call(f32[8,4,128]{2,1,0:T(4,128)} %bitcast.29, s32[8,128]{1,0:T(8,128)} %bitcast.32), custom_call_target="tpu_custom_call" | custom-call | tf_op jit(solution)/shard_map/pick_gate_grad/pallas_call | solution.py:137
  (14 shorter events, 0.0 us)
Async XLA Ops:
  2.2 18.9 %collective-permute-start.15 = (bf16[1024,256]{1,0:T(8,128)(2,1)S(1)}, bf16[1024,256]{1,0:T(8,128)(2,1)}, u32[]{:S(2)}, u32[]{:S(2)}) collective-permute-start(bf16[1024,256]{1,0:T(8,128)(2,1)S(1)} %fusion.4.refs_0_), channel_id=1, source_target_pairs={{0,2},{1,3},{2,0},{3,1},{4,6},{5,7},{6,4},{7,5},{8,10},{9,11},{10,... | collective-permute-start | bytes 1572872 | tf_op jit(solution)/shard_map/ppermute | solution.py:202
  6.3 8.6 %collective-permute-start.3 = (bf16[64,1792]{1,0:T(8,128)(2,1)S(1)}, bf16[64,1792]{1,0:T(8,128)(2,1)S(1)}, u32[]{:S(2)}, u32[]{:S(2)}) collective-permute-start(bf16[64,1792]{1,0:T(8,128)(2,1)S(1)} %get-tuple-element.6.refs_1_), channel_id=1, source_target_pairs={{8,0},{16,8},{24,16},{28,24},{20,28},{12,20},{4,12},{0,4},{9,1},{1... | collective-permute-start | bytes 688136 | tf_op jit(solution)/shard_map/ppermute | solution.py:175
  7.8 8.5 %collective-permute-start = (bf16[64,1792]{1,0:T(8,128)(2,1)S(1)}, bf16[64,1792]{1,0:T(8,128)(2,1)S(1)}, u32[]{:S(2)}, u32[]{:S(2)}) collective-permute-start(bf16[64,1792]{1,0:T(8,128)(2,1)S(1)} %get-tuple-element.7.refs_0_), channel_id=1, source_target_pairs={{0,8},{8,16},{16,24},{24,28},{28,20},{20,12},{12,4},{4,0},{1,9},{9... | collective-permute-start | bytes 688136 | tf_op jit(solution)/shard_map/ppermute | solution.py:174
  8.3 10.2 %collective-permute-start.2 = (bf16[64,1792]{1,0:T(8,128)(2,1)S(1)}, bf16[64,1792]{1,0:T(8,128)(2,1)S(1)}, u32[]{:S(2)}, u32[]{:S(2)}) collective-permute-start(bf16[64,1792]{1,0:T(8,128)(2,1)S(1)} %get-tuple-element.7.refs_0_), channel_id=1, source_target_pairs={{8,0},{16,8},{24,16},{28,24},{20,28},{12,20},{4,12},{0,4},{9,1},{1... | collective-permute-start | bytes 688136 | tf_op jit(solution)/shard_map/ppermute | solution.py:175
  9.8 10.3 %collective-permute-start.1 = (bf16[64,1792]{1,0:T(8,128)(2,1)S(1)}, bf16[64,1792]{1,0:T(8,128)(2,1)S(1)}, u32[]{:S(2)}, u32[]{:S(2)}) collective-permute-start(bf16[64,1792]{1,0:T(8,128)(2,1)S(1)} %get-tuple-element.6.refs_1_), channel_id=1, source_target_pairs={{0,8},{8,16},{16,24},{24,28},{28,20},{20,12},{12,4},{4,0},{1,9},{9... | collective-permute-start | bytes 688136 | tf_op jit(solution)/shard_map/ppermute | solution.py:174
  14.8 24.1 %collective-permute-start.14 = (bf16[1024,256]{1,0:T(8,128)(2,1)S(1)}, bf16[1024,256]{1,0:T(8,128)(2,1)}, u32[]{:S(2)}, u32[]{:S(2)}) collective-permute-start(bf16[1024,256]{1,0:T(8,128)(2,1)S(1)} %fusion.4.refs_0_), channel_id=1, source_target_pairs={{0,1},{1,0},{2,3},{3,2},{4,5},{5,4},{6,7},{7,6},{8,9},{9,8},{10,11... | collective-permute-start | bytes 1572872 | tf_op jit(solution)/shard_map/ppermute | solution.py:202
  16.4 12.1 %collective-permute-start.7 = (bf16[64,1792]{1,0:T(8,128)(2,1)S(1)}, bf16[64,1792]{1,0:T(8,128)(2,1)S(1)}, u32[]{:S(2)}, u32[]{:S(2)}) collective-permute-start(bf16[64,1792]{1,0:T(8,128)(2,1)S(1)} %collective-permute-done.3.refs_5_), channel_id=1, source_target_pairs={{8,0},{16,8},{24,16},{28,24},{20,28},{12,20},{4,12},{0,4},{9,1},{1... | collective-permute-start | bytes 688136 | tf_op jit(solution)/shard_map/ppermute | solution.py:175
  18.6 11.9 %collective-permute-start.4 = (bf16[64,1792]{1,0:T(8,128)(2,1)S(1)}, bf16[64,1792]{1,0:T(8,128)(2,1)S(1)}, u32[]{:S(2)}, u32[]{:S(2)}) collective-permute-start(bf16[64,1792]{1,0:T(8,128)(2,1)S(1)} %collective-permute-done.refs_2_), channel_id=1, source_target_pairs={{0,8},{8,16},{16,24},{24,28},{28,20},{20,12},{12,4},{4,0},{1,9},{9... | collective-permute-start | bytes 688136 | tf_op jit(solution)/shard_map/ppermute | solution.py:174
  20.2 10.4 %collective-permute-start.6 = (bf16[64,1792]{1,0:T(8,128)(2,1)S(1)}, bf16[64,1792]{1,0:T(8,128)(2,1)S(1)}, u32[]{:S(2)}, u32[]{:S(2)}) collective-permute-start(bf16[64,1792]{1,0:T(8,128)(2,1)S(1)} %collective-permute-done.2.refs_4_), channel_id=1, source_target_pairs={{8,0},{16,8},{24,16},{28,24},{20,28},{12,20},{4,12},{0,4},{9,1},{1... | collective-permute-start | bytes 688136 | tf_op jit(solution)/shard_map/ppermute | solution.py:175
  21.1 22.9 %collective-permute-start.16 = (bf16[1024,256]{1,0:T(8,128)(2,1)}, bf16[1024,256]{1,0:T(8,128)(2,1)}, u32[]{:S(2)}, u32[]{:S(2)}) collective-permute-start(bf16[1024,256]{1,0:T(8,128)(2,1)} %collective-permute-done.15.refs_2_), channel_id=1, source_target_pairs={{0,1},{1,0},{2,3},{3,2},{4,5},{5,4},{6,7},{7,6},{8,9},{9,8},{10,11... | collective-permute-start | bytes 1572872 | tf_op jit(solution)/shard_map/ppermute | solution.py:202
  23.1 11.7 %all-to-all-start = ((bf16[8,1,128]{2,1,0:T(2,128)(2,1)}), bf16[8,1,128]{2,1,0:T(2,128)(2,1)S(1)}, u32[]{:S(2)}, u32[]{:S(2)}) async-start(bf16[8,1,128]{2,1,0:T(2,128)(2,1)} %copy.14), calls=%async_computation | async-start | bytes 8192 | tf_op jit(solution)/shard_map/all_to_all | solution.py:191
  28.4 8.6 %collective-permute-start.5 = (bf16[64,1792]{1,0:T(8,128)(2,1)S(1)}, bf16[64,1792]{1,0:T(8,128)(2,1)S(1)}, u32[]{:S(2)}, u32[]{:S(2)}) collective-permute-start(bf16[64,1792]{1,0:T(8,128)(2,1)S(1)} %collective-permute-done.1.refs_3_), channel_id=1, source_target_pairs={{0,8},{8,16},{16,24},{24,28},{28,20},{20,12},{12,4},{4,0},{1,9},{9... | collective-permute-start | bytes 688136 | tf_op jit(solution)/shard_map/ppermute | solution.py:174
  30.4 13.4 %collective-permute-start.11 = (bf16[64,1792]{1,0:T(8,128)(2,1)S(1)}, bf16[64,1792]{1,0:T(8,128)(2,1)S(1)}, u32[]{:S(2)}, u32[]{:S(2)}) collective-permute-start(bf16[64,1792]{1,0:T(8,128)(2,1)S(1)} %collective-permute-done.7.refs_9_), channel_id=1, source_target_pairs={{8,0},{16,8},{24,16},{28,24},{20,28},{12,20},{4,12},{0,4},{9,1},{1... | collective-permute-start | bytes 688136 | tf_op jit(solution)/shard_map/ppermute | solution.py:175
  30.5 11.4 %collective-permute-start.8 = (bf16[64,1792]{1,0:T(8,128)(2,1)S(1)}, bf16[64,1792]{1,0:T(8,128)(2,1)S(1)}, u32[]{:S(2)}, u32[]{:S(2)}) collective-permute-start(bf16[64,1792]{1,0:T(8,128)(2,1)S(1)} %collective-permute-done.4.refs_6_), channel_id=1, source_target_pairs={{0,8},{8,16},{16,24},{24,28},{28,20},{20,12},{12,4},{4,0},{1,9},{9... | collective-permute-start | bytes 688136 | tf_op jit(solution)/shard_map/ppermute | solution.py:174
  37.0 19.5 %collective-permute-start.10 = (bf16[64,1792]{1,0:T(8,128)(2,1)S(1)}, bf16[64,1792]{1,0:T(8,128)(2,1)S(1)}, u32[]{:S(2)}, u32[]{:S(2)}) collective-permute-start(bf16[64,1792]{1,0:T(8,128)(2,1)S(1)} %collective-permute-done.6.refs_8_), channel_id=1, source_target_pairs={{8,0},{16,8},{24,16},{28,24},{20,28},{12,20},{4,12},{0,4},{9,1},{1... | collective-permute-start | bytes 688136 | tf_op jit(solution)/shard_map/ppermute | solution.py:175
  38.9 17.5 %collective-permute-start.9 = (bf16[64,1792]{1,0:T(8,128)(2,1)S(1)}, bf16[64,1792]{1,0:T(8,128)(2,1)S(1)}, u32[]{:S(2)}, u32[]{:S(2)}) collective-permute-start(bf16[64,1792]{1,0:T(8,128)(2,1)S(1)} %collective-permute-done.5.refs_7_), channel_id=1, source_target_pairs={{0,8},{8,16},{16,24},{24,28},{28,20},{20,12},{12,4},{4,0},{1,9},{9... | collective-permute-start | bytes 688136 | tf_op jit(solution)/shard_map/ppermute | solution.py:174
  41.9 20.4 %collective-permute-start.12 = (bf16[64,1792]{1,0:T(8,128)(2,1)S(1)}, bf16[64,1792]{1,0:T(8,128)(2,1)}, u32[]{:S(2)}, u32[]{:S(2)}) collective-permute-start(bf16[64,1792]{1,0:T(8,128)(2,1)S(1)} %collective-permute-done.8.refs_10_), channel_id=1, source_target_pairs={{0,8},{8,16},{16,24},{24,28},{28,20},{20,12},{12,4},{4,0},{1,9},{9... | collective-permute-start | bytes 688136 | tf_op jit(solution)/shard_map/ppermute | solution.py:179
  43.8 18.5 %collective-permute-start.13 = (bf16[64,1792]{1,0:T(8,128)(2,1)S(1)}, bf16[64,1792]{1,0:T(8,128)(2,1)}, u32[]{:S(2)}, u32[]{:S(2)}) collective-permute-start(bf16[64,1792]{1,0:T(8,128)(2,1)S(1)} %collective-permute-done.11.refs_13_), channel_id=1, source_target_pairs={{8,0},{16,8},{24,16},{28,24},{20,28},{12,20},{4,12},{0,4},{9,1},{1... | collective-permute-start | bytes 688136 | tf_op jit(solution)/shard_map/ppermute | solution.py:179
  44.0 2.0 %copy-start.6 = (bf16[1,1024,1792]{2,1,0:T(8,128)(2,1)S(1)}, bf16[1,1024,1792]{2,1,0:T(8,128)(2,1)}, u32[]{:S(2)}) copy-start(bf16[1,1024,1792]{2,1,0:T(8,128)(2,1)} %param.13) | copy-start | bytes 11010052
  55.2 1.3 %copy-start.7 = (bf16[1024,1024]{1,0:T(8,128)(2,1)}, bf16[1024,1024]{1,0:T(8,128)(2,1)S(1)}, u32[]{:S(2)}) copy-start(bf16[1024,1024]{1,0:T(8,128)(2,1)S(1)} %get-tuple-element.4.refs_17_) | copy-start | bytes 6291460
  56.5 3.1 %copy-start = (f32[1024,1792]{1,0:T(8,128)S(1)}, f32[1024,1792]{1,0:T(8,128)}, u32[]{:S(2)}) copy-start(f32[1024,1792]{1,0:T(8,128)} %get-tuple-element.5.refs_14_.refs_2_) | copy-start | bytes 22020100
  60.9 0.7 copy-start.2
  61.6 0.7 copy-start.4
  62.4 3.1 %copy-start.1 = (f32[1024,1792]{1,0:T(8,128)S(1)}, f32[1024,1792]{1,0:T(8,128)}, u32[]{:S(2)}) copy-start(f32[1024,1792]{1,0:T(8,128)} %get-tuple-element.5.refs_14_.refs_2_) | copy-start | bytes 22020100
  65.4 7.5 %copy-start.3 = (bf16[64,1792]{1,0:T(8,128)(2,1)S(1)}, bf16[64,1792]{1,0:T(8,128)(2,1)}, u32[]{:S(2)}) copy-start(bf16[64,1792]{1,0:T(8,128)(2,1)} %copy-done.2) | copy-start | bytes 688132
  65.4 7.5 %copy-start.5 = (bf16[64,1792]{1,0:T(8,128)(2,1)S(1)}, bf16[64,1792]{1,0:T(8,128)(2,1)}, u32[]{:S(2)}) copy-start(bf16[64,1792]{1,0:T(8,128)(2,1)} %copy-done.4) | copy-start | bytes 688132
  68.0 15.3 %all-to-all-start.1 = ((f32[32,1,128]{2,1,0:T(1,128)}), f32[32,1,128]{2,1,0:T(1,128)S(1)}, u32[]{:S(2)}, u32[]{:S(2)}) async-start(f32[32,1,128]{2,1,0:T(1,128)} %bitcast.16), calls=%async_computation.1 | async-start | bytes 32768 | tf_op jit(solution)/shard_map/all_to_all | solution.py:213
  73.0 1.6 %copy-start.8 = (bf16[1024,1024]{1,0:T(8,128)(2,1)S(1)}, bf16[1024,1024]{1,0:T(8,128)(2,1)}, u32[]{:S(2)}) copy-start(bf16[1024,1024]{1,0:T(8,128)(2,1)} %copy-done.7) | copy-start | bytes 6291460
  83.3 0.6 copy-start.9

commit v2 on v0

--- a/solution.py
+++ b/solution.py
@@ -1,10 +1,381 @@
 import jax
 import jax.numpy as jnp
 from jax import lax
+from jax.experimental import pallas as pl
+from jax.experimental.pallas import tpu as pltpu
 from jax.sharding import PartitionSpec as P
 
-
-def local(out_grad, gate_weights, routes, gate_pre, up_pre, down_weight):
+MIB = 1024 * 1024
+BF16 = jnp.bfloat16
+F32 = jnp.float32
+LANES = 128
+
+
+def vmem_spec():
+    return pl.BlockSpec(memory_space=pltpu.VMEM)
+
+
+def smem_spec():
+    return pl.BlockSpec(memory_space=pltpu.SMEM)
+
+
+def any_spec():
+    return pl.BlockSpec(memory_space=pl.ANY)
+
+
+def params(mib):
+    return pltpu.CompilerParams(vmem_limit_bytes=mib * MIB)
+
+
+def cost(flops, moved):
+    return pl.CostEstimate(flops=int(flops) // 1000, bytes_accessed=int(moved) // 1000, transcendentals=0)
+
+
+def in_hbm(x):
+    return pltpu.with_memory_space_constraint(x, pltpu.HBM)
+
+
+def ring_of(experts):
+    return list(range(0, experts, 2)) + list(range(experts - 1, 0, -2))
+
+
+def source_of(me, step, experts):
+    at = jnp.where(me % 2 == 0, me // 2, experts - 1 - me // 2)
+    at = (at + step + experts) % experts
+    return jnp.where(at < experts // 2, 2 * at, 2 * (experts - 1 - at) + 1)
+
+
+def front(out_grad, gate_pre, up_pre, gates_t, routes_t):
+    slots, width = gate_pre.shape
+    tokens, feats = out_grad.shape
+    experts = routes_t.shape[0]
+    half = tokens // 2
+    cols = feats // LANES
+    blocks = 4
+    rows = slots // blocks
+
+    def body(rows_ref, pre_ref, up_ref, g_ref, r_ref, top_ref, bottom_ref, hidden_ref, *scr):
+        rows_scr, g_scr, r_scr, pre_scr, up_scr, sems = scr
+        first = [
+            pltpu.make_async_copy(src, dst, sems.at[2 * blocks + i])
+            for i, (src, dst) in enumerate(((rows_ref, rows_scr), (g_ref, g_scr), (r_ref, r_scr)))
+        ]
+        copies = []
+        for i in range(blocks):
+            here = pl.ds(i * rows, rows)
+            copies.append(
+                [
+                    pltpu.make_async_copy(src.at[here], dst.at[here], sems.at[2 * i + j])
+                    for j, (src, dst) in enumerate(((pre_ref, pre_scr), (up_ref, up_scr)))
+                ]
+            )
+        for copy in first + sum(copies, []):
+            copy.start()
+        for copy in first:
+            copy.wait()
+        routes = r_scr[...]
+        gates = g_scr[...].astype(F32)
+        by = [
+            jnp.sum(jnp.where(routes == e, gates, 0.0), axis=0, keepdims=True) for e in range(experts)
+        ]
+        by = jnp.concatenate(by + [jnp.zeros((16 - experts, tokens), F32)], axis=0).astype(BF16)
+        for c, ref in enumerate((top_ref, bottom_ref)):
+            for j in range(cols):
+                ref[j * half : (j + 1) * half, :] = rows_scr[
+                    c * half : (c + 1) * half, j * LANES : (j + 1) * LANES
+                ]
+            ref[cols * half :, :] = by
+        for i in range(blocks):
+            for copy in copies[i]:
+                copy.wait()
+            here = pl.ds(i * rows, rows)
+            pre = pre_scr[here, :].astype(F32)
+            hidden_ref[here, :] = (pre / (1.0 + jnp.exp(-pre)) * up_scr[here, :].astype(F32)).astype(BF16)
+
+    return pl.pallas_call(
+        body,
+        in_specs=[any_spec()] * 5,
+        out_specs=[vmem_spec()] * 3,
+        out_shape=[pltpu.VMEM((cols * half + 16, LANES), BF16)] * 2 + [pltpu.VMEM((slots, width), BF16)],
+        scratch_shapes=[
+            pltpu.VMEM(out_grad.shape, BF16),
+            pltpu.VMEM(gates_t.shape, BF16),
+            pltpu.VMEM(routes_t.shape, jnp.int32),
+            pltpu.VMEM((slots, width), BF16),
+            pltpu.VMEM((slots, width), BF16),
+            pltpu.SemaphoreType.DMA((2 * blocks + 3,)),
+        ],
+        compiler_params=params(6),
+        cost_estimate=cost(8 * slots * width, 6 * slots * width),
+        name="front",
+    )(*[in_hbm(x) for x in (out_grad, gate_pre, up_pre, gates_t, routes_t)])
+
+
+def fetch(weight):
+    def body(in_ref, out_ref, sem):
+        copy = pltpu.make_async_copy(in_ref, out_ref, sem)
+        copy.start()
+        copy.wait()
+
+    return pl.pallas_call(
+        body,
+        in_specs=[any_spec()],
+        out_specs=vmem_spec(),
+        out_shape=pltpu.VMEM(weight.shape, weight.dtype),
+        scratch_shapes=[pltpu.SemaphoreType.DMA(())],
+        compiler_params=params(1),
+        cost_estimate=cost(0, 4 * weight.size),
+        name="fetch_weight",
+    )(in_hbm(weight))
+
+
+def assemble(info, parts, weight, tokens, steps):
+    slots, width = parts[0].shape
+    units, feats = weight.shape
+    groups, experts = len(parts), slots // tokens
+    cols = 256
+    blocks = feats // cols
+
+    def body(info_ref, *refs):
+        part_refs, (w_ref, ht_ref, eo_ref, h_scr) = refs[:groups], refs[groups:]
+
+        for m, ref in enumerate(part_refs):
+            at = pl.multiple_of((info_ref[0] ^ m) * width, width)
+            for i, step in enumerate(steps):
+                start = pl.multiple_of(source_of(info_ref[1], step, experts) * tokens, tokens)
+                value = ref[pl.ds(start, tokens), :]
+                here = slice(i * tokens, (i + 1) * tokens)
+                h_scr[here, pl.ds(at, width)] = value
+                ht_ref[pl.ds(at, width), here] = value.T
+        for j in range(blocks):
+            here = slice(j * cols, (j + 1) * cols)
+            eo_ref[:, here] = jnp.dot(h_scr[...], w_ref[:, here], preferred_element_type=F32)
+
+    return pl.pallas_call(
+        body,
+        in_specs=[smem_spec()] + [vmem_spec()] * (groups + 1),
+        out_specs=[vmem_spec(), vmem_spec()],
+        out_shape=[pltpu.VMEM((units, slots), BF16), pltpu.VMEM((slots, feats), F32)],
+        scratch_shapes=[pltpu.VMEM((slots, units), BF16)],
+        compiler_params=params(6),
+        cost_estimate=cost(0.5 * slots * units * feats, 4 * units * slots),
+        name="expert_out",
+    )(info, *parts, weight)
+
+
+def take(chunk_ref, eo_ref, scaled_ref, at, held_at, half, me):
+    cols = eo_ref.shape[1] // LANES
+    by = chunk_ref[cols * half :, :].astype(F32)
+    row = lax.broadcasted_iota(jnp.int32, by.shape, 0)
+    gate = jnp.sum(jnp.where(row == me, by, 0.0), axis=0, keepdims=True)
+    first = at % (2 * half)
+    gate = jnp.broadcast_to(gate, (8, gate.shape[1])).T[first : first + half, :1]
+    total = jnp.zeros((half, LANES), F32)
+    for j in range(cols):
+        value = chunk_ref[j * half : (j + 1) * half, :].astype(F32)
+        here = slice(j * LANES, (j + 1) * LANES)
+        total = total + value * eo_ref[at : at + half, here]
+        scaled_ref[held_at : held_at + half, here] = (value * gate).astype(BF16)
+    return jnp.sum(total, axis=1, keepdims=True)
+
+
+def absorb(info, chunks, expert_out, first, tokens, weigh=1):
+    half = tokens // 2
+    slots, feats = expert_out.shape
+    experts = slots // tokens
+    count = len(chunks) // 2
+
+    def body(info_ref, *refs):
+        chunk_refs, (eo_ref, sums_ref, scaled_ref, held, sems) = refs[: 2 * count], refs[2 * count :]
+        lanes, copies = [], []
+        for i in range(count):
+            sums = []
+            for c in range(2):
+                at, held_at = (first + i) * tokens + c * half, i * tokens + c * half
+                sums.append(take(chunk_refs[2 * i + c], eo_ref, held, at, held_at, half, info_ref[1]))
+            lanes.append(jnp.concatenate(sums, axis=0))
+            here = pl.ds(i * tokens, tokens)
+            copy = pltpu.make_async_copy(held.at[here], scaled_ref.at[here], sems.at[i])
+            copy.start()
+            copies.append(copy)
+        lanes += [jnp.zeros((tokens, 1), F32)] * (experts - count)
+        sums_ref[...] = jnp.concatenate(lanes, axis=1).T
+        for copy in copies:
+            copy.wait()
+
+    return pl.pallas_call(
+        body,
+        in_specs=[smem_spec()] + [vmem_spec()] * (2 * count + 1),
+        out_specs=[vmem_spec(), any_spec()],
+        out_shape=[pltpu.VMEM((experts, tokens), F32), pltpu.HBM((count * tokens, feats), BF16)],
+        scratch_shapes=[
+            pltpu.VMEM((count * tokens, feats), BF16),
+            pltpu.SemaphoreType.DMA((count,)),
+        ],
+        compiler_params=params(6),
+        cost_estimate=cost(weigh * 3 * count * tokens * feats, weigh * 8 * count * tokens * feats),
+        name="absorb",
+    )(info, *chunks, expert_out)
+
+
+def absorb_last(info, chunks, expert_out, earlier, counts, groups, steps, tokens):
+    half = tokens // 2
+    slots, feats = expert_out.shape
+    experts = slots // tokens
+    last = experts - 1
+
+    def body(info_ref, top_ref, bottom_ref, eo_ref, *refs):
+        early_refs, (out_ref, scaled_ref) = refs[: len(earlier)], refs[len(earlier) :]
+        sums = [
+            take(ref, eo_ref, scaled_ref, last * tokens + c * half, c * half, half, info_ref[1])
+            for c, ref in enumerate((top_ref, bottom_ref))
+        ]
+        own = jnp.broadcast_to(jnp.concatenate(sums, axis=0), (tokens, experts)).T
+        rows = [ref[i : i + 1, :] for ref, n in zip(early_refs, counts) for i in range(n)] + [own[0:1]]
+        for step, row in zip(steps, rows):
+            out_ref[source_of(info_ref[1], step, experts)] = jnp.broadcast_to(row, (groups, tokens))
+
+    return pl.pallas_call(
+        body,
+        in_specs=[smem_spec()] + [vmem_spec()] * (3 + len(earlier)),
+        out_specs=[vmem_spec(), vmem_spec()],
+        out_shape=[
+            jax.ShapeDtypeStruct((experts, groups, tokens), F32),
+            pltpu.VMEM((tokens, feats), BF16),
+        ],
+        compiler_params=params(4),
+        cost_estimate=cost(3 * tokens * feats, 8 * tokens * feats),
+        name="absorb_last",
+    )(info, *chunks, expert_out, *earlier)
+
+
+def weight_grad(scaled, scaled_last, hidden_t):
+    units, slots = hidden_t.shape
+    feats = scaled_last.shape[1]
+    blocks = 4
+    rows = units // blocks
+    counts = [s.shape[0] for s in scaled]
+    done = sum(counts)
+
+    def body(*refs):
+        scaled_refs = refs[: len(scaled)]
+        last_ref, ht_ref, out_ref, rows_scr, held, in_sems, out_sems = refs[len(scaled) :]
+        copies = [
+            pltpu.make_async_copy(
+                ref, rows_scr.at[pl.ds(sum(counts[:i]), counts[i])], in_sems.at[i]
+            )
+            for i, ref in enumerate(scaled_refs)
+        ]
+        for copy in copies:
+            copy.start()
+        rows_scr[done:, :] = last_ref[...]
+        for copy in copies:
+            copy.wait()
+        copies = []
+        for i in range(blocks):
+            here = pl.ds(i * rows, rows)
+            held[here, :] = jnp.dot(ht_ref[here, :], rows_scr[...], preferred_element_type=F32).astype(BF16)
+            copy = pltpu.make_async_copy(held.at[here], out_ref.at[here], out_sems.at[i])
+            copy.start()
+            copies.append(copy)
+        for copy in copies:
+            copy.wait()
+
+    return pl.pallas_call(
+        body,
+        in_specs=[any_spec()] * len(scaled) + [vmem_spec()] * 2,
+        out_specs=any_spec(),
+        out_shape=jax.ShapeDtypeStruct((units, feats), BF16),
+        scratch_shapes=[
+            pltpu.VMEM((slots, feats), BF16),
+            pltpu.VMEM((units, feats), BF16),
+            pltpu.SemaphoreType.DMA((len(scaled),)),
+            pltpu.SemaphoreType.DMA((blocks,)),
+        ],
+        compiler_params=params(12),
+        cost_estimate=cost(2 * slots * units * feats, 4 * units * feats),
+        name="weight_grad",
+    )(*[in_hbm(s) for s in scaled], scaled_last, hidden_t)
+
+
+def pick(returned, routes_t):
+    topk, tokens = routes_t.shape
+    experts, groups, _ = returned.shape
+
+    def body(back_ref, routes_ref, out_ref):
+        routes = routes_ref[...]
+        total = jnp.zeros((topk, tokens), F32)
+        for e in range(experts):
+            value = jnp.sum(back_ref[e], axis=0, keepdims=True)
+            total = jnp.where(routes == e, jnp.broadcast_to(value, total.shape), total)
+        out_ref[...] = total
+
+    return pl.pallas_call(
+        body,
+        in_specs=[vmem_spec(), vmem_spec()],
+        out_specs=vmem_spec(),
+        out_shape=jax.ShapeDtypeStruct((topk, tokens), F32),
+        compiler_params=params(2),
+        name="pick_gate_grad",
+    )(returned, routes_t)
+
+
+def dense(out_grad, gate_weights, routes, gate_pre, up_pre, down_weight):
+    tokens, topk = routes.shape
+    experts, groups = lax.axis_size("ep"), lax.axis_size("et")
+    weight = down_weight[0]
+    barrier = lax.optimization_barrier
+
+    ring = ring_of(experts)
+    forth = [(ring[i], ring[(i + 1) % experts]) for i in range(experts)]
+    back = [(b, a) for a, b in forth]
+    far = experts // 2
+    steps = [0] + [s for k in range(1, far) for s in (-k, k)] + [far]
+    info = jnp.stack([lax.axis_index("et").astype(jnp.int32), lax.axis_index("ep").astype(jnp.int32)])
+    out_grad, info = barrier((out_grad, info))
+
+    top, bottom, hidden = front(out_grad, gate_pre[0], up_pre[0], gate_weights.T, routes.T)
+    chips, cores = [(i, i ^ 2) for i in range(groups)], [(i, i ^ 1) for i in range(groups)]
+
+    def hop(c):
+        up[c] = lax.ppermute(up[c], "ep", forth)
+        down[c] = lax.ppermute(down[c], "ep", back)
+
+    up, down = [top, bottom], [bottom, top]
+    chunks = [top, bottom]
+    hop(0)
+    hop(1)
+    chunks += [up[0], up[1], down[1], down[0]]
+    over = lax.ppermute(hidden, "et", chips)
+    beside, across = lax.ppermute(hidden, "et", cores), lax.ppermute(over, "et", cores)
+    weight, _ = barrier((weight, up[0]))
+    weight = fetch(weight)
+
+    hop(0)
+    hop(1)
+    chunks += [up[0], up[1], down[1], down[0]]
+    up[0], weight = barrier((up[0], weight))
+
+    hop(0)
+    hop(1)
+    third = [up[0], up[1], down[1], down[0]]
+
+    hop(0)
+    hidden_t, expert_out = assemble(info, [hidden, beside, over, across], weight, tokens, steps)
+    sums_a, scaled_a = absorb(info, chunks, expert_out, 0, tokens)
+    sums_b, scaled_b = absorb(info, third, expert_out, 5, tokens, 3000)
+    outgoing, scaled_c = absorb_last(
+        info, [up[0], down[0]], expert_out, [sums_a, sums_b], [5, 2], groups, steps, tokens
+    )
+    returned = lax.all_to_all(
+        outgoing.reshape(experts * groups, tokens), ("ep", "et"), split_axis=0, concat_axis=0, tiled=True
+    )
+    grad = weight_grad([scaled_a, scaled_b], scaled_c, hidden_t)
+    d_gate = pick(returned.reshape(experts, groups, tokens), routes.T).T
+    return grad[None], d_gate
+
+
+def routed(out_grad, gate_weights, routes, gate_pre, up_pre, down_weight):
     tok_rows, topk = routes.shape
     experts = lax.axis_size("ep")
     slot_total = gate_pre.shape[1]
@@ -38,11 +409,9 @@
     )
     piece = lax.all_gather(hidden_part, "et", axis=1, tiled=True)
     expert_out = jnp.dot(piece, weight, preferred_element_type=jnp.float32)
-    block = lax.dot_general(
+    grad_weight = lax.dot_general(
         piece, scaled, (((0,), (0,)), ((), ())), preferred_element_type=jnp.float32
     )
-    grad_weight = block
-    expert_out, grad_weight = (expert_out, grad_weight)
     partial_grad = jnp.sum(rows_in.astype(jnp.float32) * expert_out, axis=1)
     slot_grad = lax.psum(partial_grad, "et")
     returned = lax.all_to_all(
@@ -53,6 +422,15 @@
 
 
 def solution(mesh):
+    sizes = dict(mesh.shape)
+
+    def local(out_grad, gate_weights, routes, gate_pre, up_pre, down_weight):
+        tokens, topk = routes.shape
+        whole = topk == sizes["ep"] and gate_pre.shape[1] == topk * tokens
+        if whole and sizes["ep"] == 8 and sizes["et"] == 4:
+            return dense(out_grad, gate_weights, routes, gate_pre, up_pre, down_weight)
+        return routed(out_grad, gate_weights, routes, gate_pre, up_pre, down_weight)
+
     in_specs = (
         P("ep", "et"),
         P("ep", None),

time: 173 us -> 62.3 us (0.36)
  waiting for transfers between devices: 80.3 us -> 15.2 us
  local copies, waits for them, and re-layouts: 29.6 us -> 0.01 us
  Pallas kernels: 0 us -> 22.2 us
  matrix products: 15.9 us -> 0 us
  between operations: 14.2 us -> 0.75 us
  other arithmetic: 8.6 us -> 0.08 us
  blocking collectives: 6.26 us -> 0 us
  starting transfers between devices: 18.3 us -> 23.9 us
    all_to_all x3 -> x1, waiting for transfers between devices: 54.8 us -> 0.31 us  [dense(): lax.all_to_all(outgoing.reshape(experts * groups, tokens), ('ep', 'et'),...]
    all_gather x1 -> x0, waiting for transfers between devices: 25.4 us -> none  [local(): piece = lax.all_gather(hidden_part, 'et', axis=1, tiled=True)]
    pallas_call x0 -> x8, Pallas kernels: none -> 22.2 us  [the longest x1 6.81 us: weight_grad(): pl.pallas_call(body, in_specs=[any_spec()] * len(scaled) + [vmem_spec()]...]
    ppermute x0 -> x17, starting transfers between devices: none -> 18.4 us  [the longest x7 10.8 us: hop(): up[c] = lax.ppermute(up[c], 'ep', forth)]
    gather x3 -> x0, local copies, waits for them, and re-layouts: 17.1 us -> none  [the longest x1 6.8 us: local(): send_gates = jnp.where(filled, gate_weights.reshape(-1)[slot_pair], 0.0)]
    dot_general x2 -> x0, matrix products: 15.9 us -> none  [the longest x1 7.96 us: local(): lax.dot_general(piece, scaled, (((0,), (0,)), ((), ())), preferred_elemen...]
    ppermute x0 -> x17, waiting for transfers between devices: none -> 14.9 us  [the longest x7 10.2 us: hop(): up[c] = lax.ppermute(up[c], 'ep', forth)]
    all_to_all x3 -> x1, starting transfers between devices: 18.2 us -> 5.54 us  [dense(): lax.all_to_all(outgoing.reshape(experts * groups, tokens), ('ep', 'et'),...]
  transfers between devices with their start and end apart: 4 -> 18, of which waited for: 2 -> 7; matrix products, arithmetic and copies ran while one was open for 11% -> 0% of each run, Pallas kernels for 0% -> 30%
where the time goes in v2:
time: 62.3 us; the launch traced here: 62.1 us
  starting transfers between devices  23.9 us (38%)
  Pallas kernels  22.2 us (36%)
  waiting for transfers between devices  15.2 us (24%)
  between operations  0.75 us (1%)
    ppermute x7, starting transfers between devices, hop(): up[c] = lax.ppermute(up[c], 'ep', forth)  10.8 us
    ppermute x7, waiting for transfers between devices, hop(): up[c] = lax.ppermute(up[c], 'ep', forth)  10.2 us
    pallas_call x1, Pallas kernels, weight_grad(): pl.pallas_call(body, in_specs=[any_spec()] * len(scaled) + [vmem_spec()]...  6.81 us
    all_to_all x1, starting transfers between devices, dense(): lax.all_to_all(outgoing.reshape(experts * groups, tokens), ('ep', 'et'),...  5.54 us
    pallas_call x1, Pallas kernels, assemble(): pl.pallas_call(body, in_specs=[smem_spec()] + [vmem_spec()] * (groups + 1...  4.93 us
    pallas_call x2, Pallas kernels, absorb(): pl.pallas_call(body, in_specs=[smem_spec()] + [vmem_spec()] * (2 * count...  4.68 us
    ppermute x7, waiting for transfers between devices, hop(): down[c] = lax.ppermute(down[c], 'ep', back)  4.66 us
    ppermute x7, starting transfers between devices, hop(): down[c] = lax.ppermute(down[c], 'ep', back)  4.5 us
  transfers between devices with their start and end apart: 18, of which 7 were waited for; matrix products, arithmetic and copies ran while one was open for 0% of the time, Pallas kernels for 30%

profile of v2, /device:TPU:0, one launch (start us, length us, event | category | flops | bytes accessed | tf_op | source)
XLA Modules:
  0.0 62.1 jit_solution(17301480668312417430)
XLA Ops:
  0.6 0.1 pad_add_fusion.info_ref
  0.7 1.6 %front.1 = (bf16[912,128]{1,0:T(8,128)(2,1)S(1)}, bf16[912,128]{1,0:T(8,128)(2,1)S(1)}, bf16[1024,256]{1,0:T(8,128)(2,1)S(1)}) custom-call(bf16[128,1792]{1,0:T(8,128)(2,1)} %rows_ref, bf16[1024,256]{1,0:T(8,128)(2,1)} %bitcast.18, bf16[1024,256]{1,0:T(8,128)(2,1)} %bitcast.19, bf16[8,128]{1,0:T(8,128)(2,1)} %bitcast.21, s32[8,128]{1,0:T(8,128)} %bitcast.14), custom_call_target="tpu_custom_call" | custom-call | flops 2097 | bytes 1572 | tf_op jit(solution)/shard_map/front/pallas_call | solution.py:95
  2.3 3.0 %collective-permute-start.9 = (bf16[1024,256]{1,0:T(8,128)(2,1)S(1)}, bf16[1024,256]{1,0:T(8,128)(2,1)S(1)}, u32[]{:S(2)}, u32[]{:S(2)}) collective-permute-start(bf16[1024,256]{1,0:T(8,128)(2,1)S(1)} %get-tuple-element.22.refs_0_), channel_id=1, source_target_pairs={{0,2},{1,3},{2,0},{3,1},{4,6},{5,7},{6,4},{7,5},{8,10},{9,11},{10,... | collective-permute-start | bytes 1572872 | tf_op jit(solution)/shard_map/ppermute | solution.py:349
  5.4 1.6 %collective-permute-start = (bf16[912,128]{1,0:T(8,128)(2,1)S(1)}, bf16[912,128]{1,0:T(8,128)(2,1)S(1)}, u32[]{:S(2)}, u32[]{:S(2)}) collective-permute-start(bf16[912,128]{1,0:T(8,128)(2,1)S(1)} %get-tuple-element.20.refs_0_), channel_id=1, source_target_pairs={{0,8},{8,16},{16,24},{24,28},{28,20},{20,12},{12,4},{4,0},{1,9},{9... | collective-permute-start | bytes 700424 | tf_op jit(solution)/shard_map/ppermute | solution.py:341
  6.9 0.4 collective-permute-start.3
  7.4 1.6 %collective-permute-start.1 = (bf16[912,128]{1,0:T(8,128)(2,1)S(1)}, bf16[912,128]{1,0:T(8,128)(2,1)S(1)}, u32[]{:S(2)}, u32[]{:S(2)}) collective-permute-start(bf16[912,128]{1,0:T(8,128)(2,1)S(1)} %get-tuple-element.21.refs_1_), channel_id=1, source_target_pairs={{0,8},{8,16},{16,24},{24,28},{28,20},{20,12},{12,4},{4,0},{1,9},{9... | collective-permute-start | bytes 700424 | tf_op jit(solution)/shard_map/ppermute | solution.py:341
  9.0 0.4 collective-permute-start.2
  9.4 4.6 %collective-permute-done.refs_2_ = bf16[912,128]{1,0:T(8,128)(2,1)S(1)} collective-permute-done((bf16[912,128]{1,0:T(8,128)(2,1)S(1)}, bf16[912,128]{1,0:T(8,128)(2,1)S(1)}, u32[]{:S(2)}, u32[]{:S(2)}) %collective-permute-start) | collective-permute-done | bytes 233504 | tf_op jit(solution)/shard_map/ppermute | solution.py:341
  14.0 0.0 collective-permute-start.8
  14.0 1.6 %collective-permute-done.3.refs_5_ = bf16[912,128]{1,0:T(8,128)(2,1)S(1)} collective-permute-done((bf16[912,128]{1,0:T(8,128)(2,1)S(1)}, bf16[912,128]{1,0:T(8,128)(2,1)S(1)}, u32[]{:S(2)}, u32[]{:S(2)}) %collective-permute-start.3) | collective-permute-done | bytes 233504 | tf_op jit(solution)/shard_map/ppermute | solution.py:342
  15.6 1.6 %collective-permute-start.4 = (bf16[912,128]{1,0:T(8,128)(2,1)S(1)}, bf16[912,128]{1,0:T(8,128)(2,1)S(1)}, u32[]{:S(2)}, u32[]{:S(2)}) collective-permute-start(bf16[912,128]{1,0:T(8,128)(2,1)S(1)} %collective-permute-done.refs_2_), channel_id=1, source_target_pairs={{0,8},{8,16},{16,24},{24,28},{28,20},{20,12},{12,4},{4,0},{1,9},{9... | collective-permute-start | bytes 700424 | tf_op jit(solution)/shard_map/ppermute | solution.py:341
  17.1 0.7 %collective-permute-done.1.refs_3_ = bf16[912,128]{1,0:T(8,128)(2,1)S(1)} collective-permute-done((bf16[912,128]{1,0:T(8,128)(2,1)S(1)}, bf16[912,128]{1,0:T(8,128)(2,1)S(1)}, u32[]{:S(2)}, u32[]{:S(2)}) %collective-permute-start.1) | collective-permute-done | bytes 233504 | tf_op jit(solution)/shard_map/ppermute | solution.py:341
  17.9 1.5 %collective-permute-start.7 = (bf16[912,128]{1,0:T(8,128)(2,1)S(1)}, bf16[912,128]{1,0:T(8,128)(2,1)S(1)}, u32[]{:S(2)}, u32[]{:S(2)}) collective-permute-start(bf16[912,128]{1,0:T(8,128)(2,1)S(1)} %collective-permute-done.3.refs_5_), channel_id=1, source_target_pairs={{8,0},{16,8},{24,16},{28,24},{20,28},{12,20},{4,12},{0,4},{9,1},{1... | collective-permute-start | bytes 700424 | tf_op jit(solution)/shard_map/ppermute | solution.py:342
  19.4 0.0 collective-permute-done.2.refs_4_
  19.4 1.0 %collective-permute-start.5 = (bf16[912,128]{1,0:T(8,128)(2,1)S(1)}, bf16[912,128]{1,0:T(8,128)(2,1)S(1)}, u32[]{:S(2)}, u32[]{:S(2)}) collective-permute-start(bf16[912,128]{1,0:T(8,128)(2,1)S(1)} %collective-permute-done.1.refs_3_), channel_id=1, source_target_pairs={{0,8},{8,16},{16,24},{24,28},{28,20},{20,12},{12,4},{4,0},{1,9},{9... | collective-permute-start | bytes 700424 | tf_op jit(solution)/shard_map/ppermute | solution.py:341
  20.4 0.0 collective-permute-done.9.refs_2_
  20.4 0.0 collective-permute-start.10
  20.4 3.8 %collective-permute-done.4.refs_6_ = bf16[912,128]{1,0:T(8,128)(2,1)S(1)} collective-permute-done((bf16[912,128]{1,0:T(8,128)(2,1)S(1)}, bf16[912,128]{1,0:T(8,128)(2,1)S(1)}, u32[]{:S(2)}, u32[]{:S(2)}) %collective-permute-start.4) | collective-permute-done | bytes 233504 | tf_op jit(solution)/shard_map/ppermute | solution.py:341
  24.2 0.4 collective-permute-start.6
  24.6 2.0 %fetch_weight.1.refs_4_ = bf16[1024,1792]{1,0:T(8,128)(2,1)S(1)} custom-call(bf16[1024,1792]{1,0:T(8,128)(2,1)} %bitcast.16), custom_call_target="tpu_custom_call" | custom-call | bytes 7340 | tf_op jit(solution)/shard_map/fetch_weight/pallas_call | solution.py:120
  26.6 0.0 collective-permute-done.7.refs_9_
  26.7 1.7 %collective-permute-start.11 = (bf16[912,128]{1,0:T(8,128)(2,1)S(1)}, bf16[912,128]{1,0:T(8,128)(2,1)S(1)}, u32[]{:S(2)}, u32[]{:S(2)}) collective-permute-start(bf16[912,128]{1,0:T(8,128)(2,1)S(1)} %collective-permute-done.4.refs_6_), channel_id=1, source_target_pairs={{0,8},{8,16},{16,24},{24,28},{28,20},{20,12},{12,4},{4,0},{1,9},{9... | collective-permute-start | bytes 700424 | tf_op jit(solution)/shard_map/ppermute | solution.py:341
  28.3 0.0 collective-permute-done.5.refs_7_
  28.4 0.7 %collective-permute-start.14 = (bf16[912,128]{1,0:T(8,128)(2,1)S(1)}, bf16[912,128]{1,0:T(8,128)(2,1)S(1)}, u32[]{:S(2)}, u32[]{:S(2)}) collective-permute-start(bf16[912,128]{1,0:T(8,128)(2,1)S(1)} %collective-permute-done.7.refs_9_), channel_id=1, source_target_pairs={{8,0},{16,8},{24,16},{28,24},{20,28},{12,20},{4,12},{0,4},{9,1},{1... | collective-permute-start | bytes 700424 | tf_op jit(solution)/shard_map/ppermute | solution.py:342
  29.0 3.0 %collective-permute-done.6.refs_8_ = bf16[912,128]{1,0:T(8,128)(2,1)S(1)} collective-permute-done((bf16[912,128]{1,0:T(8,128)(2,1)S(1)}, bf16[912,128]{1,0:T(8,128)(2,1)S(1)}, u32[]{:S(2)}, u32[]{:S(2)}) %collective-permute-start.6) | collective-permute-done | bytes 233504 | tf_op jit(solution)/shard_map/ppermute | solution.py:342
  32.0 1.6 %collective-permute-start.12 = (bf16[912,128]{1,0:T(8,128)(2,1)S(1)}, bf16[912,128]{1,0:T(8,128)(2,1)S(1)}, u32[]{:S(2)}, u32[]{:S(2)}) collective-permute-start(bf16[912,128]{1,0:T(8,128)(2,1)S(1)} %collective-permute-done.5.refs_7_), channel_id=1, source_target_pairs={{0,8},{8,16},{16,24},{24,28},{28,20},{20,12},{12,4},{4,0},{1,9},{9... | collective-permute-start | bytes 700424 | tf_op jit(solution)/shard_map/ppermute | solution.py:341
  33.6 0.0 collective-permute-done.8.refs_1_
  33.6 0.5 collective-permute-start.13
  34.1 1.1 %collective-permute-done.11.refs_0_ = bf16[912,128]{1,0:T(8,128)(2,1)S(1)} collective-permute-done((bf16[912,128]{1,0:T(8,128)(2,1)S(1)}, bf16[912,128]{1,0:T(8,128)(2,1)S(1)}, u32[]{:S(2)}, u32[]{:S(2)}) %collective-permute-start.11) | collective-permute-done | bytes 233504 | tf_op jit(solution)/shard_map/ppermute | solution.py:341
  35.2 1.8 %collective-permute-start.15 = (bf16[912,128]{1,0:T(8,128)(2,1)S(1)}, bf16[912,128]{1,0:T(8,128)(2,1)S(1)}, u32[]{:S(2)}, u32[]{:S(2)}) collective-permute-start(bf16[912,128]{1,0:T(8,128)(2,1)S(1)} %collective-permute-done.11.refs_0_), channel_id=1, source_target_pairs={{0,8},{8,16},{16,24},{24,28},{28,20},{20,12},{12,4},{4,0},{1,9},{9... | collective-permute-start | bytes 700424 | tf_op jit(solution)/shard_map/ppermute | solution.py:341
  37.0 0.1 collective-permute-done.14.refs_3_
  37.0 0.6 collective-permute-start.16
  37.6 0.0 collective-permute-done.10.refs_3_
  37.6 4.9 %expert_out.1 = (bf16[1024,1024]{1,0:T(8,128)(2,1)S(1)}, f32[1024,1792]{1,0:T(8,128)S(1)}) custom-call(s32[2]{0:T(128)S(1)} %pad_add_fusion.info_ref, bf16[1024,256]{1,0:T(8,128)(2,1)S(1)} %get-tuple-element.22.refs_0_, bf16[1024,256]{1,0:T(8,128)(2,1)S(1)} %collective-permute-done.8.refs_1_, bf16[1024,256]{1,0:T(8,128)(2,1)S(1)} %collective-permute-done.9.refs_2_, ...), custom_call_target="tpu_custom_call" | custom-call | flops 939524 | bytes 4194 | tf_op jit(solution)/shard_map/expert_out/pallas_call | solution.py:154
  42.6 2.8 %absorb.2 = (f32[8,128]{1,0:T(8,128)S(1)}, bf16[640,1792]{1,0:T(8,128)(2,1)}) custom-call(s32[2]{0:T(128)S(1)} %pad_add_fusion.info_ref, bf16[912,128]{1,0:T(8,128)(2,1)S(1)} %get-tuple-element.20.refs_0_, bf16[912,128]{1,0:T(8,128)(2,1)S(1)} %get-tuple-element.21.refs_1_, bf16[912,128]{1,0:T(8,128)(2,1)S(1)} %collective-permute-done.refs_2_, ...), custom_call_target="tpu_custom_call" | custom-call | flops 3440 | bytes 9175 | tf_op jit(solution)/shard_map/absorb/pallas_call | solution.py:206
  45.3 0.0 collective-permute-done.12.refs_1_
  45.4 0.0 collective-permute-done.13.refs_2_
  45.4 1.9 %absorb.3 = (f32[8,128]{1,0:T(8,128)S(1)}, bf16[256,1792]{1,0:T(8,128)(2,1)}) custom-call(s32[2]{0:T(128)S(1)} %pad_add_fusion.info_ref, bf16[912,128]{1,0:T(8,128)(2,1)S(1)} %collective-permute-done.11.refs_0_, bf16[912,128]{1,0:T(8,128)(2,1)S(1)} %collective-permute-done.12.refs_1_, bf16[912,128]{1,0:T(8,128)(2,1)S(1)} %collective-permute-done.13.refs_2_, ...), custom_call_target="tpu_custom_call" | custom-call | flops 4128768 | bytes 11010048 | tf_op jit(solution)/shard_map/absorb/pallas_call | solution.py:206
  47.3 0.0 collective-permute-done.15.top_ref
  47.3 0.0 collective-permute-done.16.bottom_ref
  47.3 1.5 %absorb_last.1 = (f32[8,4,128]{2,1,0:T(4,128)}, bf16[128,1792]{1,0:T(8,128)(2,1)S(1)}) custom-call(s32[2]{0:T(128)S(1)} %pad_add_fusion.info_ref, bf16[912,128]{1,0:T(8,128)(2,1)S(1)} %collective-permute-done.15.top_ref, bf16[912,128]{1,0:T(8,128)(2,1)S(1)} %collective-permute-done.16.bottom_ref, f32[1024,1792]{1,0:T(8,128)S(1)} %get-tuple-element.25.refs_10_.refs_4_.eo_ref, ...), custom_call_target="tpu_custom_call" | custom-call | flops 688 | bytes 1835 | tf_op jit(solution)/shard_map/absorb_last/pallas_call | solution.py:238
  48.8 5.5 %all-to-all-start = ((f32[32,1,128]{2,1,0:T(1,128)}), f32[32,1,128]{2,1,0:T(1,128)S(1)}, u32[]{:S(2)}, u32[]{:S(2)}) async-start(f32[32,1,128]{2,1,0:T(1,128)} %bitcast.9), calls=%async_computation | async-start | bytes 32768 | tf_op jit(solution)/shard_map/all_to_all | solution.py:370
  54.3 0.0 copy-start
  54.4 6.8 %weight_grad.1 = bf16[1024,1792]{1,0:T(8,128)(2,1)} custom-call(bf16[640,1792]{1,0:T(8,128)(2,1)} %get-tuple-element.26.refs_0_, bf16[256,1792]{1,0:T(8,128)(2,1)} %get-tuple-element.28.refs_1_, bf16[128,1792]{1,0:T(8,128)(2,1)S(1)} %get-tuple-element.31.refs_2_, bf16[1024,1024]{1,0:T(8,128)(2,1)S(1)} %get-tuple-element.32.refs_3_), custom_call_target="tpu_custom_call" | custom-call | flops 3758096 | bytes 7340 | tf_op jit(solution)/shard_map/weight_grad/pallas_call | solution.py:284
  61.2 0.3 all-to-all-done
  61.5 0.0 copy-done
  61.5 0.6 pick_gate_grad.1
Async XLA Ops:
  2.3 18.1 %collective-permute-start.9 = (bf16[1024,256]{1,0:T(8,128)(2,1)S(1)}, bf16[1024,256]{1,0:T(8,128)(2,1)S(1)}, u32[]{:S(2)}, u32[]{:S(2)}) collective-permute-start(bf16[1024,256]{1,0:T(8,128)(2,1)S(1)} %get-tuple-element.22.refs_0_), channel_id=1, source_target_pairs={{0,2},{1,3},{2,0},{3,1},{4,6},{5,7},{6,4},{7,5},{8,10},{9,11},{10,... | collective-permute-start | bytes 1572872 | tf_op jit(solution)/shard_map/ppermute | solution.py:349
  5.4 8.6 %collective-permute-start = (bf16[912,128]{1,0:T(8,128)(2,1)S(1)}, bf16[912,128]{1,0:T(8,128)(2,1)S(1)}, u32[]{:S(2)}, u32[]{:S(2)}) collective-permute-start(bf16[912,128]{1,0:T(8,128)(2,1)S(1)} %get-tuple-element.20.refs_0_), channel_id=1, source_target_pairs={{0,8},{8,16},{16,24},{24,28},{28,20},{20,12},{12,4},{4,0},{1,9},{9... | collective-permute-start | bytes 700424 | tf_op jit(solution)/shard_map/ppermute | solution.py:341
  6.9 8.6 %collective-permute-start.3 = (bf16[912,128]{1,0:T(8,128)(2,1)S(1)}, bf16[912,128]{1,0:T(8,128)(2,1)S(1)}, u32[]{:S(2)}, u32[]{:S(2)}) collective-permute-start(bf16[912,128]{1,0:T(8,128)(2,1)S(1)} %get-tuple-element.21.refs_1_), channel_id=1, source_target_pairs={{8,0},{16,8},{24,16},{28,24},{20,28},{12,20},{4,12},{0,4},{9,1},{1... | collective-permute-start | bytes 700424 | tf_op jit(solution)/shard_map/ppermute | solution.py:342
  7.4 10.5 %collective-permute-start.1 = (bf16[912,128]{1,0:T(8,128)(2,1)S(1)}, bf16[912,128]{1,0:T(8,128)(2,1)S(1)}, u32[]{:S(2)}, u32[]{:S(2)}) collective-permute-start(bf16[912,128]{1,0:T(8,128)(2,1)S(1)} %get-tuple-element.21.refs_1_), channel_id=1, source_target_pairs={{0,8},{8,16},{16,24},{24,28},{28,20},{20,12},{12,4},{4,0},{1,9},{9... | collective-permute-start | bytes 700424 | tf_op jit(solution)/shard_map/ppermute | solution.py:341
  9.0 10.4 %collective-permute-start.2 = (bf16[912,128]{1,0:T(8,128)(2,1)S(1)}, bf16[912,128]{1,0:T(8,128)(2,1)S(1)}, u32[]{:S(2)}, u32[]{:S(2)}) collective-permute-start(bf16[912,128]{1,0:T(8,128)(2,1)S(1)} %get-tuple-element.20.refs_0_), channel_id=1, source_target_pairs={{8,0},{16,8},{24,16},{28,24},{20,28},{12,20},{4,12},{0,4},{9,1},{1... | collective-permute-start | bytes 700424 | tf_op jit(solution)/shard_map/ppermute | solution.py:342
  14.0 19.6 %collective-permute-start.8 = (bf16[1024,256]{1,0:T(8,128)(2,1)S(1)}, bf16[1024,256]{1,0:T(8,128)(2,1)S(1)}, u32[]{:S(2)}, u32[]{:S(2)}) collective-permute-start(bf16[1024,256]{1,0:T(8,128)(2,1)S(1)} %get-tuple-element.22.refs_0_), channel_id=1, source_target_pairs={{0,1},{1,0},{2,3},{3,2},{4,5},{5,4},{6,7},{7,6},{8,9},{9,8},{10,11... | collective-permute-start | bytes 1572872 | tf_op jit(solution)/shard_map/ppermute | solution.py:350
  15.6 8.6 %collective-permute-start.4 = (bf16[912,128]{1,0:T(8,128)(2,1)S(1)}, bf16[912,128]{1,0:T(8,128)(2,1)S(1)}, u32[]{:S(2)}, u32[]{:S(2)}) collective-permute-start(bf16[912,128]{1,0:T(8,128)(2,1)S(1)} %collective-permute-done.refs_2_), channel_id=1, source_target_pairs={{0,8},{8,16},{16,24},{24,28},{28,20},{20,12},{12,4},{4,0},{1,9},{9... | collective-permute-start | bytes 700424 | tf_op jit(solution)/shard_map/ppermute | solution.py:341
  17.9 8.8 %collective-permute-start.7 = (bf16[912,128]{1,0:T(8,128)(2,1)S(1)}, bf16[912,128]{1,0:T(8,128)(2,1)S(1)}, u32[]{:S(2)}, u32[]{:S(2)}) collective-permute-start(bf16[912,128]{1,0:T(8,128)(2,1)S(1)} %collective-permute-done.3.refs_5_), channel_id=1, source_target_pairs={{8,0},{16,8},{24,16},{28,24},{20,28},{12,20},{4,12},{0,4},{9,1},{1... | collective-permute-start | bytes 700424 | tf_op jit(solution)/shard_map/ppermute | solution.py:342
  19.4 9.0 %collective-permute-start.5 = (bf16[912,128]{1,0:T(8,128)(2,1)S(1)}, bf16[912,128]{1,0:T(8,128)(2,1)S(1)}, u32[]{:S(2)}, u32[]{:S(2)}) collective-permute-start(bf16[912,128]{1,0:T(8,128)(2,1)S(1)} %collective-permute-done.1.refs_3_), channel_id=1, source_target_pairs={{0,8},{8,16},{16,24},{24,28},{28,20},{20,12},{12,4},{4,0},{1,9},{9... | collective-permute-start | bytes 700424 | tf_op jit(solution)/shard_map/ppermute | solution.py:341
  20.4 17.2 %collective-permute-start.10 = (bf16[1024,256]{1,0:T(8,128)(2,1)S(1)}, bf16[1024,256]{1,0:T(8,128)(2,1)S(1)}, u32[]{:S(2)}, u32[]{:S(2)}) collective-permute-start(bf16[1024,256]{1,0:T(8,128)(2,1)S(1)} %collective-permute-done.9.refs_2_), channel_id=1, source_target_pairs={{0,1},{1,0},{2,3},{3,2},{4,5},{5,4},{6,7},{7,6},{8,9},{9,8},{10,11... | collective-permute-start | bytes 1572872 | tf_op jit(solution)/shard_map/ppermute | solution.py:350
  24.2 7.8 %collective-permute-start.6 = (bf16[912,128]{1,0:T(8,128)(2,1)S(1)}, bf16[912,128]{1,0:T(8,128)(2,1)S(1)}, u32[]{:S(2)}, u32[]{:S(2)}) collective-permute-start(bf16[912,128]{1,0:T(8,128)(2,1)S(1)} %collective-permute-done.2.refs_4_), channel_id=1, source_target_pairs={{8,0},{16,8},{24,16},{28,24},{20,28},{12,20},{4,12},{0,4},{9,1},{1... | collective-permute-start | bytes 700424 | tf_op jit(solution)/shard_map/ppermute | solution.py:342
  26.7 8.5 %collective-permute-start.11 = (bf16[912,128]{1,0:T(8,128)(2,1)S(1)}, bf16[912,128]{1,0:T(8,128)(2,1)S(1)}, u32[]{:S(2)}, u32[]{:S(2)}) collective-permute-start(bf16[912,128]{1,0:T(8,128)(2,1)S(1)} %collective-permute-done.4.refs_6_), channel_id=1, source_target_pairs={{0,8},{8,16},{16,24},{24,28},{28,20},{20,12},{12,4},{4,0},{1,9},{9... | collective-permute-start | bytes 700424 | tf_op jit(solution)/shard_map/ppermute | solution.py:341
  28.4 8.7 %collective-permute-start.14 = (bf16[912,128]{1,0:T(8,128)(2,1)S(1)}, bf16[912,128]{1,0:T(8,128)(2,1)S(1)}, u32[]{:S(2)}, u32[]{:S(2)}) collective-permute-start(bf16[912,128]{1,0:T(8,128)(2,1)S(1)} %collective-permute-done.7.refs_9_), channel_id=1, source_target_pairs={{8,0},{16,8},{24,16},{28,24},{20,28},{12,20},{4,12},{0,4},{9,1},{1... | collective-permute-start | bytes 700424 | tf_op jit(solution)/shard_map/ppermute | solution.py:342
  32.0 13.3 %collective-permute-start.12 = (bf16[912,128]{1,0:T(8,128)(2,1)S(1)}, bf16[912,128]{1,0:T(8,128)(2,1)S(1)}, u32[]{:S(2)}, u32[]{:S(2)}) collective-permute-start(bf16[912,128]{1,0:T(8,128)(2,1)S(1)} %collective-permute-done.5.refs_7_), channel_id=1, source_target_pairs={{0,8},{8,16},{16,24},{24,28},{28,20},{20,12},{12,4},{4,0},{1,9},{9... | collective-permute-start | bytes 700424 | tf_op jit(solution)/shard_map/ppermute | solution.py:341
  33.6 11.8 %collective-permute-start.13 = (bf16[912,128]{1,0:T(8,128)(2,1)S(1)}, bf16[912,128]{1,0:T(8,128)(2,1)S(1)}, u32[]{:S(2)}, u32[]{:S(2)}) collective-permute-start(bf16[912,128]{1,0:T(8,128)(2,1)S(1)} %collective-permute-done.6.refs_8_), channel_id=1, source_target_pairs={{8,0},{16,8},{24,16},{28,24},{20,28},{12,20},{4,12},{0,4},{9,1},{1... | collective-permute-start | bytes 700424 | tf_op jit(solution)/shard_map/ppermute | solution.py:342
  35.2 12.1 %collective-permute-start.15 = (bf16[912,128]{1,0:T(8,128)(2,1)S(1)}, bf16[912,128]{1,0:T(8,128)(2,1)S(1)}, u32[]{:S(2)}, u32[]{:S(2)}) collective-permute-start(bf16[912,128]{1,0:T(8,128)(2,1)S(1)} %collective-permute-done.11.refs_0_), channel_id=1, source_target_pairs={{0,8},{8,16},{16,24},{24,28},{28,20},{20,12},{12,4},{4,0},{1,9},{9... | collective-permute-start | bytes 700424 | tf_op jit(solution)/shard_map/ppermute | solution.py:341
  37.0 10.3 %collective-permute-start.16 = (bf16[912,128]{1,0:T(8,128)(2,1)S(1)}, bf16[912,128]{1,0:T(8,128)(2,1)S(1)}, u32[]{:S(2)}, u32[]{:S(2)}) collective-permute-start(bf16[912,128]{1,0:T(8,128)(2,1)S(1)} %collective-permute-done.14.refs_3_), channel_id=1, source_target_pairs={{8,0},{16,8},{24,16},{28,24},{20,28},{12,20},{4,12},{0,4},{9,1},{1... | collective-permute-start | bytes 700424 | tf_op jit(solution)/shard_map/ppermute | solution.py:342
  48.8 12.7 %all-to-all-start = ((f32[32,1,128]{2,1,0:T(1,128)}), f32[32,1,128]{2,1,0:T(1,128)S(1)}, u32[]{:S(2)}, u32[]{:S(2)}) async-start(f32[32,1,128]{2,1,0:T(1,128)} %bitcast.9), calls=%async_computation | async-start | bytes 32768 | tf_op jit(solution)/shard_map/all_to_all | solution.py:370
  54.3 7.1 %copy-start = (s32[128,8]{0,1:T(8,128)S(1)}, s32[128,8]{0,1:T(8,128)}, u32[]{:S(2)}) copy-start(s32[128,8]{0,1:T(8,128)} %param.8) | copy-start | bytes 12292

commit v3 on v2

v3 whole, which is shorter than its diff:
```python
import jax
import jax.numpy as jnp
from jax import lax
from jax.experimental import pallas as pl
from jax.experimental.pallas import tpu as pltpu
from jax.sharding import PartitionSpec as P

MIB = 1024 * 1024
BF16 = jnp.bfloat16
F32 = jnp.float32
LANES = 128


def vmem_spec():
    return pl.BlockSpec(memory_space=pltpu.VMEM)


def smem_spec():
    return pl.BlockSpec(memory_space=pltpu.SMEM)


def any_spec():
    return pl.BlockSpec(memory_space=pl.ANY)


def params(mib):
    return pltpu.CompilerParams(vmem_limit_bytes=mib * MIB)


def cost(flops, moved):
    return pl.CostEstimate(flops=int(flops) // 1000, bytes_accessed=int(moved) // 1000, transcendentals=0)


def in_hbm(x):
    return pltpu.with_memory_space_constraint(x, pltpu.HBM)


def ring_of(experts):
    return list(range(0, experts, 2)) + list(range(experts - 1, 0, -2))


def source_of(me, step, experts):
    at = jnp.where(me % 2 == 0, me // 2, experts - 1 - me // 2)
    at = (at + step + experts) % experts
    return jnp.where(at < experts // 2, 2 * at, 2 * (experts - 1 - at) + 1)


def chunks_of(out_grad, gates_t, routes_t):
    tokens, feats = out_grad.shape
    experts = routes_t.shape[0]
    half = tokens // 2
    cols = feats // LANES

    def body(rows_ref, g_ref, r_ref, top_ref, bottom_ref, rows_scr, g_scr, r_scr, sems):
        copies = [
            pltpu.make_async_copy(src, dst, sems.at[i])
            for i, (src, dst) in enumerate(((g_ref, g_scr), (r_ref, r_scr), (rows_ref, rows_scr)))
        ]
        for copy in copies:
            copy.start()
        for copy in copies[:2]:
            copy.wait()
        routes = r_scr[...]
        gates = g_scr[...].astype(F32)
        by = [
            jnp.sum(jnp.where(routes == e, gates, 0.0), axis=0, keepdims=True) for e in range(experts)
        ]
        by = jnp.concatenate(by + [jnp.zeros((16 - experts, tokens), F32)], axis=0).astype(BF16)
        copies[2].wait()
        for c, ref in enumerate((top_ref, bottom_ref)):
            for j in range(cols):
                ref[j * half : (j + 1) * half, :] = rows_scr[
                    c * half : (c + 1) * half, j * LANES : (j + 1) * LANES
                ]
            ref[cols * half :, :] = by

    return pl.pallas_call(
        body,
        in_specs=[any_spec()] * 3,
        out_specs=[vmem_spec()] * 2,
        out_shape=[pltpu.VMEM((cols * half + 16, LANES), BF16)] * 2,
        scratch_shapes=[
            pltpu.VMEM(out_grad.shape, BF16),
            pltpu.VMEM(gates_t.shape, BF16),
            pltpu.VMEM(routes_t.shape, jnp.int32),
            pltpu.SemaphoreType.DMA((3,)),
        ],
        compiler_params=params(4),
        cost_estimate=cost(4 * tokens * feats, 4 * tokens * feats),
        name="chunks",
    )(*[in_hbm(x) for x in (out_grad, gates_t, routes_t)])


def hidden_of(gate_pre, up_pre, weight):
    slots, width = gate_pre.shape
    blocks = 4
    rows = slots // blocks

    def body(pre_ref, up_ref, w_ref, hidden_ref, held_ref, pre_scr, up_scr, sems):
        copies = []
        for i in range(blocks):
            here = pl.ds(i * rows, rows)
            copies.append(
                [
                    pltpu.make_async_copy(src.at[here], dst.at[here], sems.at[2 * i + j])
                    for j, (src, dst) in enumerate(((pre_ref, pre_scr), (up_ref, up_scr)))
                ]
            )
        fetch = pltpu.make_async_copy(w_ref, held_ref, sems.at[2 * blocks])
        for copy in sum(copies, []):
            copy.start()
        fetch.start()
        for i in range(blocks):
            for copy in copies[i]:
                copy.wait()
            here = pl.ds(i * rows, rows)
            pre = pre_scr[here, :].astype(F32)
            hidden_ref[here, :] = (pre / (1.0 + jnp.exp(-pre)) * up_scr[here, :].astype(F32)).astype(BF16)
        fetch.wait()

    return pl.pallas_call(
        body,
        in_specs=[any_spec()] * 3,
        out_specs=[vmem_spec()] * 2,
        out_shape=[pltpu.VMEM((slots, width), BF16), pltpu.VMEM(weight.shape, BF16)],
        scratch_shapes=[
            pltpu.VMEM((slots, width), BF16),
            pltpu.VMEM((slots, width), BF16),
            pltpu.SemaphoreType.DMA((2 * blocks + 1,)),
        ],
        compiler_params=params(4),
        cost_estimate=cost(8 * slots * width, 6 * slots * width),
        name="hidden",
    )(*[in_hbm(x) for x in (gate_pre, up_pre, weight)])


def assemble(info, parts, weight, scaled, tokens, steps):
    slots, width = parts[0].shape
    units, feats = weight.shape
    groups, experts = len(parts), slots // tokens
    cols = 256
    counts = [x.shape[0] for x in scaled]

    def body(info_ref, *refs):
        part_refs, refs = refs[:groups], refs[groups:]
        scaled_refs, refs = refs[: len(scaled)], refs[len(scaled) :]
        w_ref, ht_ref, eo_ref, out_ref, h_scr, sems = refs
        copies = [
            pltpu.make_async_copy(ref, out_ref.at[pl.ds(sum(counts[:i]), counts[i])], sems.at[i])
            for i, ref in enumerate(scaled_refs)
        ]
        for copy in copies:
            copy.start()
        for m, ref in enumerate(part_refs):
            at = pl.multiple_of((info_ref[0] ^ m) * width, width)
            for i, step in enumerate(steps):
                start = pl.multiple_of(source_of(info_ref[1], step, experts) * tokens, tokens)
                value = ref[pl.ds(start, tokens), :]
                here = slice(i * tokens, (i + 1) * tokens)
                h_scr[here, pl.ds(at, width)] = value
                ht_ref[pl.ds(at, width), here] = value.T
        for j in range(feats // cols):
            here = slice(j * cols, (j + 1) * cols)
            eo_ref[:, here] = jnp.dot(h_scr[...], w_ref[:, here], preferred_element_type=F32)
        for copy in copies:
            copy.wait()

    return pl.pallas_call(
        body,
        in_specs=[smem_spec()] + [vmem_spec()] * (groups + len(scaled) + 1),
        out_specs=[vmem_spec(), vmem_spec(), any_spec()],
        out_shape=[
            pltpu.VMEM((units, slots), BF16),
            pltpu.VMEM((slots, feats), F32),
            pltpu.HBM((sum(counts), feats), BF16),
        ],
        scratch_shapes=[pltpu.VMEM((slots, units), BF16), pltpu.SemaphoreType.DMA((len(scaled),))],
        compiler_params=params(6),
        cost_estimate=pl.CostEstimate(flops=0, bytes_accessed=1000, transcendentals=0),
        name="expert_out",
    )(info, *parts, *scaled, weight)


def column(row):
    return jnp.broadcast_to(row, (8, row.shape[1])).T[:, :1]


def gate_of(chunk_ref, me, half, lower):
    by = chunk_ref[chunk_ref.shape[0] - 16 :, :].astype(F32)
    row = lax.broadcasted_iota(jnp.int32, by.shape, 0)
    gate = jnp.sum(jnp.where(row == me, by, 0.0), axis=0, keepdims=True)
    return column(gate)[lower * half : (lower + 1) * half]


def add_up(chunk_ref, eo_ref, at, half):
    total = jnp.zeros((half, LANES), F32)
    for j in range(eo_ref.shape[1] // LANES):
        value = chunk_ref[j * half : (j + 1) * half, :].astype(F32)
        total = total + value * eo_ref[at : at + half, j * LANES : (j + 1) * LANES]
    return jnp.sum(total, axis=1, keepdims=True)


def put_scaled(chunk_ref, out_ref, at, gate, half):
    for j in range(out_ref.shape[1] // LANES):
        value = chunk_ref[j * half : (j + 1) * half, :].astype(F32)
        out_ref[at : at + half, j * LANES : (j + 1) * LANES] = (value * gate).astype(BF16)


def scaled_rows(info, chunks, lowers, half, declared):
    cols = (chunks[0].shape[0] - 16) // half
    count = len(chunks)

    def body(info_ref, *refs):
        out_ref = refs[count]
        for i, ref in enumerate(refs[:count]):
            put_scaled(ref, out_ref, i * half, gate_of(ref, info_ref[1], half, lowers[i]), half)

    return pl.pallas_call(
        body,
        in_specs=[smem_spec()] + [vmem_spec()] * count,
        out_specs=vmem_spec(),
        out_shape=pltpu.VMEM((count * half, cols * LANES), BF16),
        compiler_params=params(3),
        cost_estimate=pl.CostEstimate(flops=declared, bytes_accessed=1000, transcendentals=0),
        name="scaled_rows",
    )(info, *chunks)


def absorb(info, chunks, expert_out, tokens, steps, declared):
    half = tokens // 2
    experts = expert_out.shape[0] // tokens
    count = len(chunks) // 2

    def body(info_ref, *refs):
        chunk_refs, (eo_ref, sums_ref, last_ref, own_ref) = refs[: 2 * count], refs[2 * count :]
        me = info_ref[1]
        lanes = []
        for i in range(count):
            at = i * tokens
            sums = [add_up(chunk_refs[2 * i + c], eo_ref, at + c * half, half) for c in range(2)]
            lanes.append(jnp.concatenate(sums, axis=0))
        lanes += [jnp.zeros((tokens, 1), F32)] * (experts - count)
        by_step = jnp.concatenate(lanes, axis=1).T
        row = lax.broadcasted_iota(jnp.int32, (experts, tokens), 0)
        total = jnp.zeros((experts, tokens), F32)
        for i, step in enumerate(steps[:count]):
            total = jnp.where(row == source_of(me, step, experts), by_step[i : i + 1], total)
        sums_ref[...] = total
        last_ref[...] = (row == source_of(me, steps[-1], experts)).astype(F32)
        own_ref[...] = (lax.broadcasted_iota(jnp.int32, own_ref.shape, 0) == me).astype(F32)

    return pl.pallas_call(
        body,
        in_specs=[smem_spec()] + [vmem_spec()] * (2 * count + 1),
        out_specs=[vmem_spec()] * 3,
        out_shape=[
            pltpu.VMEM((experts, tokens), F32),
            pltpu.VMEM((experts, tokens), F32),
            pltpu.VMEM((16, LANES), F32),
        ],
        compiler_params=params(4),
        cost_estimate=pl.CostEstimate(flops=declared, bytes_accessed=1000, transcendentals=0),
        name="absorb",
    )(info, *chunks, expert_out)


def absorb_last(chunks, expert_out, sums, mask, groups):
    experts, tokens = sums.shape
    half = tokens // 2
    first = expert_out.shape[0] - tokens

    def body(top_ref, bottom_ref, eo_ref, sums_ref, mask_ref, out_ref):
        parts = [add_up(ref, eo_ref, first + c * half, half) for c, ref in enumerate((top_ref, bottom_ref))]
        own = jnp.broadcast_to(jnp.concatenate(parts, axis=0), (tokens, experts)).T
        value = jnp.where(mask_ref[...] > 0.0, own, sums_ref[...])
        out_ref[...] = jnp.broadcast_to(value[:, None, :], out_ref.shape)

    return pl.pallas_call(
        body,
        in_specs=[vmem_spec()] * 5,
        out_specs=vmem_spec(),
        out_shape=jax.ShapeDtypeStruct((experts, groups, tokens), F32),
        compiler_params=params(2),
        cost_estimate=cost(3 * tokens * expert_out.shape[1], 8 * tokens * expert_out.shape[1]),
        name="absorb_last",
    )(*chunks, expert_out, sums, mask)


def weight_grad(own, early, early_places, late, late_places, last_chunks, hidden_t):
    units, slots = hidden_t.shape
    feats = late[0].shape[1]
    half = late[0].shape[0] // len(late_places[0])
    blocks = 4
    rows = units // blocks

    def body(own_ref, early_ref, *refs):
        late_refs, refs = refs[: len(late)], refs[len(late) :]
        top_ref, bottom_ref, ht_ref, out_ref, rows_scr, held, in_sems, out_sems = refs
        copies = [
            pltpu.make_async_copy(
                early_ref.at[pl.ds(i * half, half)], rows_scr.at[pl.ds(place, half)], in_sems.at[i]
            )
            for i, place in enumerate(early_places)
        ]
        for copy in copies:
            copy.start()
        for ref, at in zip(late_refs, late_places):
            for i, place in enumerate(at):
                rows_scr[place : place + half, :] = ref[i * half : (i + 1) * half, :]
        for c, ref in enumerate((top_ref, bottom_ref)):
            by = ref[ref.shape[0] - 16 :, :].astype(F32)
            gate = column(jnp.sum(by * own_ref[...], axis=0, keepdims=True))[c * half : (c + 1) * half]
            put_scaled(ref, rows_scr, slots - (2 - c) * half, gate, half)
        for copy in copies:
            copy.wait()
        copies = []
        for i in range(blocks):
            here = pl.ds(i * rows, rows)
            held[here, :] = jnp.dot(ht_ref[here, :], rows_scr[...], preferred_element_type=F32).astype(BF16)
            copy = pltpu.make_async_copy(held.at[here], out_ref.at[here], out_sems.at[i])
            copy.start()
            copies.append(copy)
        for copy in copies:
            copy.wait()

    return pl.pallas_call(
        body,
        in_specs=[vmem_spec(), any_spec()] + [vmem_spec()] * (3 + len(late)),
        out_specs=any_spec(),
        out_shape=jax.ShapeDtypeStruct((units, feats), BF16),
        scratch_shapes=[
            pltpu.VMEM((slots, feats), BF16),
            pltpu.VMEM((units, feats), BF16),
            pltpu.SemaphoreType.DMA((len(early_places),)),
            pltpu.SemaphoreType.DMA((blocks,)),
        ],
        compiler_params=params(12),
        cost_estimate=cost(2 * slots * units * feats, 4 * units * feats),
        name="weight_grad",
    )(own, in_hbm(early), *late, *last_chunks, hidden_t)


def pick(returned, routes_t):
    topk, tokens = routes_t.shape
    experts, groups, _ = returned.shape

    def body(back_ref, routes_ref, out_ref):
        routes = routes_ref[...]
        total = jnp.zeros((topk, tokens), F32)
        for e in range(experts):
            value = jnp.sum(back_ref[e], axis=0, keepdims=True)
            total = jnp.where(routes == e, jnp.broadcast_to(value, total.shape), total)
        out_ref[...] = total

    return pl.pallas_call(
        body,
        in_specs=[vmem_spec(), vmem_spec()],
        out_specs=vmem_spec(),
        out_shape=jax.ShapeDtypeStruct((topk, tokens), F32),
        compiler_params=params(2),
        name="pick_gate_grad",
    )(returned, routes_t)


def dense(out_grad, gate_weights, routes, gate_pre, up_pre, down_weight):
    tokens, topk = routes.shape
    experts, groups = lax.axis_size("ep"), lax.axis_size("et")
    weight = down_weight[0]
    barrier = lax.optimization_barrier

    ring = ring_of(experts)
    forth = [(ring[i], ring[(i + 1) % experts]) for i in range(experts)]
    back = [(b, a) for a, b in forth]
    far = experts // 2
    steps = [0] + [s for k in range(1, far) for s in (-k, k)] + [far]
    info = jnp.stack([lax.axis_index("et").astype(jnp.int32), lax.axis_index("ep").astype(jnp.int32)])
    out_grad, info = barrier((out_grad, info))

    top, bottom = chunks_of(out_grad, gate_weights.T, routes.T)
    hidden, weight = hidden_of(gate_pre[0], up_pre[0], weight)
    chips, cores = [(i, i ^ 2) for i in range(groups)], [(i, i ^ 1) for i in range(groups)]
    half = tokens // 2

    def hop(c):
        up[c] = lax.ppermute(up[c], "ep", forth)
        down[c] = lax.ppermute(down[c], "ep", back)

    def scale(chunks, lowers, declared=0):
        return scaled_rows(info, chunks, lowers, half, declared)

    up, down = [top, bottom], [bottom, top]
    hop(0)
    hop(1)
    over = lax.ppermute(hidden, "et", chips)
    beside, across = lax.ppermute(hidden, "et", cores), lax.ppermute(over, "et", cores)
    first = [up[0], up[1], down[1], down[0]]
    hop(0)
    hop(1)
    second = [up[0], up[1], down[1], down[0]]
    scaled_a = scale([top, bottom] + first, [0, 1] * 3, 4000000000)
    up[0], down[0], scaled_a = barrier((up[0], down[0], scaled_a))
    hop(0)
    scaled_b = scale(second, [0, 1] * 2, 8000000000)
    up[1], down[1], scaled_b = barrier((up[1], down[1], scaled_b))
    hop(1)
    third = [up[0], up[1], down[1], down[0]]
    scaled_c = scale([up[0], down[0]], [0, 1], 12000000000)
    scaled_d = scale([up[1], down[1]], [1, 0])
    up[0], down[0], scaled_c, beside, across = barrier((up[0], down[0], scaled_c, beside, across))

    hop(0)
    hidden_t, expert_out, early = assemble(
        info, [hidden, beside, over, across], weight, [scaled_a, scaled_b], tokens, steps
    )
    third, scaled_d = barrier((third, scaled_d))
    sums, mask, own = absorb(
        info, [top, bottom] + first + second + third, expert_out, tokens, steps, 3000
    )
    outgoing = absorb_last([up[0], down[0]], expert_out, sums, mask, groups)
    returned = lax.all_to_all(
        outgoing.reshape(experts * groups, tokens), ("ep", "et"), split_axis=0, concat_axis=0, tiled=True
    )
    late_places = [[10 * half, 13 * half], [11 * half, 12 * half]]
    grad = weight_grad(
        own, early, [i * half for i in range(10)], [scaled_c, scaled_d], late_places, [up[0], down[0]], hidden_t
    )
    d_gate = pick(returned.reshape(experts, groups, tokens), routes.T).T
    return grad[None], d_gate


def routed(out_grad, gate_weights, routes, gate_pre, up_pre, down_weight):
    tok_rows, topk = routes.shape
    experts = lax.axis_size("ep")
    slot_total = gate_pre.shape[1]
    capacity = slot_total // experts
    flat_route = routes.reshape(-1)
    pair_count = tok_rows * topk
    onehot = (flat_route[:, None] == jnp.arange(experts, dtype=jnp.int32)[None, :]).astype(
        jnp.int32
    )
    ranks = jnp.sum(jnp.cumsum(onehot, axis=0) * onehot, axis=1) - 1
    slot_of = flat_route * capacity + ranks
    pair_ids = jnp.arange(pair_count, dtype=jnp.int32)
    slot_pair = jnp.zeros((experts * capacity,), jnp.int32).at[slot_of].set(pair_ids)
    filled = jnp.zeros((experts * capacity,), jnp.bool_).at[slot_of].set(True)
    send_rows = jnp.where(filled[:, None], out_grad[slot_pair // topk], 0.0)
    send_rows = send_rows.reshape(experts, capacity, out_grad.shape[1])
    send_gates = jnp.where(filled, gate_weights.reshape(-1)[slot_pair], 0.0)
    send_gates = send_gates.reshape(experts, capacity)
    rows_in, gates_in = (
        lax.all_to_all(send_rows, "ep", split_axis=0, concat_axis=0, tiled=True),
        lax.all_to_all(send_gates, "ep", split_axis=0, concat_axis=0, tiled=True),
    )
    rows_in = rows_in.reshape(slot_total, out_grad.shape[1])
    gates_in = gates_in.reshape(slot_total)
    weight = down_weight[0]
    hidden_part = (
        jax.nn.silu(gate_pre[0].astype(jnp.float32)) * up_pre[0].astype(jnp.float32)
    ).astype(jnp.bfloat16)
    scaled = (gates_in.astype(jnp.float32)[:, None] * rows_in.astype(jnp.float32)).astype(
        jnp.bfloat16
    )
    piece = lax.all_gather(hidden_part, "et", axis=1, tiled=True)
    expert_out = jnp.dot(piece, weight, preferred_element_type=jnp.float32)
    grad_weight = lax.dot_general(
        piece, scaled, (((0,), (0,)), ((), ())), preferred_element_type=jnp.float32
    )
    partial_grad = jnp.sum(rows_in.astype(jnp.float32) * expert_out, axis=1)
    slot_grad = lax.psum(partial_grad, "et")
    returned = lax.all_to_all(
        slot_grad.reshape(experts, capacity), "ep", split_axis=0, concat_axis=0, tiled=True
    )
    d_gate = returned.reshape(-1)[slot_of].reshape(tok_rows, topk)
    return (grad_weight.astype(jnp.bfloat16)[None], d_gate)


def solution(mesh):
    sizes = dict(mesh.shape)

    def local(out_grad, gate_weights, routes, gate_pre, up_pre, down_weight):
        tokens, topk = routes.shape
        whole = topk == sizes["ep"] and gate_pre.shape[1] == topk * tokens
        if whole and sizes["ep"] == 8 and sizes["et"] == 4:
            return dense(out_grad, gate_weights, routes, gate_pre, up_pre, down_weight)
        return routed(out_grad, gate_weights, routes, gate_pre, up_pre, down_weight)

    in_specs = (
        P("ep", "et"),
        P("ep", None),
        P("ep", None),
        P("ep", None, "et"),
        P("ep", None, "et"),
        P("ep", None, "et"),
    )
    out_specs = (P("ep", None, "et"), P("ep", None))
    return jax.shard_map(local, mesh=mesh, in_specs=in_specs, out_specs=out_specs, check_vma=False)
```

time: 62.3 us -> 60.1 us (0.965)
  waiting for transfers between devices: 15.2 us -> 13.6 us
    ppermute x7, starting transfers between devices: 4.5 us -> 0.55 us  [hop(): down[c] = lax.ppermute(down[c], 'ep', back)]
    ppermute x7, starting transfers between devices: 10.8 us -> 14.6 us  [hop(): up[c] = lax.ppermute(up[c], 'ep', forth)]
    pallas_call x5 -> x9, Pallas kernels: 16.9 us -> 20.1 us  [the longest x1 6.71 us: weight_grad(): pl.pallas_call(body, in_specs=[vmem_spec(), any_spec()] + [vmem_spec()] *...]
    pallas_call x2 -> x1, Pallas kernels: 4.68 us -> 1.48 us  [absorb(): pl.pallas_call(body, in_specs=[smem_spec()] + [vmem_spec()] * (2 * count...]
    ppermute x7, waiting for transfers between devices: 10.2 us -> 7.2 us  [hop(): up[c] = lax.ppermute(up[c], 'ep', forth)]
    ppermute x1, starting transfers between devices: 3.03 us -> 2.03 us  [dense(): over = lax.ppermute(hidden, 'et', chips)]
    ppermute x7, waiting for transfers between devices: 4.66 us -> 5.47 us  [hop(): down[c] = lax.ppermute(down[c], 'ep', back)]
  transfers between devices with their start and end apart: 18 -> 18, of which waited for: 7 -> 9; matrix products, arithmetic and copies ran while one was open for 0% -> 0% of each run, Pallas kernels for 30% -> 33%
where the time goes in v3:
time: 60.1 us; the launch traced here: 59.9 us
  starting transfers between devices  23.3 us (39%)
  Pallas kernels  22.2 us (37%)
  waiting for transfers between devices  13.6 us (23%)
  between operations  0.76 us (1%)
    ppermute x7, starting transfers between devices, hop(): up[c] = lax.ppermute(up[c], 'ep', forth)  14.6 us
    ppermute x7, waiting for transfers between devices, hop(): up[c] = lax.ppermute(up[c], 'ep', forth)  7.2 us
    pallas_call x1, Pallas kernels, weight_grad(): pl.pallas_call(body, in_specs=[vmem_spec(), any_spec()] + [vmem_spec()] *...  6.71 us
    all_to_all x1, starting transfers between devices, dense(): lax.all_to_all(outgoing.reshape(experts * groups, tokens), ('ep', 'et'),...  6.09 us
    ppermute x7, waiting for transfers between devices, hop(): down[c] = lax.ppermute(down[c], 'ep', back)  5.47 us
    pallas_call x1, Pallas kernels, assemble(): pl.pallas_call(body, in_specs=[smem_spec()] + [vmem_spec()] * (groups + l...  5.31 us
    pallas_call x4, Pallas kernels, scaled_rows(): pl.pallas_call(body, in_specs=[smem_spec()] + [vmem_spec()] * count, out_...  3.44 us
    pallas_call x1, Pallas kernels, hidden_of(): pl.pallas_call(body, in_specs=[any_spec()] * 3, out_specs=[vmem_spec()] *...  2.55 us
  transfers between devices with their start and end apart: 18, of which 9 were waited for; matrix products, arithmetic and copies ran while one was open for 0% of the time, Pallas kernels for 33%

profile of v3, /device:TPU:0, one launch (start us, length us, event | category | flops | bytes accessed | tf_op | source)
XLA Modules:
  0.0 59.9 jit_solution(1417148356857458139)
XLA Ops:
  0.6 0.1 pad_add_fusion.info_ref
  0.7 1.2 %chunks.1 = (bf16[912,128]{1,0:T(8,128)(2,1)S(1)}, bf16[912,128]{1,0:T(8,128)(2,1)S(1)}) custom-call(bf16[128,1792]{1,0:T(8,128)(2,1)} %rows_ref, bf16[8,128]{1,0:T(8,128)(2,1)} %bitcast.21, s32[8,128]{1,0:T(8,128)} %bitcast.14), custom_call_target="tpu_custom_call" | custom-call | flops 917 | bytes 917 | tf_op jit(solution)/shard_map/chunks/pallas_call | solution.py:77
  1.9 3.1 %collective-permute-start = (bf16[912,128]{1,0:T(8,128)(2,1)S(1)}, bf16[912,128]{1,0:T(8,128)(2,1)S(1)}, u32[]{:S(2)}, u32[]{:S(2)}) collective-permute-start(bf16[912,128]{1,0:T(8,128)(2,1)S(1)} %get-tuple-element.32.refs_0_), channel_id=1, source_target_pairs={{0,8},{8,16},{16,24},{24,28},{28,20},{20,12},{12,4},{4,0},{1,9},{9... | collective-permute-start | bytes 700424 | tf_op jit(solution)/shard_map/ppermute | solution.py:385
  4.9 0.0 collective-permute-start.3
  5.0 2.0 %collective-permute-start.1 = (bf16[912,128]{1,0:T(8,128)(2,1)S(1)}, bf16[912,128]{1,0:T(8,128)(2,1)S(1)}, u32[]{:S(2)}, u32[]{:S(2)}) collective-permute-start(bf16[912,128]{1,0:T(8,128)(2,1)S(1)} %get-tuple-element.33.refs_1_), channel_id=1, source_target_pairs={{0,8},{8,16},{16,24},{24,28},{28,20},{20,12},{12,4},{4,0},{1,9},{9... | collective-permute-start | bytes 700424 | tf_op jit(solution)/shard_map/ppermute | solution.py:385
  7.0 0.0 collective-permute-start.2
  7.0 2.5 %hidden.1 = (bf16[1024,256]{1,0:T(8,128)(2,1)S(1)}, bf16[1024,1792]{1,0:T(8,128)(2,1)S(1)}) custom-call(bf16[1024,256]{1,0:T(8,128)(2,1)} %bitcast.18, bf16[1024,256]{1,0:T(8,128)(2,1)} %bitcast.19, bf16[1024,1792]{1,0:T(8,128)(2,1)} %bitcast.17), custom_call_target="tpu_custom_call" | custom-call | flops 2097 | bytes 1572 | tf_op jit(solution)/shard_map/hidden/pallas_call | solution.py:121
  9.5 2.0 %collective-permute-start.13 = (bf16[1024,256]{1,0:T(8,128)(2,1)S(1)}, bf16[1024,256]{1,0:T(8,128)(2,1)S(1)}, u32[]{:S(2)}, u32[]{:S(2)}) collective-permute-start(bf16[1024,256]{1,0:T(8,128)(2,1)S(1)} %get-tuple-element.42.refs_0_), channel_id=1, source_target_pairs={{0,2},{1,3},{2,0},{3,1},{4,6},{5,7},{6,4},{7,5},{8,10},{9,11},{10,... | collective-permute-start | bytes 1572872 | tf_op jit(solution)/shard_map/ppermute | solution.py:394
  11.6 0.0 collective-permute-done.refs_2_
  11.6 2.0 %collective-permute-start.4 = (bf16[912,128]{1,0:T(8,128)(2,1)S(1)}, bf16[912,128]{1,0:T(8,128)(2,1)S(1)}, u32[]{:S(2)}, u32[]{:S(2)}) collective-permute-start(bf16[912,128]{1,0:T(8,128)(2,1)S(1)} %collective-permute-done.refs_2_), channel_id=1, source_target_pairs={{0,8},{8,16},{16,24},{24,28},{28,20},{20,12},{12,4},{4,0},{1,9},{9... | collective-permute-start | bytes 700424 | tf_op jit(solution)/shard_map/ppermute | solution.py:385
  13.5 0.0 collective-permute-done.3.refs_5_
  13.6 0.0 collective-permute-start.7
  13.6 2.8 %collective-permute-done.1.refs_3_ = bf16[912,128]{1,0:T(8,128)(2,1)S(1)} collective-permute-done((bf16[912,128]{1,0:T(8,128)(2,1)S(1)}, bf16[912,128]{1,0:T(8,128)(2,1)S(1)}, u32[]{:S(2)}, u32[]{:S(2)}) %collective-permute-start.1) | collective-permute-done | bytes 233504 | tf_op jit(solution)/shard_map/ppermute | solution.py:385
  16.4 2.1 %collective-permute-start.5 = (bf16[912,128]{1,0:T(8,128)(2,1)S(1)}, bf16[912,128]{1,0:T(8,128)(2,1)S(1)}, u32[]{:S(2)}, u32[]{:S(2)}) collective-permute-start(bf16[912,128]{1,0:T(8,128)(2,1)S(1)} %collective-permute-done.1.refs_3_), channel_id=1, source_target_pairs={{0,8},{8,16},{16,24},{24,28},{28,20},{20,12},{12,4},{4,0},{1,9},{9... | collective-permute-start | bytes 700424 | tf_op jit(solution)/shard_map/ppermute | solution.py:385
  18.5 0.0 collective-permute-done.2.refs_4_
  18.6 0.0 collective-permute-start.6
  18.6 1.0 %scaled_rows.4.refs_4_ = bf16[384,1792]{1,0:T(8,128)(2,1)S(1)} custom-call(s32[2]{0:T(128)S(1)} %pad_add_fusion.info_ref, bf16[912,128]{1,0:T(8,128)(2,1)S(1)} %get-tuple-element.32.refs_0_, bf16[912,128]{1,0:T(8,128)(2,1)S(1)} %get-tuple-element.33.refs_1_, bf16[912,128]{1,0:T(8,128)(2,1)S(1)} %collective-permute-done.refs_2_, ...), custom_call_target="tpu_custom_call" | custom-call | flops 4000000000 | bytes 1000 | tf_op jit(solution)/shard_map/scaled_rows/pallas_call | solution.py:218
  19.6 1.8 %collective-permute-done.4.refs_0_.refs_6_ = bf16[912,128]{1,0:T(8,128)(2,1)S(1)} collective-permute-done((bf16[912,128]{1,0:T(8,128)(2,1)S(1)}, bf16[912,128]{1,0:T(8,128)(2,1)S(1)}, u32[]{:S(2)}, u32[]{:S(2)}) %collective-permute-start.4) | collective-permute-done | bytes 233504 | tf_op jit(solution)/shard_map/ppermute | solution.py:385
  21.4 0.0 collective-permute-start.12
  21.4 2.2 %collective-permute-done.7.refs_3_.refs_9_ = bf16[912,128]{1,0:T(8,128)(2,1)S(1)} collective-permute-done((bf16[912,128]{1,0:T(8,128)(2,1)S(1)}, bf16[912,128]{1,0:T(8,128)(2,1)S(1)}, u32[]{:S(2)}, u32[]{:S(2)}) %collective-permute-start.7) | collective-permute-done | bytes 233504 | tf_op jit(solution)/shard_map/ppermute | solution.py:386
  23.6 0.0 collective-permute-start.11
  23.6 2.0 %collective-permute-done.5.refs_1_.refs_7_ = bf16[912,128]{1,0:T(8,128)(2,1)S(1)} collective-permute-done((bf16[912,128]{1,0:T(8,128)(2,1)S(1)}, bf16[912,128]{1,0:T(8,128)(2,1)S(1)}, u32[]{:S(2)}, u32[]{:S(2)}) %collective-permute-start.5) | collective-permute-done | bytes 233504 | tf_op jit(solution)/shard_map/ppermute | solution.py:385
  25.6 1.8 %collective-permute-start.8 = (bf16[912,128]{1,0:T(8,128)(2,1)S(1)}, bf16[912,128]{1,0:T(8,128)(2,1)S(1)}, u32[]{:S(2)}, u32[]{:S(2)}) collective-permute-start(bf16[912,128]{1,0:T(8,128)(2,1)S(1)} %collective-permute-done.4.refs_0_.refs_6_), channel_id=1, source_target_pairs={{0,8},{8,16},{16,24},{24,28},{28,20},{20,12},{12,4},{4,0},{1,9},{9... | collective-permute-start | bytes 700424 | tf_op jit(solution)/shard_map/ppermute | solution.py:385
  27.4 1.2 %collective-permute-done.6.refs_2_.refs_8_ = bf16[912,128]{1,0:T(8,128)(2,1)S(1)} collective-permute-done((bf16[912,128]{1,0:T(8,128)(2,1)S(1)}, bf16[912,128]{1,0:T(8,128)(2,1)S(1)}, u32[]{:S(2)}, u32[]{:S(2)}) %collective-permute-start.6) | collective-permute-done | bytes 233504 | tf_op jit(solution)/shard_map/ppermute | solution.py:386
  28.6 0.9 %scaled_rows.5.refs_5_ = bf16[256,1792]{1,0:T(8,128)(2,1)S(1)} custom-call(s32[2]{0:T(128)S(1)} %pad_add_fusion.info_ref, bf16[912,128]{1,0:T(8,128)(2,1)S(1)} %collective-permute-done.4.refs_0_.refs_6_, bf16[912,128]{1,0:T(8,128)(2,1)S(1)} %collective-permute-done.5.refs_1_.refs_7_, bf16[912,128]{1,0:T(8,128)(2,1)S(1)} %collective-permute-done.6.refs_2_.refs_8_, ...), custom_call_target="tpu_custom_call" | custom-call | flops 8000000000 | bytes 1000 | tf_op jit(solution)/shard_map/scaled_rows/pallas_call | solution.py:218
  29.5 0.1 collective-permute-start.10
  29.5 0.0 collective-permute-done.13.refs_2_
  29.5 2.0 %collective-permute-start.9 = (bf16[912,128]{1,0:T(8,128)(2,1)S(1)}, bf16[912,128]{1,0:T(8,128)(2,1)S(1)}, u32[]{:S(2)}, u32[]{:S(2)}) collective-permute-start(bf16[912,128]{1,0:T(8,128)(2,1)S(1)} %collective-permute-done.5.refs_1_.refs_7_), channel_id=1, source_target_pairs={{0,8},{8,16},{16,24},{24,28},{28,20},{20,12},{12,4},{4,0},{1,9},{9... | collective-permute-start | bytes 700424 | tf_op jit(solution)/shard_map/ppermute | solution.py:385
  31.5 2.0 %collective-permute-done.11.refs_1_.refs_13_ = bf16[912,128]{1,0:T(8,128)(2,1)S(1)} collective-permute-done((bf16[912,128]{1,0:T(8,128)(2,1)S(1)}, bf16[912,128]{1,0:T(8,128)(2,1)S(1)}, u32[]{:S(2)}, u32[]{:S(2)}) %collective-permute-start.11) | collective-permute-done | bytes 233504 | tf_op jit(solution)/shard_map/ppermute | solution.py:386
  33.6 0.0 collective-permute-start.14
  33.6 0.6 %collective-permute-done.8.refs_0_.refs_10_ = bf16[912,128]{1,0:T(8,128)(2,1)S(1)} collective-permute-done((bf16[912,128]{1,0:T(8,128)(2,1)S(1)}, bf16[912,128]{1,0:T(8,128)(2,1)S(1)}, u32[]{:S(2)}, u32[]{:S(2)}) %collective-permute-start.8) | collective-permute-done | bytes 233504 | tf_op jit(solution)/shard_map/ppermute | solution.py:385
  34.2 0.8 %scaled_rows.7.refs_0_ = bf16[128,1792]{1,0:T(8,128)(2,1)S(1)} custom-call(s32[2]{0:T(128)S(1)} %pad_add_fusion.info_ref, bf16[912,128]{1,0:T(8,128)(2,1)S(1)} %collective-permute-done.8.refs_0_.refs_10_, bf16[912,128]{1,0:T(8,128)(2,1)S(1)} %collective-permute-done.11.refs_1_.refs_13_), custom_call_target="tpu_custom_call" | custom-call | flops 12000000000 | bytes 1000 | tf_op jit(solution)/shard_map/scaled_rows/pallas_call | solution.py:218
  35.0 0.0 collective-permute-done.12.refs_1_
  35.0 0.5 collective-permute-done.14.refs_3_
  35.5 1.6 %collective-permute-start.15 = (bf16[912,128]{1,0:T(8,128)(2,1)S(1)}, bf16[912,128]{1,0:T(8,128)(2,1)S(1)}, u32[]{:S(2)}, u32[]{:S(2)}) collective-permute-start(bf16[912,128]{1,0:T(8,128)(2,1)S(1)} %collective-permute-done.8.refs_0_.refs_10_), channel_id=1, source_target_pairs={{0,8},{8,16},{16,24},{24,28},{28,20},{20,12},{12,4},{4,0},{1,9},{9... | collective-permute-start | bytes 700424 | tf_op jit(solution)/shard_map/ppermute | solution.py:385
  37.1 0.4 collective-permute-start.16
  37.5 0.0 collective-permute-done.10.refs_1_.refs_12_
  37.5 0.0 collective-permute-done.9.refs_0_.refs_11_
  37.5 0.8 %scaled_rows.6.refs_1_ = bf16[128,1792]{1,0:T(8,128)(2,1)S(1)} custom-call(s32[2]{0:T(128)S(1)} %pad_add_fusion.info_ref, bf16[912,128]{1,0:T(8,128)(2,1)S(1)} %collective-permute-done.9.refs_0_.refs_11_, bf16[912,128]{1,0:T(8,128)(2,1)S(1)} %collective-permute-done.10.refs_1_.refs_12_), custom_call_target="tpu_custom_call" | custom-call | bytes 1000 | tf_op jit(solution)/shard_map/scaled_rows/pallas_call | solution.py:218
  38.3 5.3 %expert_out.1 = (bf16[1024,1024]{1,0:T(8,128)(2,1)S(1)}, f32[1024,1792]{1,0:T(8,128)S(1)}, bf16[640,1792]{1,0:T(8,128)(2,1)}) custom-call(s32[2]{0:T(128)S(1)} %pad_add_fusion.info_ref, bf16[1024,256]{1,0:T(8,128)(2,1)S(1)} %get-tuple-element.42.refs_0_, bf16[1024,256]{1,0:T(8,128)(2,1)S(1)} %collective-permute-done.12.refs_1_, ...), custom_call_target="tpu_custom_call" | custom-call | bytes 1000 | tf_op jit(solution)/shard_map/expert_out/pallas_call | solution.py:168
  43.6 1.5 %absorb.1 = (f32[8,128]{1,0:T(8,128)S(1)}, f32[8,128]{1,0:T(8,128)S(1)}, f32[16,128]{1,0:T(8,128)S(1)}) custom-call(s32[2]{0:T(128)S(1)} %pad_add_fusion.info_ref, bf16[912,128]{1,0:T(8,128)(2,1)S(1)} %get-tuple-element.32.refs_0_, bf16[912,128]{1,0:T(8,128)(2,1)S(1)} %get-tuple-element.33.refs_1_, bf16[912,128]{1,0:T(8,128)(2,1)S(1)} %collective-permute-done.refs_2_, ...), custom_call_target="tpu_custom_call" | custom-call | flops 3000 | bytes 1000 | tf_op jit(solution)/shard_map/absorb/pallas_call | solution.py:252
  45.1 0.0 collective-permute-done.15.refs_2_.top_ref
  45.1 0.0 collective-permute-done.16.refs_3_.bottom_ref
  45.1 0.9 %absorb_last.1 = f32[8,4,128]{2,1,0:T(4,128)} custom-call(bf16[912,128]{1,0:T(8,128)(2,1)S(1)} %collective-permute-done.15.refs_2_.top_ref, bf16[912,128]{1,0:T(8,128)(2,1)S(1)} %collective-permute-done.16.refs_3_.bottom_ref, f32[1024,1792]{1,0:T(8,128)S(1)} %get-tuple-element.48.refs_14_.eo_ref, f32[8,128]{1,0:T(8,128)S(1)} %get-tuple-element.56.sums_ref, ...), custom_call_target="tpu_custom_call" | custom-call | flops 688 | bytes 1835 | tf_op jit(solution)/shard_map/absorb_last/pallas_call | solution.py:278
  46.0 6.1 %all-to-all-start = ((f32[32,1,128]{2,1,0:T(1,128)}), f32[32,1,128]{2,1,0:T(1,128)S(1)}, u32[]{:S(2)}, u32[]{:S(2)}) async-start(f32[32,1,128]{2,1,0:T(1,128)} %bitcast.9), calls=%async_computation | async-start | bytes 32768 | tf_op jit(solution)/shard_map/all_to_all | solution.py:420
  52.1 0.0 copy-start
  52.2 6.7 %weight_grad.1 = bf16[1024,1792]{1,0:T(8,128)(2,1)} custom-call(f32[16,128]{1,0:T(8,128)S(1)} %get-tuple-element.49.own_ref, bf16[640,1792]{1,0:T(8,128)(2,1)} %get-tuple-element.50.early_ref, bf16[128,1792]{1,0:T(8,128)(2,1)S(1)} %scaled_rows.7.refs_0_, bf16[128,1792]{1,0:T(8,128)(2,1)S(1)} %scaled_rows.6.refs_1_, ...), custom_call_target="tpu_custom_call" | custom-call | flops 3758096 | bytes 7340 | tf_op jit(solution)/shard_map/weight_grad/pallas_call | solution.py:326
  58.9 0.4 all-to-all-done
  59.3 0.0 copy-done
  59.3 0.6 %pick_gate_grad.1 = f32[8,128]{1,0:T(8,128)} custom-call(f32[8,4,128]{2,1,0:T(4,128)S(1)} %bitcast.13, s32[8,128]{1,0:T(8,128)S(1)} %bitcast.15), custom_call_target="tpu_custom_call" | custom-call | tf_op jit(solution)/shard_map/pick_gate_grad/pallas_call | solution.py:355
Async XLA Ops:
  1.9 9.7 %collective-permute-start = (bf16[912,128]{1,0:T(8,128)(2,1)S(1)}, bf16[912,128]{1,0:T(8,128)(2,1)S(1)}, u32[]{:S(2)}, u32[]{:S(2)}) collective-permute-start(bf16[912,128]{1,0:T(8,128)(2,1)S(1)} %get-tuple-element.32.refs_0_), channel_id=1, source_target_pairs={{0,8},{8,16},{16,24},{24,28},{28,20},{20,12},{12,4},{4,0},{1,9},{9... | collective-permute-start | bytes 700424 | tf_op jit(solution)/shard_map/ppermute | solution.py:385
  4.9 8.6 %collective-permute-start.3 = (bf16[912,128]{1,0:T(8,128)(2,1)S(1)}, bf16[912,128]{1,0:T(8,128)(2,1)S(1)}, u32[]{:S(2)}, u32[]{:S(2)}) collective-permute-start(bf16[912,128]{1,0:T(8,128)(2,1)S(1)} %get-tuple-element.33.refs_1_), channel_id=1, source_target_pairs={{8,0},{16,8},{24,16},{28,24},{20,28},{12,20},{4,12},{0,4},{9,1},{1... | collective-permute-start | bytes 700424 | tf_op jit(solution)/shard_map/ppermute | solution.py:386
  5.0 11.4 %collective-permute-start.1 = (bf16[912,128]{1,0:T(8,128)(2,1)S(1)}, bf16[912,128]{1,0:T(8,128)(2,1)S(1)}, u32[]{:S(2)}, u32[]{:S(2)}) collective-permute-start(bf16[912,128]{1,0:T(8,128)(2,1)S(1)} %get-tuple-element.33.refs_1_), channel_id=1, source_target_pairs={{0,8},{8,16},{16,24},{24,28},{28,20},{20,12},{12,4},{4,0},{1,9},{9... | collective-permute-start | bytes 700424 | tf_op jit(solution)/shard_map/ppermute | solution.py:385
  7.0 11.6 %collective-permute-start.2 = (bf16[912,128]{1,0:T(8,128)(2,1)S(1)}, bf16[912,128]{1,0:T(8,128)(2,1)S(1)}, u32[]{:S(2)}, u32[]{:S(2)}) collective-permute-start(bf16[912,128]{1,0:T(8,128)(2,1)S(1)} %get-tuple-element.32.refs_0_), channel_id=1, source_target_pairs={{8,0},{16,8},{24,16},{28,24},{20,28},{12,20},{4,12},{0,4},{9,1},{1... | collective-permute-start | bytes 700424 | tf_op jit(solution)/shard_map/ppermute | solution.py:386
  9.5 20.0 %collective-permute-start.13 = (bf16[1024,256]{1,0:T(8,128)(2,1)S(1)}, bf16[1024,256]{1,0:T(8,128)(2,1)S(1)}, u32[]{:S(2)}, u32[]{:S(2)}) collective-permute-start(bf16[1024,256]{1,0:T(8,128)(2,1)S(1)} %get-tuple-element.42.refs_0_), channel_id=1, source_target_pairs={{0,2},{1,3},{2,0},{3,1},{4,6},{5,7},{6,4},{7,5},{8,10},{9,11},{10,... | collective-permute-start | bytes 1572872 | tf_op jit(solution)/shard_map/ppermute | solution.py:394
  11.6 9.8 %collective-permute-start.4 = (bf16[912,128]{1,0:T(8,128)(2,1)S(1)}, bf16[912,128]{1,0:T(8,128)(2,1)S(1)}, u32[]{:S(2)}, u32[]{:S(2)}) collective-permute-start(bf16[912,128]{1,0:T(8,128)(2,1)S(1)} %collective-permute-done.refs_2_), channel_id=1, source_target_pairs={{0,8},{8,16},{16,24},{24,28},{28,20},{20,12},{12,4},{4,0},{1,9},{9... | collective-permute-start | bytes 700424 | tf_op jit(solution)/shard_map/ppermute | solution.py:385
  13.6 10.0 %collective-permute-start.7 = (bf16[912,128]{1,0:T(8,128)(2,1)S(1)}, bf16[912,128]{1,0:T(8,128)(2,1)S(1)}, u32[]{:S(2)}, u32[]{:S(2)}) collective-permute-start(bf16[912,128]{1,0:T(8,128)(2,1)S(1)} %collective-permute-done.3.refs_5_), channel_id=1, source_target_pairs={{8,0},{16,8},{24,16},{28,24},{20,28},{12,20},{4,12},{0,4},{9,1},{1... | collective-permute-start | bytes 700424 | tf_op jit(solution)/shard_map/ppermute | solution.py:386
  16.4 9.2 %collective-permute-start.5 = (bf16[912,128]{1,0:T(8,128)(2,1)S(1)}, bf16[912,128]{1,0:T(8,128)(2,1)S(1)}, u32[]{:S(2)}, u32[]{:S(2)}) collective-permute-start(bf16[912,128]{1,0:T(8,128)(2,1)S(1)} %collective-permute-done.1.refs_3_), channel_id=1, source_target_pairs={{0,8},{8,16},{16,24},{24,28},{28,20},{20,12},{12,4},{4,0},{1,9},{9... | collective-permute-start | bytes 700424 | tf_op jit(solution)/shard_map/ppermute | solution.py:385
  18.6 10.0 %collective-permute-start.6 = (bf16[912,128]{1,0:T(8,128)(2,1)S(1)}, bf16[912,128]{1,0:T(8,128)(2,1)S(1)}, u32[]{:S(2)}, u32[]{:S(2)}) collective-permute-start(bf16[912,128]{1,0:T(8,128)(2,1)S(1)} %collective-permute-done.2.refs_4_), channel_id=1, source_target_pairs={{8,0},{16,8},{24,16},{28,24},{20,28},{12,20},{4,12},{0,4},{9,1},{1... | collective-permute-start | bytes 700424 | tf_op jit(solution)/shard_map/ppermute | solution.py:386
  21.4 13.6 %collective-permute-start.12 = (bf16[1024,256]{1,0:T(8,128)(2,1)S(1)}, bf16[1024,256]{1,0:T(8,128)(2,1)S(1)}, u32[]{:S(2)}, u32[]{:S(2)}) collective-permute-start(bf16[1024,256]{1,0:T(8,128)(2,1)S(1)} %get-tuple-element.42.refs_0_), channel_id=1, source_target_pairs={{0,1},{1,0},{2,3},{3,2},{4,5},{5,4},{6,7},{7,6},{8,9},{9,8},{10,11... | collective-permute-start | bytes 1572872 | tf_op jit(solution)/shard_map/ppermute | solution.py:395
  23.6 10.0 %collective-permute-start.11 = (bf16[912,128]{1,0:T(8,128)(2,1)S(1)}, bf16[912,128]{1,0:T(8,128)(2,1)S(1)}, u32[]{:S(2)}, u32[]{:S(2)}) collective-permute-start(bf16[912,128]{1,0:T(8,128)(2,1)S(1)} %collective-permute-done.7.refs_3_.refs_9_), channel_id=1, source_target_pairs={{8,0},{16,8},{24,16},{28,24},{20,28},{12,20},{4,12},{0,4},{9,1},{1... | collective-permute-start | bytes 700424 | tf_op jit(solution)/shard_map/ppermute | solution.py:386
  25.6 8.6 %collective-permute-start.8 = (bf16[912,128]{1,0:T(8,128)(2,1)S(1)}, bf16[912,128]{1,0:T(8,128)(2,1)S(1)}, u32[]{:S(2)}, u32[]{:S(2)}) collective-permute-start(bf16[912,128]{1,0:T(8,128)(2,1)S(1)} %collective-permute-done.4.refs_0_.refs_6_), channel_id=1, source_target_pairs={{0,8},{8,16},{16,24},{24,28},{28,20},{20,12},{12,4},{4,0},{1,9},{9... | collective-permute-start | bytes 700424 | tf_op jit(solution)/shard_map/ppermute | solution.py:385
  29.5 8.1 %collective-permute-start.10 = (bf16[912,128]{1,0:T(8,128)(2,1)S(1)}, bf16[912,128]{1,0:T(8,128)(2,1)S(1)}, u32[]{:S(2)}, u32[]{:S(2)}) collective-permute-start(bf16[912,128]{1,0:T(8,128)(2,1)S(1)} %collective-permute-done.6.refs_2_.refs_8_), channel_id=1, source_target_pairs={{8,0},{16,8},{24,16},{28,24},{20,28},{12,20},{4,12},{0,4},{9,1},{1... | collective-permute-start | bytes 700424 | tf_op jit(solution)/shard_map/ppermute | solution.py:386
  29.5 8.0 %collective-permute-start.9 = (bf16[912,128]{1,0:T(8,128)(2,1)S(1)}, bf16[912,128]{1,0:T(8,128)(2,1)S(1)}, u32[]{:S(2)}, u32[]{:S(2)}) collective-permute-start(bf16[912,128]{1,0:T(8,128)(2,1)S(1)} %collective-permute-done.5.refs_1_.refs_7_), channel_id=1, source_target_pairs={{0,8},{8,16},{16,24},{24,28},{28,20},{20,12},{12,4},{4,0},{1,9},{9... | collective-permute-start | bytes 700424 | tf_op jit(solution)/shard_map/ppermute | solution.py:385
  33.6 1.9 %collective-permute-start.14 = (bf16[1024,256]{1,0:T(8,128)(2,1)S(1)}, bf16[1024,256]{1,0:T(8,128)(2,1)S(1)}, u32[]{:S(2)}, u32[]{:S(2)}) collective-permute-start(bf16[1024,256]{1,0:T(8,128)(2,1)S(1)} %collective-permute-done.13.refs_2_), channel_id=1, source_target_pairs={{0,1},{1,0},{2,3},{3,2},{4,5},{5,4},{6,7},{7,6},{8,9},{9,8},{10,11... | collective-permute-start | bytes 1572872 | tf_op jit(solution)/shard_map/ppermute | solution.py:395
  35.5 9.6 %collective-permute-start.15 = (bf16[912,128]{1,0:T(8,128)(2,1)S(1)}, bf16[912,128]{1,0:T(8,128)(2,1)S(1)}, u32[]{:S(2)}, u32[]{:S(2)}) collective-permute-start(bf16[912,128]{1,0:T(8,128)(2,1)S(1)} %collective-permute-done.8.refs_0_.refs_10_), channel_id=1, source_target_pairs={{0,8},{8,16},{16,24},{24,28},{28,20},{20,12},{12,4},{4,0},{1,9},{9... | collective-permute-start | bytes 700424 | tf_op jit(solution)/shard_map/ppermute | solution.py:385
  37.1 8.0 %collective-permute-start.16 = (bf16[912,128]{1,0:T(8,128)(2,1)S(1)}, bf16[912,128]{1,0:T(8,128)(2,1)S(1)}, u32[]{:S(2)}, u32[]{:S(2)}) collective-permute-start(bf16[912,128]{1,0:T(8,128)(2,1)S(1)} %collective-permute-done.11.refs_1_.refs_13_), channel_id=1, source_target_pairs={{8,0},{16,8},{24,16},{28,24},{20,28},{12,20},{4,12},{0,4},{9,1},{1... | collective-permute-start | bytes 700424 | tf_op jit(solution)/shard_map/ppermute | solution.py:386
  46.0 13.2 %all-to-all-start = ((f32[32,1,128]{2,1,0:T(1,128)}), f32[32,1,128]{2,1,0:T(1,128)S(1)}, u32[]{:S(2)}, u32[]{:S(2)}) async-start(f32[32,1,128]{2,1,0:T(1,128)} %bitcast.9), calls=%async_computation | async-start | bytes 32768 | tf_op jit(solution)/shard_map/all_to_all | solution.py:420
  52.1 7.1 %copy-start = (s32[128,8]{0,1:T(8,128)S(1)}, s32[128,8]{0,1:T(8,128)}, u32[]{:S(2)}) copy-start(s32[128,8]{0,1:T(8,128)} %param.8) | copy-start | bytes 12292

commit v4 on v3

--- a/solution.py
+++ b/solution.py
@@ -134,51 +134,72 @@
     )(*[in_hbm(x) for x in (gate_pre, up_pre, weight)])
 
 
-def assemble(info, parts, weight, scaled, tokens, steps):
+def assemble(info, parts, weight, tokens, steps, feats):
     slots, width = parts[0].shape
-    units, feats = weight.shape
+    units = weight.shape[0]
     groups, experts = len(parts), slots // tokens
     cols = 256
+
+    def body(info_ref, *refs):
+        part_refs, (w_ref, h_ref, ht_ref, eo_ref) = refs[:groups], refs[groups:]
+        for m, ref in enumerate(part_refs):
+            at = pl.multiple_of((info_ref[0] ^ m) * width, width)
+            for i, step in enumerate(steps):
+                start = pl.multiple_of(source_of(info_ref[1], step, experts) * tokens, tokens)
+                value = ref[pl.ds(start, tokens), :]
+                here = slice(i * tokens, (i + 1) * tokens)
+                h_ref[here, pl.ds(at, width)] = value
+                ht_ref[pl.ds(at, width), here] = value.T
+        for j in range(feats // cols):
+            here = slice(j * cols, (j + 1) * cols)
+            eo_ref[:, here] = jnp.dot(h_ref[...], w_ref[:, here], preferred_element_type=F32)
+
+    return pl.pallas_call(
+        body,
+        in_specs=[smem_spec()] + [vmem_spec()] * (groups + 1),
+        out_specs=[vmem_spec()] * 3,
+        out_shape=[
+            pltpu.VMEM((slots, units), BF16),
+            pltpu.VMEM((units, slots), BF16),
+            pltpu.VMEM((slots, feats), F32),
+        ],
+        compiler_params=params(6),
+        cost_estimate=pl.CostEstimate(flops=0, bytes_accessed=1000, transcendentals=0),
+        name="expert_out_first",
+    )(info, *parts, weight)
+
+
+def expert_out_rest(hidden, weight, scaled, feats):
+    slots = hidden.shape[0]
+    first, feats = feats, weight.shape[1]
+    cols = 256
     counts = [x.shape[0] for x in scaled]
 
-    def body(info_ref, *refs):
-        part_refs, refs = refs[:groups], refs[groups:]
-        scaled_refs, refs = refs[: len(scaled)], refs[len(scaled) :]
-        w_ref, ht_ref, eo_ref, out_ref, h_scr, sems = refs
+    def body(h_ref, w_ref, *refs):
+        scaled_refs, (eo_ref, out_ref, sems) = refs[: len(scaled)], refs[len(scaled) :]
         copies = [
             pltpu.make_async_copy(ref, out_ref.at[pl.ds(sum(counts[:i]), counts[i])], sems.at[i])
             for i, ref in enumerate(scaled_refs)
         ]
         for copy in copies:
             copy.start()
-        for m, ref in enumerate(part_refs):
-            at = pl.multiple_of((info_ref[0] ^ m) * width, width)
-            for i, step in enumerate(steps):
-                start = pl.multiple_of(source_of(info_ref[1], step, experts) * tokens, tokens)
-                value = ref[pl.ds(start, tokens), :]
-                here = slice(i * tokens, (i + 1) * tokens)
-                h_scr[here, pl.ds(at, width)] = value
-                ht_ref[pl.ds(at, width), here] = value.T
-        for j in range(feats // cols):
-            here = slice(j * cols, (j + 1) * cols)
-            eo_ref[:, here] = jnp.dot(h_scr[...], w_ref[:, here], preferred_element_type=F32)
+        for j in range(first, feats, cols):
+            eo_ref[:, j - first : j - first + cols] = jnp.dot(
+                h_ref[...], w_ref[:, j : j + cols], preferred_element_type=F32
+            )
         for copy in copies:
             copy.wait()
 
     return pl.pallas_call(
         body,
-        in_specs=[smem_spec()] + [vmem_spec()] * (groups + len(scaled) + 1),
-        out_specs=[vmem_spec(), vmem_spec(), any_spec()],
-        out_shape=[
-            pltpu.VMEM((units, slots), BF16),
-            pltpu.VMEM((slots, feats), F32),
-            pltpu.HBM((sum(counts), feats), BF16),
-        ],
-        scratch_shapes=[pltpu.VMEM((slots, units), BF16), pltpu.SemaphoreType.DMA((len(scaled),))],
+        in_specs=[vmem_spec()] * (2 + len(scaled)),
+        out_specs=[vmem_spec(), any_spec()],
+        out_shape=[pltpu.VMEM((slots, feats - first), F32), pltpu.HBM((sum(counts), feats), BF16)],
+        scratch_shapes=[pltpu.SemaphoreType.DMA((len(scaled),))],
         compiler_params=params(6),
         cost_estimate=pl.CostEstimate(flops=0, bytes_accessed=1000, transcendentals=0),
-        name="expert_out",
-    )(info, *parts, *scaled, weight)
+        name="expert_out_rest",
+    )(hidden, weight, *scaled)
 
 
 def column(row):
@@ -192,11 +213,14 @@
     return column(gate)[lower * half : (lower + 1) * half]
 
 
-def add_up(chunk_ref, eo_ref, at, half):
+def add_up(chunk_ref, eo_refs, at, half):
     total = jnp.zeros((half, LANES), F32)
-    for j in range(eo_ref.shape[1] // LANES):
-        value = chunk_ref[j * half : (j + 1) * half, :].astype(F32)
-        total = total + value * eo_ref[at : at + half, j * LANES : (j + 1) * LANES]
+    j = 0
+    for ref in eo_refs:
+        for k in range(ref.shape[1] // LANES):
+            value = chunk_ref[j * half : (j + 1) * half, :].astype(F32)
+            total = total + value * ref[at : at + half, k * LANES : (k + 1) * LANES]
+            j += 1
     return jnp.sum(total, axis=1, keepdims=True)
 
 
@@ -228,16 +252,17 @@
 
 def absorb(info, chunks, expert_out, tokens, steps, declared):
     half = tokens // 2
-    experts = expert_out.shape[0] // tokens
+    experts = expert_out[0].shape[0] // tokens
     count = len(chunks) // 2
 
     def body(info_ref, *refs):
-        chunk_refs, (eo_ref, sums_ref, last_ref, own_ref) = refs[: 2 * count], refs[2 * count :]
+        chunk_refs, eo_refs = refs[: 2 * count], refs[2 * count : 2 * count + 2]
+        sums_ref, last_ref, own_ref = refs[2 * count + 2 :]
         me = info_ref[1]
         lanes = []
         for i in range(count):
             at = i * tokens
-            sums = [add_up(chunk_refs[2 * i + c], eo_ref, at + c * half, half) for c in range(2)]
+            sums = [add_up(chunk_refs[2 * i + c], eo_refs, at + c * half, half) for c in range(2)]
             lanes.append(jnp.concatenate(sums, axis=0))
         lanes += [jnp.zeros((tokens, 1), F32)] * (experts - count)
         by_step = jnp.concatenate(lanes, axis=1).T
@@ -251,7 +276,7 @@
 
     return pl.pallas_call(
         body,
-        in_specs=[smem_spec()] + [vmem_spec()] * (2 * count + 1),
+        in_specs=[smem_spec()] + [vmem_spec()] * (2 * count + 2),
         out_specs=[vmem_spec()] * 3,
         out_shape=[
             pltpu.VMEM((experts, tokens), F32),
@@ -261,29 +286,29 @@
         compiler_params=params(4),
         cost_estimate=pl.CostEstimate(flops=declared, bytes_accessed=1000, transcendentals=0),
         name="absorb",
-    )(info, *chunks, expert_out)
+    )(info, *chunks, *expert_out)
 
 
 def absorb_last(chunks, expert_out, sums, mask, groups):
     experts, tokens = sums.shape
     half = tokens // 2
-    first = expert_out.shape[0] - tokens
-
-    def body(top_ref, bottom_ref, eo_ref, sums_ref, mask_ref, out_ref):
-        parts = [add_up(ref, eo_ref, first + c * half, half) for c, ref in enumerate((top_ref, bottom_ref))]
+    first = expert_out[0].shape[0] - tokens
+
+    def body(top_ref, bottom_ref, eo_ref, rest_ref, sums_ref, mask_ref, out_ref):
+        parts = [add_up(ref, (eo_ref, rest_ref), first + c * half, half) for c, ref in enumerate((top_ref, bottom_ref))]
         own = jnp.broadcast_to(jnp.concatenate(parts, axis=0), (tokens, experts)).T
         value = jnp.where(mask_ref[...] > 0.0, own, sums_ref[...])
         out_ref[...] = jnp.broadcast_to(value[:, None, :], out_ref.shape)
 
     return pl.pallas_call(
         body,
-        in_specs=[vmem_spec()] * 5,
+        in_specs=[vmem_spec()] * 6,
         out_specs=vmem_spec(),
         out_shape=jax.ShapeDtypeStruct((experts, groups, tokens), F32),
         compiler_params=params(2),
-        cost_estimate=cost(3 * tokens * expert_out.shape[1], 8 * tokens * expert_out.shape[1]),
+        cost_estimate=cost(tokens * LANES, tokens * LANES),
         name="absorb_last",
-    )(*chunks, expert_out, sums, mask)
+    )(*chunks, *expert_out, sums, mask)
 
 
 def weight_grad(own, early, early_places, late, late_places, last_chunks, hidden_t):
@@ -393,6 +418,7 @@
     hop(1)
     over = lax.ppermute(hidden, "et", chips)
     beside, across = lax.ppermute(hidden, "et", cores), lax.ppermute(over, "et", cores)
+    up[0], down[0] = barrier((up[0], down[0]))
     first = [up[0], up[1], down[1], down[0]]
     hop(0)
     hop(1)
@@ -403,15 +429,18 @@
     scaled_b = scale(second, [0, 1] * 2, 8000000000)
     up[1], down[1], scaled_b = barrier((up[1], down[1], scaled_b))
     hop(1)
+    cut = weight.shape[1] // 256 * 3 // 7 * 256
+    hidden, hidden_t, start = assemble(info, [hidden, beside, over, across], weight, tokens, steps, cut)
+    up[0], down[0], hidden_t = barrier((up[0], down[0], hidden_t))
     third = [up[0], up[1], down[1], down[0]]
     scaled_c = scale([up[0], down[0]], [0, 1], 12000000000)
-    scaled_d = scale([up[1], down[1]], [1, 0])
-    up[0], down[0], scaled_c, beside, across = barrier((up[0], down[0], scaled_c, beside, across))
+    up[0], down[0], scaled_c = barrier((up[0], down[0], scaled_c))
 
     hop(0)
-    hidden_t, expert_out, early = assemble(
-        info, [hidden, beside, over, across], weight, [scaled_a, scaled_b], tokens, steps
-    )
+    rest, early = expert_out_rest(hidden, weight, [scaled_a, scaled_b], cut)
+    expert_out = [start, rest]
+    third, early = barrier((third, early))
+    scaled_d = scale([third[1], third[2]], [1, 0])
     third, scaled_d = barrier((third, scaled_d))
     sums, mask, own = absorb(
         info, [top, bottom] + first + second + third, expert_out, tokens, steps, 3000

time: 60.1 us -> 57.3 us (0.953)
  waiting for transfers between devices: 13.6 us -> 8.72 us
  starting transfers between devices: 23.3 us -> 25.5 us
    ppermute x7, starting transfers between devices: 0.55 us -> 5.37 us  [hop(): down[c] = lax.ppermute(down[c], 'ep', back)]
    ppermute x7, starting transfers between devices: 14.6 us -> 11.9 us  [hop(): up[c] = lax.ppermute(up[c], 'ep', forth)]
    ppermute x7, waiting for transfers between devices: 7.2 us -> 4.6 us  [hop(): up[c] = lax.ppermute(up[c], 'ep', forth)]
    ppermute x7, waiting for transfers between devices: 5.47 us -> 3.69 us  [hop(): down[c] = lax.ppermute(down[c], 'ep', back)]
    pallas_call x2 -> x3, Pallas kernels: 6.24 us -> 6.06 us  [the longest x1 2.77 us: assemble(): pl.pallas_call(body, in_specs=[smem_spec()] + [vmem_spec()] * (groups + 1...]
  transfers between devices with their start and end apart: 18 -> 18, of which waited for: 9 -> 8; matrix products, arithmetic and copies ran while one was open for 0% -> 0% of each run, Pallas kernels for 33% -> 34%
where the time goes in v4:
time: 57.3 us; the launch traced here: 57.1 us
  starting transfers between devices  25.5 us (45%)
  Pallas kernels  22.1 us (39%)
  waiting for transfers between devices  8.72 us (15%)
  between operations  0.77 us (1%)
    ppermute x7, starting transfers between devices, hop(): up[c] = lax.ppermute(up[c], 'ep', forth)  11.9 us
    pallas_call x1, Pallas kernels, weight_grad(): pl.pallas_call(body, in_specs=[vmem_spec(), any_spec()] + [vmem_spec()] *...  6.71 us
    all_to_all x1, starting transfers between devices, dense(): lax.all_to_all(outgoing.reshape(experts * groups, tokens), ('ep', 'et'),...  6.2 us
    ppermute x7, starting transfers between devices, hop(): down[c] = lax.ppermute(down[c], 'ep', back)  5.37 us
    ppermute x7, waiting for transfers between devices, hop(): up[c] = lax.ppermute(up[c], 'ep', forth)  4.6 us
    ppermute x7, waiting for transfers between devices, hop(): down[c] = lax.ppermute(down[c], 'ep', back)  3.69 us
    pallas_call x4, Pallas kernels, scaled_rows(): pl.pallas_call(body, in_specs=[smem_spec()] + [vmem_spec()] * count, out_...  3.45 us
    pallas_call x1, Pallas kernels, assemble(): pl.pallas_call(body, in_specs=[smem_spec()] + [vmem_spec()] * (groups + 1...  2.77 us
  transfers between devices with their start and end apart: 18, of which 8 were waited for; matrix products, arithmetic and copies ran while one was open for 0% of the time, Pallas kernels for 34%

profile of v4, /device:TPU:0, one launch (start us, length us, event | category | flops | bytes accessed | tf_op | source)
XLA Modules:
  0.0 57.1 jit_solution(10888972865960519029)
XLA Ops:
  0.6 0.1 pad_add_fusion.info_ref
  0.7 1.2 %chunks.1 = (bf16[912,128]{1,0:T(8,128)(2,1)S(1)}, bf16[912,128]{1,0:T(8,128)(2,1)S(1)}) custom-call(bf16[128,1792]{1,0:T(8,128)(2,1)} %rows_ref, bf16[8,128]{1,0:T(8,128)(2,1)} %bitcast.21, s32[8,128]{1,0:T(8,128)} %bitcast.14), custom_call_target="tpu_custom_call" | custom-call | flops 917 | bytes 917 | tf_op jit(solution)/shard_map/chunks/pallas_call | solution.py:77
  1.9 3.1 %collective-permute-start = (bf16[912,128]{1,0:T(8,128)(2,1)S(1)}, bf16[912,128]{1,0:T(8,128)(2,1)S(1)}, u32[]{:S(2)}, u32[]{:S(2)}) collective-permute-start(bf16[912,128]{1,0:T(8,128)(2,1)S(1)} %get-tuple-element.42.refs_0_), channel_id=1, source_target_pairs={{0,8},{8,16},{16,24},{24,28},{28,20},{20,12},{12,4},{4,0},{1,9},{9... | collective-permute-start | bytes 700424 | tf_op jit(solution)/shard_map/ppermute | solution.py:410
  4.9 0.0 collective-permute-start.1
  5.0 2.0 %collective-permute-start.2 = (bf16[912,128]{1,0:T(8,128)(2,1)S(1)}, bf16[912,128]{1,0:T(8,128)(2,1)S(1)}, u32[]{:S(2)}, u32[]{:S(2)}) collective-permute-start(bf16[912,128]{1,0:T(8,128)(2,1)S(1)} %get-tuple-element.43.refs_1_), channel_id=1, source_target_pairs={{0,8},{8,16},{16,24},{24,28},{28,20},{20,12},{12,4},{4,0},{1,9},{9... | collective-permute-start | bytes 700424 | tf_op jit(solution)/shard_map/ppermute | solution.py:410
  7.0 0.0 collective-permute-start.3
  7.0 2.5 %hidden.1 = (bf16[1024,256]{1,0:T(8,128)(2,1)S(1)}, bf16[1024,1792]{1,0:T(8,128)(2,1)S(1)}) custom-call(bf16[1024,256]{1,0:T(8,128)(2,1)} %bitcast.18, bf16[1024,256]{1,0:T(8,128)(2,1)} %bitcast.19, bf16[1024,1792]{1,0:T(8,128)(2,1)} %bitcast.17), custom_call_target="tpu_custom_call" | custom-call | flops 2097 | bytes 1572 | tf_op jit(solution)/shard_map/hidden/pallas_call | solution.py:121
  9.5 2.0 %collective-permute-start.11 = (bf16[1024,256]{1,0:T(8,128)(2,1)S(1)}, bf16[1024,256]{1,0:T(8,128)(2,1)S(1)}, u32[]{:S(2)}, u32[]{:S(2)}) collective-permute-start(bf16[1024,256]{1,0:T(8,128)(2,1)S(1)} %get-tuple-element.48.refs_0_), channel_id=1, source_target_pairs={{0,2},{1,3},{2,0},{3,1},{4,6},{5,7},{6,4},{7,5},{8,10},{9,11},{10,... | collective-permute-start | bytes 1572872 | tf_op jit(solution)/shard_map/ppermute | solution.py:419
  11.6 0.0 collective-permute-done.refs_2_
  11.6 2.0 %collective-permute-done.1.refs_5_ = bf16[912,128]{1,0:T(8,128)(2,1)S(1)} collective-permute-done((bf16[912,128]{1,0:T(8,128)(2,1)S(1)}, bf16[912,128]{1,0:T(8,128)(2,1)S(1)}, u32[]{:S(2)}, u32[]{:S(2)}) %collective-permute-start.1) | collective-permute-done | bytes 233504 | tf_op jit(solution)/shard_map/ppermute | solution.py:411
  13.6 1.6 %collective-permute-start.4 = (bf16[912,128]{1,0:T(8,128)(2,1)S(1)}, bf16[912,128]{1,0:T(8,128)(2,1)S(1)}, u32[]{:S(2)}, u32[]{:S(2)}) collective-permute-start(bf16[912,128]{1,0:T(8,128)(2,1)S(1)} %collective-permute-done.refs_2_), channel_id=1, source_target_pairs={{0,8},{8,16},{16,24},{24,28},{28,20},{20,12},{12,4},{4,0},{1,9},{9... | collective-permute-start | bytes 700424 | tf_op jit(solution)/shard_map/ppermute | solution.py:410
  15.1 0.4 collective-permute-start.7
  15.6 0.8 %collective-permute-done.2.refs_3_ = bf16[912,128]{1,0:T(8,128)(2,1)S(1)} collective-permute-done((bf16[912,128]{1,0:T(8,128)(2,1)S(1)}, bf16[912,128]{1,0:T(8,128)(2,1)S(1)}, u32[]{:S(2)}, u32[]{:S(2)}) %collective-permute-start.2) | collective-permute-done | bytes 233504 | tf_op jit(solution)/shard_map/ppermute | solution.py:410
  16.4 2.1 %collective-permute-start.5 = (bf16[912,128]{1,0:T(8,128)(2,1)S(1)}, bf16[912,128]{1,0:T(8,128)(2,1)S(1)}, u32[]{:S(2)}, u32[]{:S(2)}) collective-permute-start(bf16[912,128]{1,0:T(8,128)(2,1)S(1)} %collective-permute-done.2.refs_3_), channel_id=1, source_target_pairs={{0,8},{8,16},{16,24},{24,28},{28,20},{20,12},{12,4},{4,0},{1,9},{9... | collective-permute-start | bytes 700424 | tf_op jit(solution)/shard_map/ppermute | solution.py:410
  18.5 0.0 collective-permute-done.3.refs_4_
  18.6 0.0 collective-permute-start.6
  18.6 1.0 %scaled_rows.4.refs_0_ = bf16[384,1792]{1,0:T(8,128)(2,1)S(1)} custom-call(s32[2]{0:T(128)S(1)} %pad_add_fusion.info_ref, bf16[912,128]{1,0:T(8,128)(2,1)S(1)} %get-tuple-element.42.refs_0_, bf16[912,128]{1,0:T(8,128)(2,1)S(1)} %get-tuple-element.43.refs_1_, bf16[912,128]{1,0:T(8,128)(2,1)S(1)} %collective-permute-done.refs_2_, ...), custom_call_target="tpu_custom_call" | custom-call | flops 4000000000 | bytes 1000 | tf_op jit(solution)/shard_map/scaled_rows/pallas_call | solution.py:242
  19.6 2.6 %collective-permute-done.4.refs_0_.refs_6_ = bf16[912,128]{1,0:T(8,128)(2,1)S(1)} collective-permute-done((bf16[912,128]{1,0:T(8,128)(2,1)S(1)}, bf16[912,128]{1,0:T(8,128)(2,1)S(1)}, u32[]{:S(2)}, u32[]{:S(2)}) %collective-permute-start.4) | collective-permute-done | bytes 233504 | tf_op jit(solution)/shard_map/ppermute | solution.py:410
  22.2 0.0 collective-permute-start.10
  22.2 1.6 %collective-permute-done.7.refs_3_.refs_9_ = bf16[912,128]{1,0:T(8,128)(2,1)S(1)} collective-permute-done((bf16[912,128]{1,0:T(8,128)(2,1)S(1)}, bf16[912,128]{1,0:T(8,128)(2,1)S(1)}, u32[]{:S(2)}, u32[]{:S(2)}) %collective-permute-start.7) | collective-permute-done | bytes 233504 | tf_op jit(solution)/shard_map/ppermute | solution.py:411
  23.8 1.6 %collective-permute-start.8 = (bf16[912,128]{1,0:T(8,128)(2,1)S(1)}, bf16[912,128]{1,0:T(8,128)(2,1)S(1)}, u32[]{:S(2)}, u32[]{:S(2)}) collective-permute-start(bf16[912,128]{1,0:T(8,128)(2,1)S(1)} %collective-permute-done.4.refs_0_.refs_6_), channel_id=1, source_target_pairs={{0,8},{8,16},{16,24},{24,28},{28,20},{20,12},{12,4},{4,0},{1,9},{9... | collective-permute-start | bytes 700424 | tf_op jit(solution)/shard_map/ppermute | solution.py:410
  25.4 0.4 collective-permute-done.5.refs_1_.refs_7_
  25.8 2.2 %collective-permute-start.9 = (bf16[912,128]{1,0:T(8,128)(2,1)S(1)}, bf16[912,128]{1,0:T(8,128)(2,1)S(1)}, u32[]{:S(2)}, u32[]{:S(2)}) collective-permute-start(bf16[912,128]{1,0:T(8,128)(2,1)S(1)} %collective-permute-done.7.refs_3_.refs_9_), channel_id=1, source_target_pairs={{8,0},{16,8},{24,16},{28,24},{20,28},{12,20},{4,12},{0,4},{9,1},{1... | collective-permute-start | bytes 700424 | tf_op jit(solution)/shard_map/ppermute | solution.py:411
  28.0 0.0 collective-permute-done.11.refs_2_
  28.0 0.0 collective-permute-start.12
  28.0 0.0 collective-permute-done.6.refs_2_.refs_8_
  28.0 0.9 %scaled_rows.5.refs_1_ = bf16[256,1792]{1,0:T(8,128)(2,1)S(1)} custom-call(s32[2]{0:T(128)S(1)} %pad_add_fusion.info_ref, bf16[912,128]{1,0:T(8,128)(2,1)S(1)} %collective-permute-done.4.refs_0_.refs_6_, bf16[912,128]{1,0:T(8,128)(2,1)S(1)} %collective-permute-done.5.refs_1_.refs_7_, bf16[912,128]{1,0:T(8,128)(2,1)S(1)} %collective-permute-done.6.refs_2_.refs_8_, ...), custom_call_target="tpu_custom_call" | custom-call | flops 8000000000 | bytes 1000 | tf_op jit(solution)/shard_map/scaled_rows/pallas_call | solution.py:242
  28.9 0.7 %collective-permute-start.13 = (bf16[912,128]{1,0:T(8,128)(2,1)S(1)}, bf16[912,128]{1,0:T(8,128)(2,1)S(1)}, u32[]{:S(2)}, u32[]{:S(2)}) collective-permute-start(bf16[912,128]{1,0:T(8,128)(2,1)S(1)} %collective-permute-done.5.refs_1_.refs_7_), channel_id=1, source_target_pairs={{0,8},{8,16},{16,24},{24,28},{28,20},{20,12},{12,4},{4,0},{1,9},{9... | collective-permute-start | bytes 700424 | tf_op jit(solution)/shard_map/ppermute | solution.py:410
  29.6 0.0 collective-permute-done.10.refs_1_
  29.6 1.3 %collective-permute-start.14 = (bf16[912,128]{1,0:T(8,128)(2,1)S(1)}, bf16[912,128]{1,0:T(8,128)(2,1)S(1)}, u32[]{:S(2)}, u32[]{:S(2)}) collective-permute-start(bf16[912,128]{1,0:T(8,128)(2,1)S(1)} %collective-permute-done.6.refs_2_.refs_8_), channel_id=1, source_target_pairs={{8,0},{16,8},{24,16},{28,24},{20,28},{12,20},{4,12},{0,4},{9,1},{1... | collective-permute-start | bytes 700424 | tf_op jit(solution)/shard_map/ppermute | solution.py:411
  31.0 0.0 collective-permute-done.12.refs_3_
  31.0 2.8 %expert_out_first.1 = (bf16[1024,1024]{1,0:T(8,128)(2,1)S(1)}, bf16[1024,1024]{1,0:T(8,128)(2,1)S(1)}, f32[1024,768]{1,0:T(8,128)S(1)}) custom-call(s32[2]{0:T(128)S(1)} %pad_add_fusion.info_ref, bf16[1024,256]{1,0:T(8,128)(2,1)S(1)} %get-tuple-element.48.refs_0_, bf16[1024,256]{1,0:T(8,128)(2,1)S(1)} %collective-permute-done.10.refs_1_, ...), custom_call_target="tpu_custom_call" | custom-call | bytes 1000 | tf_op jit(solution)/shard_map/expert_out_first/pallas_call | solution.py:157
  33.8 0.0 collective-permute-done.8.refs_10_.refs_0_
  33.8 0.0 collective-permute-done.9.refs_13_.refs_1_
  33.8 0.8 %scaled_rows.7.refs_0_ = bf16[128,1792]{1,0:T(8,128)(2,1)S(1)} custom-call(s32[2]{0:T(128)S(1)} %pad_add_fusion.info_ref, bf16[912,128]{1,0:T(8,128)(2,1)S(1)} %collective-permute-done.8.refs_10_.refs_0_, bf16[912,128]{1,0:T(8,128)(2,1)S(1)} %collective-permute-done.9.refs_13_.refs_1_), custom_call_target="tpu_custom_call" | custom-call | flops 12000000000 | bytes 1000 | tf_op jit(solution)/shard_map/scaled_rows/pallas_call | solution.py:242
  34.6 0.7 %collective-permute-start.15 = (bf16[912,128]{1,0:T(8,128)(2,1)S(1)}, bf16[912,128]{1,0:T(8,128)(2,1)S(1)}, u32[]{:S(2)}, u32[]{:S(2)}) collective-permute-start(bf16[912,128]{1,0:T(8,128)(2,1)S(1)} %collective-permute-done.8.refs_10_.refs_0_), channel_id=1, source_target_pairs={{0,8},{8,16},{16,24},{24,28},{28,20},{20,12},{12,4},{4,0},{1,9},{9... | collective-permute-start | bytes 700424 | tf_op jit(solution)/shard_map/ppermute | solution.py:410
  35.3 1.3 %collective-permute-start.16 = (bf16[912,128]{1,0:T(8,128)(2,1)S(1)}, bf16[912,128]{1,0:T(8,128)(2,1)S(1)}, u32[]{:S(2)}, u32[]{:S(2)}) collective-permute-start(bf16[912,128]{1,0:T(8,128)(2,1)S(1)} %collective-permute-done.9.refs_13_.refs_1_), channel_id=1, source_target_pairs={{8,0},{16,8},{24,16},{28,24},{20,28},{12,20},{4,12},{0,4},{9,1},{1... | collective-permute-start | bytes 700424 | tf_op jit(solution)/shard_map/ppermute | solution.py:411
  36.6 2.4 %expert_out_rest.1 = (f32[1024,1024]{1,0:T(8,128)S(1)}, bf16[640,1792]{1,0:T(8,128)(2,1)}) custom-call(bf16[1024,1024]{1,0:T(8,128)(2,1)S(1)} %get-tuple-element.55.h_ref, bf16[1024,1792]{1,0:T(8,128)(2,1)S(1)} %get-tuple-element.49.refs_4_.w_ref, bf16[384,1792]{1,0:T(8,128)(2,1)S(1)} %scaled_rows.4.refs_0_, bf16[256,1792]{1,0:T(8,128)(2,1)S(1)} %scaled_rows.5.refs_1_), custom_call_target="tpu_custom_call" | custom-call | bytes 1000 | tf_op jit(solution)/shard_map/expert_out_rest/pallas_call | solution.py:193
  39.0 0.0 collective-permute-done.13.refs_0_.refs_11_
  39.0 0.0 collective-permute-done.14.refs_1_.refs_12_
  39.0 0.8 %scaled_rows.6.refs_1_ = bf16[128,1792]{1,0:T(8,128)(2,1)S(1)} custom-call(s32[2]{0:T(128)S(1)} %pad_add_fusion.info_ref, bf16[912,128]{1,0:T(8,128)(2,1)S(1)} %collective-permute-done.13.refs_0_.refs_11_, bf16[912,128]{1,0:T(8,128)(2,1)S(1)} %collective-permute-done.14.refs_1_.refs_12_), custom_call_target="tpu_custom_call" | custom-call | bytes 1000 | tf_op jit(solution)/shard_map/scaled_rows/pallas_call | solution.py:242
  39.8 1.5 %absorb.1 = (f32[8,128]{1,0:T(8,128)S(1)}, f32[8,128]{1,0:T(8,128)S(1)}, f32[16,128]{1,0:T(8,128)S(1)}) custom-call(s32[2]{0:T(128)S(1)} %pad_add_fusion.info_ref, bf16[912,128]{1,0:T(8,128)(2,1)S(1)} %get-tuple-element.42.refs_0_, bf16[912,128]{1,0:T(8,128)(2,1)S(1)} %get-tuple-element.43.refs_1_, bf16[912,128]{1,0:T(8,128)(2,1)S(1)} %collective-permute-done.refs_2_, ...), custom_call_target="tpu_custom_call" | custom-call | flops 3000 | bytes 1000 | tf_op jit(solution)/shard_map/absorb/pallas_call | solution.py:277
  41.4 0.8 %collective-permute-done.15.refs_2_.top_ref = bf16[912,128]{1,0:T(8,128)(2,1)S(1)} collective-permute-done((bf16[912,128]{1,0:T(8,128)(2,1)S(1)}, bf16[912,128]{1,0:T(8,128)(2,1)S(1)}, u32[]{:S(2)}, u32[]{:S(2)}) %collective-permute-start.15) | collective-permute-done | bytes 233504 | tf_op jit(solution)/shard_map/ppermute | solution.py:410
  42.1 0.1 collective-permute-done.16.refs_3_.bottom_ref
  42.2 0.9 %absorb_last.1 = f32[8,4,128]{2,1,0:T(4,128)} custom-call(bf16[912,128]{1,0:T(8,128)(2,1)S(1)} %collective-permute-done.15.refs_2_.top_ref, bf16[912,128]{1,0:T(8,128)(2,1)S(1)} %collective-permute-done.16.refs_3_.bottom_ref, f32[1024,768]{1,0:T(8,128)S(1)} %get-tuple-element.67.refs_14_.eo_ref, f32[1024,1024]{1,0:T(8,128)S(1)} %get-tuple-element.68.refs_15_.rest_ref, ...), custom_call_target="tpu_custom_call" | custom-call | flops 16 | bytes 16 | tf_op jit(solution)/shard_map/absorb_last/pallas_call | solution.py:303
  43.1 6.2 %all-to-all-start = ((f32[32,1,128]{2,1,0:T(1,128)}), f32[32,1,128]{2,1,0:T(1,128)S(1)}, u32[]{:S(2)}, u32[]{:S(2)}) async-start(f32[32,1,128]{2,1,0:T(1,128)} %bitcast.9), calls=%async_computation | async-start | bytes 32768 | tf_op jit(solution)/shard_map/all_to_all | solution.py:449
  49.4 0.0 copy-start
  49.4 6.7 %weight_grad.1 = bf16[1024,1792]{1,0:T(8,128)(2,1)} custom-call(f32[16,128]{1,0:T(8,128)S(1)} %get-tuple-element.69.own_ref, bf16[640,1792]{1,0:T(8,128)(2,1)} %get-tuple-element.70.early_ref, bf16[128,1792]{1,0:T(8,128)(2,1)S(1)} %scaled_rows.7.refs_0_, bf16[128,1792]{1,0:T(8,128)(2,1)S(1)} %scaled_rows.6.refs_1_, ...), custom_call_target="tpu_custom_call" | custom-call | flops 3758096 | bytes 7340 | tf_op jit(solution)/shard_map/weight_grad/pallas_call | solution.py:351
  56.1 0.4 all-to-all-done
  56.5 0.0 copy-done
  56.5 0.6 %pick_gate_grad.1 = f32[8,128]{1,0:T(8,128)} custom-call(f32[8,4,128]{2,1,0:T(4,128)S(1)} %bitcast.13, s32[8,128]{1,0:T(8,128)S(1)} %bitcast.15), custom_call_target="tpu_custom_call" | custom-call | tf_op jit(solution)/shard_map/pick_gate_grad/pallas_call | solution.py:380
Async XLA Ops:
  1.9 9.7 %collective-permute-start = (bf16[912,128]{1,0:T(8,128)(2,1)S(1)}, bf16[912,128]{1,0:T(8,128)(2,1)S(1)}, u32[]{:S(2)}, u32[]{:S(2)}) collective-permute-start(bf16[912,128]{1,0:T(8,128)(2,1)S(1)} %get-tuple-element.42.refs_0_), channel_id=1, source_target_pairs={{0,8},{8,16},{16,24},{24,28},{28,20},{20,12},{12,4},{4,0},{1,9},{9... | collective-permute-start | bytes 700424 | tf_op jit(solution)/shard_map/ppermute | solution.py:410
  4.9 8.6 %collective-permute-start.1 = (bf16[912,128]{1,0:T(8,128)(2,1)S(1)}, bf16[912,128]{1,0:T(8,128)(2,1)S(1)}, u32[]{:S(2)}, u32[]{:S(2)}) collective-permute-start(bf16[912,128]{1,0:T(8,128)(2,1)S(1)} %get-tuple-element.43.refs_1_), channel_id=1, source_target_pairs={{8,0},{16,8},{24,16},{28,24},{20,28},{12,20},{4,12},{0,4},{9,1},{1... | collective-permute-start | bytes 700424 | tf_op jit(solution)/shard_map/ppermute | solution.py:411
  5.0 11.4 %collective-permute-start.2 = (bf16[912,128]{1,0:T(8,128)(2,1)S(1)}, bf16[912,128]{1,0:T(8,128)(2,1)S(1)}, u32[]{:S(2)}, u32[]{:S(2)}) collective-permute-start(bf16[912,128]{1,0:T(8,128)(2,1)S(1)} %get-tuple-element.43.refs_1_), channel_id=1, source_target_pairs={{0,8},{8,16},{16,24},{24,28},{28,20},{20,12},{12,4},{4,0},{1,9},{9... | collective-permute-start | bytes 700424 | tf_op jit(solution)/shard_map/ppermute | solution.py:410
  7.0 11.6 %collective-permute-start.3 = (bf16[912,128]{1,0:T(8,128)(2,1)S(1)}, bf16[912,128]{1,0:T(8,128)(2,1)S(1)}, u32[]{:S(2)}, u32[]{:S(2)}) collective-permute-start(bf16[912,128]{1,0:T(8,128)(2,1)S(1)} %get-tuple-element.42.refs_0_), channel_id=1, source_target_pairs={{8,0},{16,8},{24,16},{28,24},{20,28},{12,20},{4,12},{0,4},{9,1},{1... | collective-permute-start | bytes 700424 | tf_op jit(solution)/shard_map/ppermute | solution.py:411
  9.5 18.5 %collective-permute-start.11 = (bf16[1024,256]{1,0:T(8,128)(2,1)S(1)}, bf16[1024,256]{1,0:T(8,128)(2,1)S(1)}, u32[]{:S(2)}, u32[]{:S(2)}) collective-permute-start(bf16[1024,256]{1,0:T(8,128)(2,1)S(1)} %get-tuple-element.48.refs_0_), channel_id=1, source_target_pairs={{0,2},{1,3},{2,0},{3,1},{4,6},{5,7},{6,4},{7,5},{8,10},{9,11},{10,... | collective-permute-start | bytes 1572872 | tf_op jit(solution)/shard_map/ppermute | solution.py:419
  13.6 8.6 %collective-permute-start.4 = (bf16[912,128]{1,0:T(8,128)(2,1)S(1)}, bf16[912,128]{1,0:T(8,128)(2,1)S(1)}, u32[]{:S(2)}, u32[]{:S(2)}) collective-permute-start(bf16[912,128]{1,0:T(8,128)(2,1)S(1)} %collective-permute-done.refs_2_), channel_id=1, source_target_pairs={{0,8},{8,16},{16,24},{24,28},{28,20},{20,12},{12,4},{4,0},{1,9},{9... | collective-permute-start | bytes 700424 | tf_op jit(solution)/shard_map/ppermute | solution.py:410
  15.1 8.6 %collective-permute-start.7 = (bf16[912,128]{1,0:T(8,128)(2,1)S(1)}, bf16[912,128]{1,0:T(8,128)(2,1)S(1)}, u32[]{:S(2)}, u32[]{:S(2)}) collective-permute-start(bf16[912,128]{1,0:T(8,128)(2,1)S(1)} %collective-permute-done.1.refs_5_), channel_id=1, source_target_pairs={{8,0},{16,8},{24,16},{28,24},{20,28},{12,20},{4,12},{0,4},{9,1},{1... | collective-permute-start | bytes 700424 | tf_op jit(solution)/shard_map/ppermute | solution.py:411
  16.4 9.4 %collective-permute-start.5 = (bf16[912,128]{1,0:T(8,128)(2,1)S(1)}, bf16[912,128]{1,0:T(8,128)(2,1)S(1)}, u32[]{:S(2)}, u32[]{:S(2)}) collective-permute-start(bf16[912,128]{1,0:T(8,128)(2,1)S(1)} %collective-permute-done.2.refs_3_), channel_id=1, source_target_pairs={{0,8},{8,16},{16,24},{24,28},{28,20},{20,12},{12,4},{4,0},{1,9},{9... | collective-permute-start | bytes 700424 | tf_op jit(solution)/shard_map/ppermute | solution.py:410
  18.6 9.4 %collective-permute-start.6 = (bf16[912,128]{1,0:T(8,128)(2,1)S(1)}, bf16[912,128]{1,0:T(8,128)(2,1)S(1)}, u32[]{:S(2)}, u32[]{:S(2)}) collective-permute-start(bf16[912,128]{1,0:T(8,128)(2,1)S(1)} %collective-permute-done.3.refs_4_), channel_id=1, source_target_pairs={{8,0},{16,8},{24,16},{28,24},{20,28},{12,20},{4,12},{0,4},{9,1},{1... | collective-permute-start | bytes 700424 | tf_op jit(solution)/shard_map/ppermute | solution.py:411
  22.2 7.4 %collective-permute-start.10 = (bf16[1024,256]{1,0:T(8,128)(2,1)S(1)}, bf16[1024,256]{1,0:T(8,128)(2,1)S(1)}, u32[]{:S(2)}, u32[]{:S(2)}) collective-permute-start(bf16[1024,256]{1,0:T(8,128)(2,1)S(1)} %get-tuple-element.48.refs_0_), channel_id=1, source_target_pairs={{0,1},{1,0},{2,3},{3,2},{4,5},{5,4},{6,7},{7,6},{8,9},{9,8},{10,11... | collective-permute-start | bytes 1572872 | tf_op jit(solution)/shard_map/ppermute | solution.py:420
  23.8 10.0 %collective-permute-start.8 = (bf16[912,128]{1,0:T(8,128)(2,1)S(1)}, bf16[912,128]{1,0:T(8,128)(2,1)S(1)}, u32[]{:S(2)}, u32[]{:S(2)}) collective-permute-start(bf16[912,128]{1,0:T(8,128)(2,1)S(1)} %collective-permute-done.4.refs_0_.refs_6_), channel_id=1, source_target_pairs={{0,8},{8,16},{16,24},{24,28},{28,20},{20,12},{12,4},{4,0},{1,9},{9... | collective-permute-start | bytes 700424 | tf_op jit(solution)/shard_map/ppermute | solution.py:410
  25.8 8.0 %collective-permute-start.9 = (bf16[912,128]{1,0:T(8,128)(2,1)S(1)}, bf16[912,128]{1,0:T(8,128)(2,1)S(1)}, u32[]{:S(2)}, u32[]{:S(2)}) collective-permute-start(bf16[912,128]{1,0:T(8,128)(2,1)S(1)} %collective-permute-done.7.refs_3_.refs_9_), channel_id=1, source_target_pairs={{8,0},{16,8},{24,16},{28,24},{20,28},{12,20},{4,12},{0,4},{9,1},{1... | collective-permute-start | bytes 700424 | tf_op jit(solution)/shard_map/ppermute | solution.py:411
  28.0 3.0 %collective-permute-start.12 = (bf16[1024,256]{1,0:T(8,128)(2,1)S(1)}, bf16[1024,256]{1,0:T(8,128)(2,1)S(1)}, u32[]{:S(2)}, u32[]{:S(2)}) collective-permute-start(bf16[1024,256]{1,0:T(8,128)(2,1)S(1)} %collective-permute-done.11.refs_2_), channel_id=1, source_target_pairs={{0,1},{1,0},{2,3},{3,2},{4,5},{5,4},{6,7},{7,6},{8,9},{9,8},{10,11... | collective-permute-start | bytes 1572872 | tf_op jit(solution)/shard_map/ppermute | solution.py:420
  28.9 10.1 %collective-permute-start.13 = (bf16[912,128]{1,0:T(8,128)(2,1)S(1)}, bf16[912,128]{1,0:T(8,128)(2,1)S(1)}, u32[]{:S(2)}, u32[]{:S(2)}) collective-permute-start(bf16[912,128]{1,0:T(8,128)(2,1)S(1)} %collective-permute-done.5.refs_1_.refs_7_), channel_id=1, source_target_pairs={{0,8},{8,16},{16,24},{24,28},{28,20},{20,12},{12,4},{4,0},{1,9},{9... | collective-permute-start | bytes 700424 | tf_op jit(solution)/shard_map/ppermute | solution.py:410
  29.6 9.4 %collective-permute-start.14 = (bf16[912,128]{1,0:T(8,128)(2,1)S(1)}, bf16[912,128]{1,0:T(8,128)(2,1)S(1)}, u32[]{:S(2)}, u32[]{:S(2)}) collective-permute-start(bf16[912,128]{1,0:T(8,128)(2,1)S(1)} %collective-permute-done.6.refs_2_.refs_8_), channel_id=1, source_target_pairs={{8,0},{16,8},{24,16},{28,24},{20,28},{12,20},{4,12},{0,4},{9,1},{1... | collective-permute-start | bytes 700424 | tf_op jit(solution)/shard_map/ppermute | solution.py:411
  34.6 7.6 %collective-permute-start.15 = (bf16[912,128]{1,0:T(8,128)(2,1)S(1)}, bf16[912,128]{1,0:T(8,128)(2,1)S(1)}, u32[]{:S(2)}, u32[]{:S(2)}) collective-permute-start(bf16[912,128]{1,0:T(8,128)(2,1)S(1)} %collective-permute-done.8.refs_10_.refs_0_), channel_id=1, source_target_pairs={{0,8},{8,16},{16,24},{24,28},{28,20},{20,12},{12,4},{4,0},{1,9},{9... | collective-permute-start | bytes 700424 | tf_op jit(solution)/shard_map/ppermute | solution.py:410
  35.3 6.9 %collective-permute-start.16 = (bf16[912,128]{1,0:T(8,128)(2,1)S(1)}, bf16[912,128]{1,0:T(8,128)(2,1)S(1)}, u32[]{:S(2)}, u32[]{:S(2)}) collective-permute-start(bf16[912,128]{1,0:T(8,128)(2,1)S(1)} %collective-permute-done.9.refs_13_.refs_1_), channel_id=1, source_target_pairs={{8,0},{16,8},{24,16},{28,24},{20,28},{12,20},{4,12},{0,4},{9,1},{1... | collective-permute-start | bytes 700424 | tf_op jit(solution)/shard_map/ppermute | solution.py:411
  43.1 13.4 %all-to-all-start = ((f32[32,1,128]{2,1,0:T(1,128)}), f32[32,1,128]{2,1,0:T(1,128)S(1)}, u32[]{:S(2)}, u32[]{:S(2)}) async-start(f32[32,1,128]{2,1,0:T(1,128)} %bitcast.9), calls=%async_computation | async-start | bytes 32768 | tf_op jit(solution)/shard_map/all_to_all | solution.py:449
  49.4 7.2 %copy-start = (s32[128,8]{0,1:T(8,128)S(1)}, s32[128,8]{0,1:T(8,128)}, u32[]{:S(2)}) copy-start(s32[128,8]{0,1:T(8,128)} %param.8) | copy-start | bytes 12292

commit v5 on v4

--- a/solution.py
+++ b/solution.py
@@ -27,8 +27,8 @@
     return pltpu.CompilerParams(vmem_limit_bytes=mib * MIB)
 
 
-def cost(flops, moved):
-    return pl.CostEstimate(flops=int(flops) // 1000, bytes_accessed=int(moved) // 1000, transcendentals=0)
+def declared(flops=0):
+    return pl.CostEstimate(flops=int(flops), bytes_accessed=1000, transcendentals=0)
 
 
 def in_hbm(x):
@@ -51,44 +51,31 @@
     half = tokens // 2
     cols = feats // LANES
 
-    def body(rows_ref, g_ref, r_ref, top_ref, bottom_ref, rows_scr, g_scr, r_scr, sems):
-        copies = [
-            pltpu.make_async_copy(src, dst, sems.at[i])
-            for i, (src, dst) in enumerate(((g_ref, g_scr), (r_ref, r_scr), (rows_ref, rows_scr)))
-        ]
-        for copy in copies:
-            copy.start()
-        for copy in copies[:2]:
-            copy.wait()
-        routes = r_scr[...]
-        gates = g_scr[...].astype(F32)
+    def body(rows_ref, g_ref, r_ref, top_ref, bottom_ref):
+        routes = r_ref[...]
+        gates = g_ref[...].astype(F32)
         by = [
             jnp.sum(jnp.where(routes == e, gates, 0.0), axis=0, keepdims=True) for e in range(experts)
         ]
         by = jnp.concatenate(by + [jnp.zeros((16 - experts, tokens), F32)], axis=0).astype(BF16)
-        copies[2].wait()
         for c, ref in enumerate((top_ref, bottom_ref)):
             for j in range(cols):
-                ref[j * half : (j + 1) * half, :] = rows_scr[
+                ref[j * half : (j + 1) * half, :] = rows_ref[
                     c * half : (c + 1) * half, j * LANES : (j + 1) * LANES
                 ]
             ref[cols * half :, :] = by
 
-    return pl.pallas_call(
-        body,
-        in_specs=[any_spec()] * 3,
+    operands = (out_grad, gates_t, routes_t)
+    return pl.pallas_call(
+        body,
+        grid=(1,),
+        in_specs=[pl.BlockSpec(x.shape, lambda i: (0, 0)) for x in operands],
         out_specs=[vmem_spec()] * 2,
         out_shape=[pltpu.VMEM((cols * half + 16, LANES), BF16)] * 2,
-        scratch_shapes=[
-            pltpu.VMEM(out_grad.shape, BF16),
-            pltpu.VMEM(gates_t.shape, BF16),
-            pltpu.VMEM(routes_t.shape, jnp.int32),
-            pltpu.SemaphoreType.DMA((3,)),
-        ],
         compiler_params=params(4),
-        cost_estimate=cost(4 * tokens * feats, 4 * tokens * feats),
+        cost_estimate=declared(),
         name="chunks",
-    )(*[in_hbm(x) for x in (out_grad, gates_t, routes_t)])
+    )(*[in_hbm(x) for x in operands])
 
 
 def hidden_of(gate_pre, up_pre, weight):
@@ -129,7 +116,7 @@
             pltpu.SemaphoreType.DMA((2 * blocks + 1,)),
         ],
         compiler_params=params(4),
-        cost_estimate=cost(8 * slots * width, 6 * slots * width),
+        cost_estimate=declared(),
         name="hidden",
     )(*[in_hbm(x) for x in (gate_pre, up_pre, weight)])
 
@@ -164,7 +151,7 @@
             pltpu.VMEM((slots, feats), F32),
         ],
         compiler_params=params(6),
-        cost_estimate=pl.CostEstimate(flops=0, bytes_accessed=1000, transcendentals=0),
+        cost_estimate=declared(),
         name="expert_out_first",
     )(info, *parts, weight)
 
@@ -197,7 +184,7 @@
         out_shape=[pltpu.VMEM((slots, feats - first), F32), pltpu.HBM((sum(counts), feats), BF16)],
         scratch_shapes=[pltpu.SemaphoreType.DMA((len(scaled),))],
         compiler_params=params(6),
-        cost_estimate=pl.CostEstimate(flops=0, bytes_accessed=1000, transcendentals=0),
+        cost_estimate=declared(),
         name="expert_out_rest",
     )(hidden, weight, *scaled)
 
@@ -230,7 +217,7 @@
         out_ref[at : at + half, j * LANES : (j + 1) * LANES] = (value * gate).astype(BF16)
 
 
-def scaled_rows(info, chunks, lowers, half, declared):
+def scaled_rows(info, chunks, lowers, half, flops):
     cols = (chunks[0].shape[0] - 16) // half
     count = len(chunks)
 
@@ -245,12 +232,12 @@
         out_specs=vmem_spec(),
         out_shape=pltpu.VMEM((count * half, cols * LANES), BF16),
         compiler_params=params(3),
-        cost_estimate=pl.CostEstimate(flops=declared, bytes_accessed=1000, transcendentals=0),
+        cost_estimate=declared(flops),
         name="scaled_rows",
     )(info, *chunks)
 
 
-def absorb(info, chunks, expert_out, tokens, steps, declared):
+def absorb(info, chunks, expert_out, tokens, steps):
     half = tokens // 2
     experts = expert_out[0].shape[0] // tokens
     count = len(chunks) // 2
@@ -284,7 +271,7 @@
             pltpu.VMEM((16, LANES), F32),
         ],
         compiler_params=params(4),
-        cost_estimate=pl.CostEstimate(flops=declared, bytes_accessed=1000, transcendentals=0),
+        cost_estimate=declared(),
         name="absorb",
     )(info, *chunks, *expert_out)
 
@@ -306,7 +293,7 @@
         out_specs=vmem_spec(),
         out_shape=jax.ShapeDtypeStruct((experts, groups, tokens), F32),
         compiler_params=params(2),
-        cost_estimate=cost(tokens * LANES, tokens * LANES),
+        cost_estimate=declared(),
         name="absorb_last",
     )(*chunks, *expert_out, sums, mask)
 
@@ -360,7 +347,7 @@
             pltpu.SemaphoreType.DMA((blocks,)),
         ],
         compiler_params=params(12),
-        cost_estimate=cost(2 * slots * units * feats, 4 * units * feats),
+        cost_estimate=declared(),
         name="weight_grad",
     )(own, in_hbm(early), *late, *last_chunks, hidden_t)
 
@@ -410,8 +397,8 @@
         up[c] = lax.ppermute(up[c], "ep", forth)
         down[c] = lax.ppermute(down[c], "ep", back)
 
-    def scale(chunks, lowers, declared=0):
-        return scaled_rows(info, chunks, lowers, half, declared)
+    def scale(chunks, lowers, flops=0):
+        return scaled_rows(info, chunks, lowers, half, flops)
 
     up, down = [top, bottom], [bottom, top]
     hop(0)
@@ -423,17 +410,17 @@
     hop(0)
     hop(1)
     second = [up[0], up[1], down[1], down[0]]
-    scaled_a = scale([top, bottom] + first, [0, 1] * 3, 4000000000)
+    scaled_a = scale([top, bottom] + first, [0, 1] * 3, 4e9)
     up[0], down[0], scaled_a = barrier((up[0], down[0], scaled_a))
     hop(0)
-    scaled_b = scale(second, [0, 1] * 2, 8000000000)
+    scaled_b = scale(second, [0, 1] * 2, 8e9)
     up[1], down[1], scaled_b = barrier((up[1], down[1], scaled_b))
     hop(1)
     cut = weight.shape[1] // 256 * 3 // 7 * 256
     hidden, hidden_t, start = assemble(info, [hidden, beside, over, across], weight, tokens, steps, cut)
     up[0], down[0], hidden_t = barrier((up[0], down[0], hidden_t))
     third = [up[0], up[1], down[1], down[0]]
-    scaled_c = scale([up[0], down[0]], [0, 1], 12000000000)
+    scaled_c = scale([up[0], down[0]], [0, 1], 12e9)
     up[0], down[0], scaled_c = barrier((up[0], down[0], scaled_c))
 
     hop(0)
@@ -442,9 +429,7 @@
     third, early = barrier((third, early))
     scaled_d = scale([third[1], third[2]], [1, 0])
     third, scaled_d = barrier((third, scaled_d))
-    sums, mask, own = absorb(
-        info, [top, bottom] + first + second + third, expert_out, tokens, steps, 3000
-    )
+    sums, mask, own = absorb(info, [top, bottom] + first + second + third, expert_out, tokens, steps)
     outgoing = absorb_last([up[0], down[0]], expert_out, sums, mask, groups)
     returned = lax.all_to_all(
         outgoing.reshape(experts * groups, tokens), ("ep", "et"), split_axis=0, concat_axis=0, tiled=True

time: 57.3 us -> 57.3 us (level)
  no operation moved by 1% of the time
where the time goes in v5:
time: 57.3 us; the launch traced here: 57.1 us
  starting transfers between devices  25.5 us (45%)
  Pallas kernels  22 us (38%)
  waiting for transfers between devices  8.72 us (15%)
  between operations  0.77 us (1%)
    ppermute x7, starting transfers between devices, hop(): up[c] = lax.ppermute(up[c], 'ep', forth)  11.9 us
    pallas_call x1, Pallas kernels, weight_grad(): pl.pallas_call(body, in_specs=[vmem_spec(), any_spec()] + [vmem_spec()] *...  6.71 us
    all_to_all x1, starting transfers between devices, dense(): lax.all_to_all(outgoing.reshape(experts * groups, tokens), ('ep', 'et'),...  6.2 us
    ppermute x7, starting transfers between devices, hop(): down[c] = lax.ppermute(down[c], 'ep', back)  5.36 us
    ppermute x7, waiting for transfers between devices, hop(): up[c] = lax.ppermute(up[c], 'ep', forth)  4.6 us
    ppermute x7, waiting for transfers between devices, hop(): down[c] = lax.ppermute(down[c], 'ep', back)  3.69 us
    pallas_call x4, Pallas kernels, scaled_rows(): pl.pallas_call(body, in_specs=[smem_spec()] + [vmem_spec()] * count, out_...  3.45 us
    pallas_call x1, Pallas kernels, assemble(): pl.pallas_call(body, in_specs=[smem_spec()] + [vmem_spec()] * (groups + 1...  2.76 us
  transfers between devices with their start and end apart: 18, of which 8 were waited for; matrix products, arithmetic and copies ran while one was open for 0% of the time, Pallas kernels for 34%

profile of v5, /device:TPU:0, one launch (start us, length us, event | category | flops | bytes accessed | tf_op | source)
XLA Modules:
  0.0 57.1 jit_solution(14083182590008057119)
XLA Ops:
  0.6 0.1 pad_add_fusion.info_ref
  0.7 1.1 %chunks.1 = (bf16[912,128]{1,0:T(8,128)(2,1)S(1)}, bf16[912,128]{1,0:T(8,128)(2,1)S(1)}) custom-call(bf16[128,1792]{1,0:T(8,128)(2,1)} %rows_ref, bf16[8,128]{1,0:T(8,128)(2,1)} %bitcast.21, s32[8,128]{1,0:T(8,128)} %bitcast.14), custom_call_target="tpu_custom_call" | custom-call | bytes 1000 | tf_op jit(solution)/shard_map/chunks/pallas_call | solution.py:69
  1.8 3.1 %collective-permute-start = (bf16[912,128]{1,0:T(8,128)(2,1)S(1)}, bf16[912,128]{1,0:T(8,128)(2,1)S(1)}, u32[]{:S(2)}, u32[]{:S(2)}) collective-permute-start(bf16[912,128]{1,0:T(8,128)(2,1)S(1)} %get-tuple-element.42.refs_0_), channel_id=1, source_target_pairs={{0,8},{8,16},{16,24},{24,28},{28,20},{20,12},{12,4},{4,0},{1,9},{9... | collective-permute-start | bytes 700424 | tf_op jit(solution)/shard_map/ppermute | solution.py:397
  4.9 0.0 collective-permute-start.1
  4.9 2.0 %collective-permute-start.2 = (bf16[912,128]{1,0:T(8,128)(2,1)S(1)}, bf16[912,128]{1,0:T(8,128)(2,1)S(1)}, u32[]{:S(2)}, u32[]{:S(2)}) collective-permute-start(bf16[912,128]{1,0:T(8,128)(2,1)S(1)} %get-tuple-element.43.refs_1_), channel_id=1, source_target_pairs={{0,8},{8,16},{16,24},{24,28},{28,20},{20,12},{12,4},{4,0},{1,9},{9... | collective-permute-start | bytes 700424 | tf_op jit(solution)/shard_map/ppermute | solution.py:397
  6.9 0.0 collective-permute-start.3
  6.9 2.5 %hidden.1 = (bf16[1024,256]{1,0:T(8,128)(2,1)S(1)}, bf16[1024,1792]{1,0:T(8,128)(2,1)S(1)}) custom-call(bf16[1024,256]{1,0:T(8,128)(2,1)} %bitcast.18, bf16[1024,256]{1,0:T(8,128)(2,1)} %bitcast.19, bf16[1024,1792]{1,0:T(8,128)(2,1)} %bitcast.17), custom_call_target="tpu_custom_call" | custom-call | bytes 1000 | tf_op jit(solution)/shard_map/hidden/pallas_call | solution.py:108
  9.5 2.0 %collective-permute-start.11 = (bf16[1024,256]{1,0:T(8,128)(2,1)S(1)}, bf16[1024,256]{1,0:T(8,128)(2,1)S(1)}, u32[]{:S(2)}, u32[]{:S(2)}) collective-permute-start(bf16[1024,256]{1,0:T(8,128)(2,1)S(1)} %get-tuple-element.48.refs_0_), channel_id=1, source_target_pairs={{0,2},{1,3},{2,0},{3,1},{4,6},{5,7},{6,4},{7,5},{8,10},{9,11},{10,... | collective-permute-start | bytes 1572872 | tf_op jit(solution)/shard_map/ppermute | solution.py:406
  11.5 0.0 collective-permute-done.refs_2_
  11.5 2.0 %collective-permute-done.1.refs_5_ = bf16[912,128]{1,0:T(8,128)(2,1)S(1)} collective-permute-done((bf16[912,128]{1,0:T(8,128)(2,1)S(1)}, bf16[912,128]{1,0:T(8,128)(2,1)S(1)}, u32[]{:S(2)}, u32[]{:S(2)}) %collective-permute-start.1) | collective-permute-done | bytes 233504 | tf_op jit(solution)/shard_map/ppermute | solution.py:398
  13.5 1.6 %collective-permute-start.4 = (bf16[912,128]{1,0:T(8,128)(2,1)S(1)}, bf16[912,128]{1,0:T(8,128)(2,1)S(1)}, u32[]{:S(2)}, u32[]{:S(2)}) collective-permute-start(bf16[912,128]{1,0:T(8,128)(2,1)S(1)} %collective-permute-done.refs_2_), channel_id=1, source_target_pairs={{0,8},{8,16},{16,24},{24,28},{28,20},{20,12},{12,4},{4,0},{1,9},{9... | collective-permute-start | bytes 700424 | tf_op jit(solution)/shard_map/ppermute | solution.py:397
  15.1 0.4 collective-permute-start.7
  15.6 0.8 %collective-permute-done.2.refs_3_ = bf16[912,128]{1,0:T(8,128)(2,1)S(1)} collective-permute-done((bf16[912,128]{1,0:T(8,128)(2,1)S(1)}, bf16[912,128]{1,0:T(8,128)(2,1)S(1)}, u32[]{:S(2)}, u32[]{:S(2)}) %collective-permute-start.2) | collective-permute-done | bytes 233504 | tf_op jit(solution)/shard_map/ppermute | solution.py:397
  16.3 2.1 %collective-permute-start.5 = (bf16[912,128]{1,0:T(8,128)(2,1)S(1)}, bf16[912,128]{1,0:T(8,128)(2,1)S(1)}, u32[]{:S(2)}, u32[]{:S(2)}) collective-permute-start(bf16[912,128]{1,0:T(8,128)(2,1)S(1)} %collective-permute-done.2.refs_3_), channel_id=1, source_target_pairs={{0,8},{8,16},{16,24},{24,28},{28,20},{20,12},{12,4},{4,0},{1,9},{9... | collective-permute-start | bytes 700424 | tf_op jit(solution)/shard_map/ppermute | solution.py:397
  18.5 0.0 collective-permute-done.3.refs_4_
  18.5 0.0 collective-permute-start.6
  18.5 1.0 %scaled_rows.4.refs_0_ = bf16[384,1792]{1,0:T(8,128)(2,1)S(1)} custom-call(s32[2]{0:T(128)S(1)} %pad_add_fusion.info_ref, bf16[912,128]{1,0:T(8,128)(2,1)S(1)} %get-tuple-element.42.refs_0_, bf16[912,128]{1,0:T(8,128)(2,1)S(1)} %get-tuple-element.43.refs_1_, bf16[912,128]{1,0:T(8,128)(2,1)S(1)} %collective-permute-done.refs_2_, ...), custom_call_target="tpu_custom_call" | custom-call | flops 4000000000 | bytes 1000 | tf_op jit(solution)/shard_map/scaled_rows/pallas_call | solution.py:229
  19.5 2.6 %collective-permute-done.4.refs_0_.refs_6_ = bf16[912,128]{1,0:T(8,128)(2,1)S(1)} collective-permute-done((bf16[912,128]{1,0:T(8,128)(2,1)S(1)}, bf16[912,128]{1,0:T(8,128)(2,1)S(1)}, u32[]{:S(2)}, u32[]{:S(2)}) %collective-permute-start.4) | collective-permute-done | bytes 233504 | tf_op jit(solution)/shard_map/ppermute | solution.py:397
  22.2 0.0 collective-permute-start.10
  22.2 1.6 %collective-permute-done.7.refs_3_.refs_9_ = bf16[912,128]{1,0:T(8,128)(2,1)S(1)} collective-permute-done((bf16[912,128]{1,0:T(8,128)(2,1)S(1)}, bf16[912,128]{1,0:T(8,128)(2,1)S(1)}, u32[]{:S(2)}, u32[]{:S(2)}) %collective-permute-start.7) | collective-permute-done | bytes 233504 | tf_op jit(solution)/shard_map/ppermute | solution.py:398
  23.7 1.6 %collective-permute-start.8 = (bf16[912,128]{1,0:T(8,128)(2,1)S(1)}, bf16[912,128]{1,0:T(8,128)(2,1)S(1)}, u32[]{:S(2)}, u32[]{:S(2)}) collective-permute-start(bf16[912,128]{1,0:T(8,128)(2,1)S(1)} %collective-permute-done.4.refs_0_.refs_6_), channel_id=1, source_target_pairs={{0,8},{8,16},{16,24},{24,28},{28,20},{20,12},{12,4},{4,0},{1,9},{9... | collective-permute-start | bytes 700424 | tf_op jit(solution)/shard_map/ppermute | solution.py:397
  25.3 0.4 collective-permute-done.5.refs_1_.refs_7_
  25.7 2.2 %collective-permute-start.9 = (bf16[912,128]{1,0:T(8,128)(2,1)S(1)}, bf16[912,128]{1,0:T(8,128)(2,1)S(1)}, u32[]{:S(2)}, u32[]{:S(2)}) collective-permute-start(bf16[912,128]{1,0:T(8,128)(2,1)S(1)} %collective-permute-done.7.refs_3_.refs_9_), channel_id=1, source_target_pairs={{8,0},{16,8},{24,16},{28,24},{20,28},{12,20},{4,12},{0,4},{9,1},{1... | collective-permute-start | bytes 700424 | tf_op jit(solution)/shard_map/ppermute | solution.py:398
  27.9 0.0 collective-permute-done.11.refs_2_
  27.9 0.0 collective-permute-start.12
  28.0 0.0 collective-permute-done.6.refs_2_.refs_8_
  28.0 0.9 %scaled_rows.5.refs_1_ = bf16[256,1792]{1,0:T(8,128)(2,1)S(1)} custom-call(s32[2]{0:T(128)S(1)} %pad_add_fusion.info_ref, bf16[912,128]{1,0:T(8,128)(2,1)S(1)} %collective-permute-done.4.refs_0_.refs_6_, bf16[912,128]{1,0:T(8,128)(2,1)S(1)} %collective-permute-done.5.refs_1_.refs_7_, bf16[912,128]{1,0:T(8,128)(2,1)S(1)} %collective-permute-done.6.refs_2_.refs_8_, ...), custom_call_target="tpu_custom_call" | custom-call | flops 8000000000 | bytes 1000 | tf_op jit(solution)/shard_map/scaled_rows/pallas_call | solution.py:229
  28.9 0.7 %collective-permute-start.13 = (bf16[912,128]{1,0:T(8,128)(2,1)S(1)}, bf16[912,128]{1,0:T(8,128)(2,1)S(1)}, u32[]{:S(2)}, u32[]{:S(2)}) collective-permute-start(bf16[912,128]{1,0:T(8,128)(2,1)S(1)} %collective-permute-done.5.refs_1_.refs_7_), channel_id=1, source_target_pairs={{0,8},{8,16},{16,24},{24,28},{28,20},{20,12},{12,4},{4,0},{1,9},{9... | collective-permute-start | bytes 700424 | tf_op jit(solution)/shard_map/ppermute | solution.py:397
  29.6 0.0 collective-permute-done.10.refs_1_
  29.6 1.3 %collective-permute-start.14 = (bf16[912,128]{1,0:T(8,128)(2,1)S(1)}, bf16[912,128]{1,0:T(8,128)(2,1)S(1)}, u32[]{:S(2)}, u32[]{:S(2)}) collective-permute-start(bf16[912,128]{1,0:T(8,128)(2,1)S(1)} %collective-permute-done.6.refs_2_.refs_8_), channel_id=1, source_target_pairs={{8,0},{16,8},{24,16},{28,24},{20,28},{12,20},{4,12},{0,4},{9,1},{1... | collective-permute-start | bytes 700424 | tf_op jit(solution)/shard_map/ppermute | solution.py:398
  30.9 0.0 collective-permute-done.12.refs_3_
  30.9 2.8 %expert_out_first.1 = (bf16[1024,1024]{1,0:T(8,128)(2,1)S(1)}, bf16[1024,1024]{1,0:T(8,128)(2,1)S(1)}, f32[1024,768]{1,0:T(8,128)S(1)}) custom-call(s32[2]{0:T(128)S(1)} %pad_add_fusion.info_ref, bf16[1024,256]{1,0:T(8,128)(2,1)S(1)} %get-tuple-element.48.refs_0_, bf16[1024,256]{1,0:T(8,128)(2,1)S(1)} %collective-permute-done.10.refs_1_, ...), custom_call_target="tpu_custom_call" | custom-call | bytes 1000 | tf_op jit(solution)/shard_map/expert_out_first/pallas_call | solution.py:144
  33.7 0.0 collective-permute-done.8.refs_10_.refs_0_
  33.7 0.0 collective-permute-done.9.refs_13_.refs_1_
  33.7 0.8 %scaled_rows.7.refs_0_ = bf16[128,1792]{1,0:T(8,128)(2,1)S(1)} custom-call(s32[2]{0:T(128)S(1)} %pad_add_fusion.info_ref, bf16[912,128]{1,0:T(8,128)(2,1)S(1)} %collective-permute-done.8.refs_10_.refs_0_, bf16[912,128]{1,0:T(8,128)(2,1)S(1)} %collective-permute-done.9.refs_13_.refs_1_), custom_call_target="tpu_custom_call" | custom-call | flops 12000000000 | bytes 1000 | tf_op jit(solution)/shard_map/scaled_rows/pallas_call | solution.py:229
  34.5 0.7 %collective-permute-start.15 = (bf16[912,128]{1,0:T(8,128)(2,1)S(1)}, bf16[912,128]{1,0:T(8,128)(2,1)S(1)}, u32[]{:S(2)}, u32[]{:S(2)}) collective-permute-start(bf16[912,128]{1,0:T(8,128)(2,1)S(1)} %collective-permute-done.8.refs_10_.refs_0_), channel_id=1, source_target_pairs={{0,8},{8,16},{16,24},{24,28},{28,20},{20,12},{12,4},{4,0},{1,9},{9... | collective-permute-start | bytes 700424 | tf_op jit(solution)/shard_map/ppermute | solution.py:397
  35.3 1.3 %collective-permute-start.16 = (bf16[912,128]{1,0:T(8,128)(2,1)S(1)}, bf16[912,128]{1,0:T(8,128)(2,1)S(1)}, u32[]{:S(2)}, u32[]{:S(2)}) collective-permute-start(bf16[912,128]{1,0:T(8,128)(2,1)S(1)} %collective-permute-done.9.refs_13_.refs_1_), channel_id=1, source_target_pairs={{8,0},{16,8},{24,16},{28,24},{20,28},{12,20},{4,12},{0,4},{9,1},{1... | collective-permute-start | bytes 700424 | tf_op jit(solution)/shard_map/ppermute | solution.py:398
  36.6 2.4 %expert_out_rest.1 = (f32[1024,1024]{1,0:T(8,128)S(1)}, bf16[640,1792]{1,0:T(8,128)(2,1)}) custom-call(bf16[1024,1024]{1,0:T(8,128)(2,1)S(1)} %get-tuple-element.55.h_ref, bf16[1024,1792]{1,0:T(8,128)(2,1)S(1)} %get-tuple-element.49.refs_4_.w_ref, bf16[384,1792]{1,0:T(8,128)(2,1)S(1)} %scaled_rows.4.refs_0_, bf16[256,1792]{1,0:T(8,128)(2,1)S(1)} %scaled_rows.5.refs_1_), custom_call_target="tpu_custom_call" | custom-call | bytes 1000 | tf_op jit(solution)/shard_map/expert_out_rest/pallas_call | solution.py:180
  39.0 0.0 collective-permute-done.13.refs_0_.refs_11_
  39.0 0.0 collective-permute-done.14.refs_1_.refs_12_
  39.0 0.8 %scaled_rows.6.refs_1_ = bf16[128,1792]{1,0:T(8,128)(2,1)S(1)} custom-call(s32[2]{0:T(128)S(1)} %pad_add_fusion.info_ref, bf16[912,128]{1,0:T(8,128)(2,1)S(1)} %collective-permute-done.13.refs_0_.refs_11_, bf16[912,128]{1,0:T(8,128)(2,1)S(1)} %collective-permute-done.14.refs_1_.refs_12_), custom_call_target="tpu_custom_call" | custom-call | bytes 1000 | tf_op jit(solution)/shard_map/scaled_rows/pallas_call | solution.py:229
  39.8 1.5 %absorb.1 = (f32[8,128]{1,0:T(8,128)S(1)}, f32[8,128]{1,0:T(8,128)S(1)}, f32[16,128]{1,0:T(8,128)S(1)}) custom-call(s32[2]{0:T(128)S(1)} %pad_add_fusion.info_ref, bf16[912,128]{1,0:T(8,128)(2,1)S(1)} %get-tuple-element.42.refs_0_, bf16[912,128]{1,0:T(8,128)(2,1)S(1)} %get-tuple-element.43.refs_1_, bf16[912,128]{1,0:T(8,128)(2,1)S(1)} %collective-permute-done.refs_2_, ...), custom_call_target="tpu_custom_call" | custom-call | bytes 1000 | tf_op jit(solution)/shard_map/absorb/pallas_call | solution.py:264
  41.3 0.8 %collective-permute-done.15.refs_2_.top_ref = bf16[912,128]{1,0:T(8,128)(2,1)S(1)} collective-permute-done((bf16[912,128]{1,0:T(8,128)(2,1)S(1)}, bf16[912,128]{1,0:T(8,128)(2,1)S(1)}, u32[]{:S(2)}, u32[]{:S(2)}) %collective-permute-start.15) | collective-permute-done | bytes 233504 | tf_op jit(solution)/shard_map/ppermute | solution.py:397
  42.1 0.1 collective-permute-done.16.refs_3_.bottom_ref
  42.2 0.9 %absorb_last.1 = f32[8,4,128]{2,1,0:T(4,128)} custom-call(bf16[912,128]{1,0:T(8,128)(2,1)S(1)} %collective-permute-done.15.refs_2_.top_ref, bf16[912,128]{1,0:T(8,128)(2,1)S(1)} %collective-permute-done.16.refs_3_.bottom_ref, f32[1024,768]{1,0:T(8,128)S(1)} %get-tuple-element.67.refs_14_.eo_ref, f32[1024,1024]{1,0:T(8,128)S(1)} %get-tuple-element.68.refs_15_.rest_ref, ...), custom_call_target="tpu_custom_call" | custom-call | bytes 1000 | tf_op jit(solution)/shard_map/absorb_last/pallas_call | solution.py:290
  43.1 6.2 %all-to-all-start = ((f32[32,1,128]{2,1,0:T(1,128)}), f32[32,1,128]{2,1,0:T(1,128)S(1)}, u32[]{:S(2)}, u32[]{:S(2)}) async-start(f32[32,1,128]{2,1,0:T(1,128)} %bitcast.9), calls=%async_computation | async-start | bytes 32768 | tf_op jit(solution)/shard_map/all_to_all | solution.py:434
  49.3 0.0 copy-start
  49.3 6.7 %weight_grad.1 = bf16[1024,1792]{1,0:T(8,128)(2,1)} custom-call(f32[16,128]{1,0:T(8,128)S(1)} %get-tuple-element.69.own_ref, bf16[640,1792]{1,0:T(8,128)(2,1)} %get-tuple-element.70.early_ref, bf16[128,1792]{1,0:T(8,128)(2,1)S(1)} %scaled_rows.7.refs_0_, bf16[128,1792]{1,0:T(8,128)(2,1)S(1)} %scaled_rows.6.refs_1_, ...), custom_call_target="tpu_custom_call" | custom-call | bytes 1000 | tf_op jit(solution)/shard_map/weight_grad/pallas_call | solution.py:338
  56.0 0.4 all-to-all-done
  56.5 0.0 copy-done
  56.5 0.6 %pick_gate_grad.1 = f32[8,128]{1,0:T(8,128)} custom-call(f32[8,4,128]{2,1,0:T(4,128)S(1)} %bitcast.13, s32[8,128]{1,0:T(8,128)S(1)} %bitcast.15), custom_call_target="tpu_custom_call" | custom-call | tf_op jit(solution)/shard_map/pick_gate_grad/pallas_call | solution.py:367
Async XLA Ops:
  1.8 9.7 %collective-permute-start = (bf16[912,128]{1,0:T(8,128)(2,1)S(1)}, bf16[912,128]{1,0:T(8,128)(2,1)S(1)}, u32[]{:S(2)}, u32[]{:S(2)}) collective-permute-start(bf16[912,128]{1,0:T(8,128)(2,1)S(1)} %get-tuple-element.42.refs_0_), channel_id=1, source_target_pairs={{0,8},{8,16},{16,24},{24,28},{28,20},{20,12},{12,4},{4,0},{1,9},{9... | collective-permute-start | bytes 700424 | tf_op jit(solution)/shard_map/ppermute | solution.py:397
  4.9 8.6 %collective-permute-start.1 = (bf16[912,128]{1,0:T(8,128)(2,1)S(1)}, bf16[912,128]{1,0:T(8,128)(2,1)S(1)}, u32[]{:S(2)}, u32[]{:S(2)}) collective-permute-start(bf16[912,128]{1,0:T(8,128)(2,1)S(1)} %get-tuple-element.43.refs_1_), channel_id=1, source_target_pairs={{8,0},{16,8},{24,16},{28,24},{20,28},{12,20},{4,12},{0,4},{9,1},{1... | collective-permute-start | bytes 700424 | tf_op jit(solution)/shard_map/ppermute | solution.py:398
  4.9 11.4 %collective-permute-start.2 = (bf16[912,128]{1,0:T(8,128)(2,1)S(1)}, bf16[912,128]{1,0:T(8,128)(2,1)S(1)}, u32[]{:S(2)}, u32[]{:S(2)}) collective-permute-start(bf16[912,128]{1,0:T(8,128)(2,1)S(1)} %get-tuple-element.43.refs_1_), channel_id=1, source_target_pairs={{0,8},{8,16},{16,24},{24,28},{28,20},{20,12},{12,4},{4,0},{1,9},{9... | collective-permute-start | bytes 700424 | tf_op jit(solution)/shard_map/ppermute | solution.py:397
  6.9 11.6 %collective-permute-start.3 = (bf16[912,128]{1,0:T(8,128)(2,1)S(1)}, bf16[912,128]{1,0:T(8,128)(2,1)S(1)}, u32[]{:S(2)}, u32[]{:S(2)}) collective-permute-start(bf16[912,128]{1,0:T(8,128)(2,1)S(1)} %get-tuple-element.42.refs_0_), channel_id=1, source_target_pairs={{8,0},{16,8},{24,16},{28,24},{20,28},{12,20},{4,12},{0,4},{9,1},{1... | collective-permute-start | bytes 700424 | tf_op jit(solution)/shard_map/ppermute | solution.py:398
  9.5 18.5 %collective-permute-start.11 = (bf16[1024,256]{1,0:T(8,128)(2,1)S(1)}, bf16[1024,256]{1,0:T(8,128)(2,1)S(1)}, u32[]{:S(2)}, u32[]{:S(2)}) collective-permute-start(bf16[1024,256]{1,0:T(8,128)(2,1)S(1)} %get-tuple-element.48.refs_0_), channel_id=1, source_target_pairs={{0,2},{1,3},{2,0},{3,1},{4,6},{5,7},{6,4},{7,5},{8,10},{9,11},{10,... | collective-permute-start | bytes 1572872 | tf_op jit(solution)/shard_map/ppermute | solution.py:406
  13.5 8.6 %collective-permute-start.4 = (bf16[912,128]{1,0:T(8,128)(2,1)S(1)}, bf16[912,128]{1,0:T(8,128)(2,1)S(1)}, u32[]{:S(2)}, u32[]{:S(2)}) collective-permute-start(bf16[912,128]{1,0:T(8,128)(2,1)S(1)} %collective-permute-done.refs_2_), channel_id=1, source_target_pairs={{0,8},{8,16},{16,24},{24,28},{28,20},{20,12},{12,4},{4,0},{1,9},{9... | collective-permute-start | bytes 700424 | tf_op jit(solution)/shard_map/ppermute | solution.py:397
  15.1 8.6 %collective-permute-start.7 = (bf16[912,128]{1,0:T(8,128)(2,1)S(1)}, bf16[912,128]{1,0:T(8,128)(2,1)S(1)}, u32[]{:S(2)}, u32[]{:S(2)}) collective-permute-start(bf16[912,128]{1,0:T(8,128)(2,1)S(1)} %collective-permute-done.1.refs_5_), channel_id=1, source_target_pairs={{8,0},{16,8},{24,16},{28,24},{20,28},{12,20},{4,12},{0,4},{9,1},{1... | collective-permute-start | bytes 700424 | tf_op jit(solution)/shard_map/ppermute | solution.py:398
  16.3 9.4 %collective-permute-start.5 = (bf16[912,128]{1,0:T(8,128)(2,1)S(1)}, bf16[912,128]{1,0:T(8,128)(2,1)S(1)}, u32[]{:S(2)}, u32[]{:S(2)}) collective-permute-start(bf16[912,128]{1,0:T(8,128)(2,1)S(1)} %collective-permute-done.2.refs_3_), channel_id=1, source_target_pairs={{0,8},{8,16},{16,24},{24,28},{28,20},{20,12},{12,4},{4,0},{1,9},{9... | collective-permute-start | bytes 700424 | tf_op jit(solution)/shard_map/ppermute | solution.py:397
  18.5 9.4 %collective-permute-start.6 = (bf16[912,128]{1,0:T(8,128)(2,1)S(1)}, bf16[912,128]{1,0:T(8,128)(2,1)S(1)}, u32[]{:S(2)}, u32[]{:S(2)}) collective-permute-start(bf16[912,128]{1,0:T(8,128)(2,1)S(1)} %collective-permute-done.3.refs_4_), channel_id=1, source_target_pairs={{8,0},{16,8},{24,16},{28,24},{20,28},{12,20},{4,12},{0,4},{9,1},{1... | collective-permute-start | bytes 700424 | tf_op jit(solution)/shard_map/ppermute | solution.py:398
  22.2 7.4 %collective-permute-start.10 = (bf16[1024,256]{1,0:T(8,128)(2,1)S(1)}, bf16[1024,256]{1,0:T(8,128)(2,1)S(1)}, u32[]{:S(2)}, u32[]{:S(2)}) collective-permute-start(bf16[1024,256]{1,0:T(8,128)(2,1)S(1)} %get-tuple-element.48.refs_0_), channel_id=1, source_target_pairs={{0,1},{1,0},{2,3},{3,2},{4,5},{5,4},{6,7},{7,6},{8,9},{9,8},{10,11... | collective-permute-start | bytes 1572872 | tf_op jit(solution)/shard_map/ppermute | solution.py:407
  23.7 10.0 %collective-permute-start.8 = (bf16[912,128]{1,0:T(8,128)(2,1)S(1)}, bf16[912,128]{1,0:T(8,128)(2,1)S(1)}, u32[]{:S(2)}, u32[]{:S(2)}) collective-permute-start(bf16[912,128]{1,0:T(8,128)(2,1)S(1)} %collective-permute-done.4.refs_0_.refs_6_), channel_id=1, source_target_pairs={{0,8},{8,16},{16,24},{24,28},{28,20},{20,12},{12,4},{4,0},{1,9},{9... | collective-permute-start | bytes 700424 | tf_op jit(solution)/shard_map/ppermute | solution.py:397
  25.7 8.0 %collective-permute-start.9 = (bf16[912,128]{1,0:T(8,128)(2,1)S(1)}, bf16[912,128]{1,0:T(8,128)(2,1)S(1)}, u32[]{:S(2)}, u32[]{:S(2)}) collective-permute-start(bf16[912,128]{1,0:T(8,128)(2,1)S(1)} %collective-permute-done.7.refs_3_.refs_9_), channel_id=1, source_target_pairs={{8,0},{16,8},{24,16},{28,24},{20,28},{12,20},{4,12},{0,4},{9,1},{1... | collective-permute-start | bytes 700424 | tf_op jit(solution)/shard_map/ppermute | solution.py:398
  27.9 3.0 %collective-permute-start.12 = (bf16[1024,256]{1,0:T(8,128)(2,1)S(1)}, bf16[1024,256]{1,0:T(8,128)(2,1)S(1)}, u32[]{:S(2)}, u32[]{:S(2)}) collective-permute-start(bf16[1024,256]{1,0:T(8,128)(2,1)S(1)} %collective-permute-done.11.refs_2_), channel_id=1, source_target_pairs={{0,1},{1,0},{2,3},{3,2},{4,5},{5,4},{6,7},{7,6},{8,9},{9,8},{10,11... | collective-permute-start | bytes 1572872 | tf_op jit(solution)/shard_map/ppermute | solution.py:407
  28.9 10.1 %collective-permute-start.13 = (bf16[912,128]{1,0:T(8,128)(2,1)S(1)}, bf16[912,128]{1,0:T(8,128)(2,1)S(1)}, u32[]{:S(2)}, u32[]{:S(2)}) collective-permute-start(bf16[912,128]{1,0:T(8,128)(2,1)S(1)} %collective-permute-done.5.refs_1_.refs_7_), channel_id=1, source_target_pairs={{0,8},{8,16},{16,24},{24,28},{28,20},{20,12},{12,4},{4,0},{1,9},{9... | collective-permute-start | bytes 700424 | tf_op jit(solution)/shard_map/ppermute | solution.py:397
  29.6 9.4 %collective-permute-start.14 = (bf16[912,128]{1,0:T(8,128)(2,1)S(1)}, bf16[912,128]{1,0:T(8,128)(2,1)S(1)}, u32[]{:S(2)}, u32[]{:S(2)}) collective-permute-start(bf16[912,128]{1,0:T(8,128)(2,1)S(1)} %collective-permute-done.6.refs_2_.refs_8_), channel_id=1, source_target_pairs={{8,0},{16,8},{24,16},{28,24},{20,28},{12,20},{4,12},{0,4},{9,1},{1... | collective-permute-start | bytes 700424 | tf_op jit(solution)/shard_map/ppermute | solution.py:398
  34.5 7.6 %collective-permute-start.15 = (bf16[912,128]{1,0:T(8,128)(2,1)S(1)}, bf16[912,128]{1,0:T(8,128)(2,1)S(1)}, u32[]{:S(2)}, u32[]{:S(2)}) collective-permute-start(bf16[912,128]{1,0:T(8,128)(2,1)S(1)} %collective-permute-done.8.refs_10_.refs_0_), channel_id=1, source_target_pairs={{0,8},{8,16},{16,24},{24,28},{28,20},{20,12},{12,4},{4,0},{1,9},{9... | collective-permute-start | bytes 700424 | tf_op jit(solution)/shard_map/ppermute | solution.py:397
  35.3 6.9 %collective-permute-start.16 = (bf16[912,128]{1,0:T(8,128)(2,1)S(1)}, bf16[912,128]{1,0:T(8,128)(2,1)S(1)}, u32[]{:S(2)}, u32[]{:S(2)}) collective-permute-start(bf16[912,128]{1,0:T(8,128)(2,1)S(1)} %collective-permute-done.9.refs_13_.refs_1_), channel_id=1, source_target_pairs={{8,0},{16,8},{24,16},{28,24},{20,28},{12,20},{4,12},{0,4},{9,1},{1... | collective-permute-start | bytes 700424 | tf_op jit(solution)/shard_map/ppermute | solution.py:398
  43.1 13.4 %all-to-all-start = ((f32[32,1,128]{2,1,0:T(1,128)}), f32[32,1,128]{2,1,0:T(1,128)S(1)}, u32[]{:S(2)}, u32[]{:S(2)}) async-start(f32[32,1,128]{2,1,0:T(1,128)} %bitcast.9), calls=%async_computation | async-start | bytes 32768 | tf_op jit(solution)/shard_map/all_to_all | solution.py:434
  49.3 7.2 %copy-start = (s32[128,8]{0,1:T(8,128)S(1)}, s32[128,8]{0,1:T(8,128)}, u32[]{:S(2)}) copy-start(s32[128,8]{0,1:T(8,128)} %param.8) | copy-start | bytes 12292

commit v6 on v5

--- a/solution.py
+++ b/solution.py
@@ -416,7 +416,7 @@
     scaled_b = scale(second, [0, 1] * 2, 8e9)
     up[1], down[1], scaled_b = barrier((up[1], down[1], scaled_b))
     hop(1)
-    cut = weight.shape[1] // 256 * 3 // 7 * 256
+    cut = weight.shape[1] // 256 * 4 // 7 * 256
     hidden, hidden_t, start = assemble(info, [hidden, beside, over, across], weight, tokens, steps, cut)
     up[0], down[0], hidden_t = barrier((up[0], down[0], hidden_t))
     third = [up[0], up[1], down[1], down[0]]

time: 57.3 us -> 57.3 us (level)
  starting transfers between devices: 25.5 us -> 22 us
  waiting for transfers between devices: 8.72 us -> 12.2 us
    ppermute x7, waiting for transfers between devices: 3.69 us -> 9.76 us  [hop(): down[c] = lax.ppermute(down[c], 'ep', back)]
    ppermute x7, waiting for transfers between devices: 4.6 us -> 2 us  [hop(): up[c] = lax.ppermute(up[c], 'ep', forth)]
    ppermute x7, starting transfers between devices: 5.36 us -> 3.24 us  [hop(): down[c] = lax.ppermute(down[c], 'ep', back)]
    all_to_all x1, starting transfers between devices: 6.2 us -> 4.84 us  [dense(): lax.all_to_all(outgoing.reshape(experts * groups, tokens), ('ep', 'et'),...]
where the time goes in v6:
time: 57.3 us; the launch traced here: 57 us
  Pallas kernels  22 us (38%)
  starting transfers between devices  22 us (38%)
  waiting for transfers between devices  12.2 us (21%)
  between operations  0.77 us (1%)
    ppermute x7, starting transfers between devices, hop(): up[c] = lax.ppermute(up[c], 'ep', forth)  12 us
    ppermute x7, waiting for transfers between devices, hop(): down[c] = lax.ppermute(down[c], 'ep', back)  9.76 us
    pallas_call x1, Pallas kernels, weight_grad(): pl.pallas_call(body, in_specs=[vmem_spec(), any_spec()] + [vmem_spec()] *...  6.71 us
    all_to_all x1, starting transfers between devices, dense(): lax.all_to_all(outgoing.reshape(experts * groups, tokens), ('ep', 'et'),...  4.84 us
    pallas_call x4, Pallas kernels, scaled_rows(): pl.pallas_call(body, in_specs=[smem_spec()] + [vmem_spec()] * count, out_...  3.45 us
    pallas_call x1, Pallas kernels, assemble(): pl.pallas_call(body, in_specs=[smem_spec()] + [vmem_spec()] * (groups + 1...  3.32 us
    ppermute x7, starting transfers between devices, hop(): down[c] = lax.ppermute(down[c], 'ep', back)  3.24 us
    pallas_call x1, Pallas kernels, hidden_of(): pl.pallas_call(body, in_specs=[any_spec()] * 3, out_specs=[vmem_spec()] *...  2.55 us
  transfers between devices with their start and end apart: 18, of which 8 were waited for; matrix products, arithmetic and copies ran while one was open for 0% of the time, Pallas kernels for 34%

profile of v6, /device:TPU:0, one launch (start us, length us, event | category | flops | bytes accessed | tf_op | source)
XLA Modules:
  0.0 57.0 jit_solution(16968844089038865791)
XLA Ops:
  0.6 0.1 pad_add_fusion.info_ref
  0.7 1.1 %chunks.1 = (bf16[912,128]{1,0:T(8,128)(2,1)S(1)}, bf16[912,128]{1,0:T(8,128)(2,1)S(1)}) custom-call(bf16[128,1792]{1,0:T(8,128)(2,1)} %rows_ref, bf16[8,128]{1,0:T(8,128)(2,1)} %bitcast.21, s32[8,128]{1,0:T(8,128)} %bitcast.14), custom_call_target="tpu_custom_call" | custom-call | bytes 1000 | tf_op jit(solution)/shard_map/chunks/pallas_call | solution.py:69
  1.8 3.1 %collective-permute-start = (bf16[912,128]{1,0:T(8,128)(2,1)S(1)}, bf16[912,128]{1,0:T(8,128)(2,1)S(1)}, u32[]{:S(2)}, u32[]{:S(2)}) collective-permute-start(bf16[912,128]{1,0:T(8,128)(2,1)S(1)} %get-tuple-element.42.refs_0_), channel_id=1, source_target_pairs={{0,8},{8,16},{16,24},{24,28},{28,20},{20,12},{12,4},{4,0},{1,9},{9... | collective-permute-start | bytes 700424 | tf_op jit(solution)/shard_map/ppermute | solution.py:397
  4.9 0.0 collective-permute-start.1
  4.9 1.9 %collective-permute-start.3 = (bf16[912,128]{1,0:T(8,128)(2,1)S(1)}, bf16[912,128]{1,0:T(8,128)(2,1)S(1)}, u32[]{:S(2)}, u32[]{:S(2)}) collective-permute-start(bf16[912,128]{1,0:T(8,128)(2,1)S(1)} %get-tuple-element.42.refs_0_), channel_id=1, source_target_pairs={{8,0},{16,8},{24,16},{28,24},{20,28},{12,20},{4,12},{0,4},{9,1},{1... | collective-permute-start | bytes 700424 | tf_op jit(solution)/shard_map/ppermute | solution.py:398
  6.9 0.1 collective-permute-start.2
  7.0 2.5 %hidden.1 = (bf16[1024,256]{1,0:T(8,128)(2,1)S(1)}, bf16[1024,1792]{1,0:T(8,128)(2,1)S(1)}) custom-call(bf16[1024,256]{1,0:T(8,128)(2,1)} %bitcast.18, bf16[1024,256]{1,0:T(8,128)(2,1)} %bitcast.19, bf16[1024,1792]{1,0:T(8,128)(2,1)} %bitcast.17), custom_call_target="tpu_custom_call" | custom-call | bytes 1000 | tf_op jit(solution)/shard_map/hidden/pallas_call | solution.py:108
  9.5 2.0 %collective-permute-start.11 = (bf16[1024,256]{1,0:T(8,128)(2,1)S(1)}, bf16[1024,256]{1,0:T(8,128)(2,1)S(1)}, u32[]{:S(2)}, u32[]{:S(2)}) collective-permute-start(bf16[1024,256]{1,0:T(8,128)(2,1)S(1)} %get-tuple-element.48.refs_0_), channel_id=1, source_target_pairs={{0,2},{1,3},{2,0},{3,1},{4,6},{5,7},{6,4},{7,5},{8,10},{9,11},{10,... | collective-permute-start | bytes 1572872 | tf_op jit(solution)/shard_map/ppermute | solution.py:406
  11.5 0.0 collective-permute-done.refs_2_
  11.5 2.0 %collective-permute-done.1.refs_5_ = bf16[912,128]{1,0:T(8,128)(2,1)S(1)} collective-permute-done((bf16[912,128]{1,0:T(8,128)(2,1)S(1)}, bf16[912,128]{1,0:T(8,128)(2,1)S(1)}, u32[]{:S(2)}, u32[]{:S(2)}) %collective-permute-start.1) | collective-permute-done | bytes 233504 | tf_op jit(solution)/shard_map/ppermute | solution.py:398
  13.5 1.6 %collective-permute-start.4 = (bf16[912,128]{1,0:T(8,128)(2,1)S(1)}, bf16[912,128]{1,0:T(8,128)(2,1)S(1)}, u32[]{:S(2)}, u32[]{:S(2)}) collective-permute-start(bf16[912,128]{1,0:T(8,128)(2,1)S(1)} %collective-permute-done.refs_2_), channel_id=1, source_target_pairs={{0,8},{8,16},{16,24},{24,28},{28,20},{20,12},{12,4},{4,0},{1,9},{9... | collective-permute-start | bytes 700424 | tf_op jit(solution)/shard_map/ppermute | solution.py:397
  15.1 0.4 collective-permute-start.7
  15.6 3.0 %collective-permute-done.3.refs_4_ = bf16[912,128]{1,0:T(8,128)(2,1)S(1)} collective-permute-done((bf16[912,128]{1,0:T(8,128)(2,1)S(1)}, bf16[912,128]{1,0:T(8,128)(2,1)S(1)}, u32[]{:S(2)}, u32[]{:S(2)}) %collective-permute-start.3) | collective-permute-done | bytes 233504 | tf_op jit(solution)/shard_map/ppermute | solution.py:398
  18.5 0.0 collective-permute-start.6
  18.5 0.0 collective-permute-done.2.refs_3_
  18.5 2.0 %collective-permute-start.5 = (bf16[912,128]{1,0:T(8,128)(2,1)S(1)}, bf16[912,128]{1,0:T(8,128)(2,1)S(1)}, u32[]{:S(2)}, u32[]{:S(2)}) collective-permute-start(bf16[912,128]{1,0:T(8,128)(2,1)S(1)} %collective-permute-done.2.refs_3_), channel_id=1, source_target_pairs={{0,8},{8,16},{16,24},{24,28},{28,20},{20,12},{12,4},{4,0},{1,9},{9... | collective-permute-start | bytes 700424 | tf_op jit(solution)/shard_map/ppermute | solution.py:397
  20.6 1.0 %scaled_rows.4.refs_0_ = bf16[384,1792]{1,0:T(8,128)(2,1)S(1)} custom-call(s32[2]{0:T(128)S(1)} %pad_add_fusion.info_ref, bf16[912,128]{1,0:T(8,128)(2,1)S(1)} %get-tuple-element.42.refs_0_, bf16[912,128]{1,0:T(8,128)(2,1)S(1)} %get-tuple-element.43.refs_1_, bf16[912,128]{1,0:T(8,128)(2,1)S(1)} %collective-permute-done.refs_2_, ...), custom_call_target="tpu_custom_call" | custom-call | flops 4000000000 | bytes 1000 | tf_op jit(solution)/shard_map/scaled_rows/pallas_call | solution.py:229
  21.6 0.6 %collective-permute-done.4.refs_0_.refs_6_ = bf16[912,128]{1,0:T(8,128)(2,1)S(1)} collective-permute-done((bf16[912,128]{1,0:T(8,128)(2,1)S(1)}, bf16[912,128]{1,0:T(8,128)(2,1)S(1)}, u32[]{:S(2)}, u32[]{:S(2)}) %collective-permute-start.4) | collective-permute-done | bytes 233504 | tf_op jit(solution)/shard_map/ppermute | solution.py:397
  22.2 0.0 collective-permute-start.10
  22.2 1.6 %collective-permute-done.7.refs_3_.refs_9_ = bf16[912,128]{1,0:T(8,128)(2,1)S(1)} collective-permute-done((bf16[912,128]{1,0:T(8,128)(2,1)S(1)}, bf16[912,128]{1,0:T(8,128)(2,1)S(1)}, u32[]{:S(2)}, u32[]{:S(2)}) %collective-permute-start.7) | collective-permute-done | bytes 233504 | tf_op jit(solution)/shard_map/ppermute | solution.py:398
  23.7 1.6 %collective-permute-start.8 = (bf16[912,128]{1,0:T(8,128)(2,1)S(1)}, bf16[912,128]{1,0:T(8,128)(2,1)S(1)}, u32[]{:S(2)}, u32[]{:S(2)}) collective-permute-start(bf16[912,128]{1,0:T(8,128)(2,1)S(1)} %collective-permute-done.4.refs_0_.refs_6_), channel_id=1, source_target_pairs={{0,8},{8,16},{16,24},{24,28},{28,20},{20,12},{12,4},{4,0},{1,9},{9... | collective-permute-start | bytes 700424 | tf_op jit(solution)/shard_map/ppermute | solution.py:397
  25.3 1.8 %collective-permute-done.6.refs_2_.refs_8_ = bf16[912,128]{1,0:T(8,128)(2,1)S(1)} collective-permute-done((bf16[912,128]{1,0:T(8,128)(2,1)S(1)}, bf16[912,128]{1,0:T(8,128)(2,1)S(1)}, u32[]{:S(2)}, u32[]{:S(2)}) %collective-permute-start.6) | collective-permute-done | bytes 233504 | tf_op jit(solution)/shard_map/ppermute | solution.py:398
  27.1 0.3 collective-permute-start.9
  27.4 0.0 collective-permute-done.11.refs_2_
  27.4 0.0 collective-permute-start.12
  27.4 0.0 collective-permute-done.5.refs_1_.refs_7_
  27.4 0.9 %scaled_rows.5.refs_1_ = bf16[256,1792]{1,0:T(8,128)(2,1)S(1)} custom-call(s32[2]{0:T(128)S(1)} %pad_add_fusion.info_ref, bf16[912,128]{1,0:T(8,128)(2,1)S(1)} %collective-permute-done.4.refs_0_.refs_6_, bf16[912,128]{1,0:T(8,128)(2,1)S(1)} %collective-permute-done.5.refs_1_.refs_7_, bf16[912,128]{1,0:T(8,128)(2,1)S(1)} %collective-permute-done.6.refs_2_.refs_8_, ...), custom_call_target="tpu_custom_call" | custom-call | flops 8000000000 | bytes 1000 | tf_op jit(solution)/shard_map/scaled_rows/pallas_call | solution.py:229
  28.3 1.8 %collective-permute-start.13 = (bf16[912,128]{1,0:T(8,128)(2,1)S(1)}, bf16[912,128]{1,0:T(8,128)(2,1)S(1)}, u32[]{:S(2)}, u32[]{:S(2)}) collective-permute-start(bf16[912,128]{1,0:T(8,128)(2,1)S(1)} %collective-permute-done.5.refs_1_.refs_7_), channel_id=1, source_target_pairs={{0,8},{8,16},{16,24},{24,28},{28,20},{20,12},{12,4},{4,0},{1,9},{9... | collective-permute-start | bytes 700424 | tf_op jit(solution)/shard_map/ppermute | solution.py:397
  30.1 0.0 collective-permute-done.10.refs_1_
  30.1 0.3 collective-permute-start.14
  30.3 0.0 collective-permute-done.12.refs_3_
  30.3 3.3 %expert_out_first.1 = (bf16[1024,1024]{1,0:T(8,128)(2,1)S(1)}, bf16[1024,1024]{1,0:T(8,128)(2,1)S(1)}, f32[1024,1024]{1,0:T(8,128)S(1)}) custom-call(s32[2]{0:T(128)S(1)} %pad_add_fusion.info_ref, bf16[1024,256]{1,0:T(8,128)(2,1)S(1)} %get-tuple-element.48.refs_0_, bf16[1024,256]{1,0:T(8,128)(2,1)S(1)} %collective-permute-done.10.refs_1_, ...), custom_call_target="tpu_custom_call" | custom-call | bytes 1000 | tf_op jit(solution)/shard_map/expert_out_first/pallas_call | solution.py:144
  33.7 0.0 collective-permute-done.8.refs_10_.refs_0_
  33.7 0.0 collective-permute-done.9.refs_13_.refs_1_
  33.7 0.8 %scaled_rows.7.refs_0_ = bf16[128,1792]{1,0:T(8,128)(2,1)S(1)} custom-call(s32[2]{0:T(128)S(1)} %pad_add_fusion.info_ref, bf16[912,128]{1,0:T(8,128)(2,1)S(1)} %collective-permute-done.8.refs_10_.refs_0_, bf16[912,128]{1,0:T(8,128)(2,1)S(1)} %collective-permute-done.9.refs_13_.refs_1_), custom_call_target="tpu_custom_call" | custom-call | flops 12000000000 | bytes 1000 | tf_op jit(solution)/shard_map/scaled_rows/pallas_call | solution.py:229
  34.5 1.8 %collective-permute-start.15 = (bf16[912,128]{1,0:T(8,128)(2,1)S(1)}, bf16[912,128]{1,0:T(8,128)(2,1)S(1)}, u32[]{:S(2)}, u32[]{:S(2)}) collective-permute-start(bf16[912,128]{1,0:T(8,128)(2,1)S(1)} %collective-permute-done.8.refs_10_.refs_0_), channel_id=1, source_target_pairs={{0,8},{8,16},{16,24},{24,28},{28,20},{20,12},{12,4},{4,0},{1,9},{9... | collective-permute-start | bytes 700424 | tf_op jit(solution)/shard_map/ppermute | solution.py:397
  36.3 0.3 collective-permute-start.16
  36.6 1.8 %expert_out_rest.1 = (f32[1024,768]{1,0:T(8,128)S(1)}, bf16[640,1792]{1,0:T(8,128)(2,1)}) custom-call(bf16[1024,1024]{1,0:T(8,128)(2,1)S(1)} %get-tuple-element.55.h_ref, bf16[1024,1792]{1,0:T(8,128)(2,1)S(1)} %get-tuple-element.49.refs_4_.w_ref, bf16[384,1792]{1,0:T(8,128)(2,1)S(1)} %scaled_rows.4.refs_0_, bf16[256,1792]{1,0:T(8,128)(2,1)S(1)} %scaled_rows.5.refs_1_), custom_call_target="tpu_custom_call" | custom-call | bytes 1000 | tf_op jit(solution)/shard_map/expert_out_rest/pallas_call | solution.py:180
  38.4 0.0 collective-permute-done.13.refs_0_.refs_11_
  38.4 0.0 collective-permute-done.14.refs_1_.refs_12_
  38.4 0.8 %scaled_rows.6.refs_1_ = bf16[128,1792]{1,0:T(8,128)(2,1)S(1)} custom-call(s32[2]{0:T(128)S(1)} %pad_add_fusion.info_ref, bf16[912,128]{1,0:T(8,128)(2,1)S(1)} %collective-permute-done.13.refs_0_.refs_11_, bf16[912,128]{1,0:T(8,128)(2,1)S(1)} %collective-permute-done.14.refs_1_.refs_12_), custom_call_target="tpu_custom_call" | custom-call | bytes 1000 | tf_op jit(solution)/shard_map/scaled_rows/pallas_call | solution.py:229
  39.2 1.5 %absorb.1 = (f32[8,128]{1,0:T(8,128)S(1)}, f32[8,128]{1,0:T(8,128)S(1)}, f32[16,128]{1,0:T(8,128)S(1)}) custom-call(s32[2]{0:T(128)S(1)} %pad_add_fusion.info_ref, bf16[912,128]{1,0:T(8,128)(2,1)S(1)} %get-tuple-element.42.refs_0_, bf16[912,128]{1,0:T(8,128)(2,1)S(1)} %get-tuple-element.43.refs_1_, bf16[912,128]{1,0:T(8,128)(2,1)S(1)} %collective-permute-done.refs_2_, ...), custom_call_target="tpu_custom_call" | custom-call | bytes 1000 | tf_op jit(solution)/shard_map/absorb/pallas_call | solution.py:264
  40.7 1.4 %collective-permute-done.15.refs_2_.top_ref = bf16[912,128]{1,0:T(8,128)(2,1)S(1)} collective-permute-done((bf16[912,128]{1,0:T(8,128)(2,1)S(1)}, bf16[912,128]{1,0:T(8,128)(2,1)S(1)}, u32[]{:S(2)}, u32[]{:S(2)}) %collective-permute-start.15) | collective-permute-done | bytes 233504 | tf_op jit(solution)/shard_map/ppermute | solution.py:397
  42.1 1.5 %collective-permute-done.16.refs_3_.bottom_ref = bf16[912,128]{1,0:T(8,128)(2,1)S(1)} collective-permute-done((bf16[912,128]{1,0:T(8,128)(2,1)S(1)}, bf16[912,128]{1,0:T(8,128)(2,1)S(1)}, u32[]{:S(2)}, u32[]{:S(2)}) %collective-permute-start.16) | collective-permute-done | bytes 233504 | tf_op jit(solution)/shard_map/ppermute | solution.py:398
  43.5 0.9 %absorb_last.1 = f32[8,4,128]{2,1,0:T(4,128)} custom-call(bf16[912,128]{1,0:T(8,128)(2,1)S(1)} %collective-permute-done.15.refs_2_.top_ref, bf16[912,128]{1,0:T(8,128)(2,1)S(1)} %collective-permute-done.16.refs_3_.bottom_ref, f32[1024,1024]{1,0:T(8,128)S(1)} %get-tuple-element.67.refs_14_.eo_ref, f32[1024,768]{1,0:T(8,128)S(1)} %get-tuple-element.68.refs_15_.rest_ref, ...), custom_call_target="tpu_custom_call" | custom-call | bytes 1000 | tf_op jit(solution)/shard_map/absorb_last/pallas_call | solution.py:290
  44.4 4.8 %all-to-all-start = ((f32[32,1,128]{2,1,0:T(1,128)}), f32[32,1,128]{2,1,0:T(1,128)S(1)}, u32[]{:S(2)}, u32[]{:S(2)}) async-start(f32[32,1,128]{2,1,0:T(1,128)} %bitcast.9), calls=%async_computation | async-start | bytes 32768 | tf_op jit(solution)/shard_map/all_to_all | solution.py:434
  49.3 0.0 copy-start
  49.3 6.7 %weight_grad.1 = bf16[1024,1792]{1,0:T(8,128)(2,1)} custom-call(f32[16,128]{1,0:T(8,128)S(1)} %get-tuple-element.69.own_ref, bf16[640,1792]{1,0:T(8,128)(2,1)} %get-tuple-element.70.early_ref, bf16[128,1792]{1,0:T(8,128)(2,1)S(1)} %scaled_rows.7.refs_0_, bf16[128,1792]{1,0:T(8,128)(2,1)S(1)} %scaled_rows.6.refs_1_, ...), custom_call_target="tpu_custom_call" | custom-call | bytes 1000 | tf_op jit(solution)/shard_map/weight_grad/pallas_call | solution.py:338
  56.0 0.4 all-to-all-done
  56.4 0.0 copy-done
  56.4 0.6 %pick_gate_grad.1 = f32[8,128]{1,0:T(8,128)} custom-call(f32[8,4,128]{2,1,0:T(4,128)S(1)} %bitcast.13, s32[8,128]{1,0:T(8,128)S(1)} %bitcast.15), custom_call_target="tpu_custom_call" | custom-call | tf_op jit(solution)/shard_map/pick_gate_grad/pallas_call | solution.py:367
Async XLA Ops:
  1.8 9.7 %collective-permute-start = (bf16[912,128]{1,0:T(8,128)(2,1)S(1)}, bf16[912,128]{1,0:T(8,128)(2,1)S(1)}, u32[]{:S(2)}, u32[]{:S(2)}) collective-permute-start(bf16[912,128]{1,0:T(8,128)(2,1)S(1)} %get-tuple-element.42.refs_0_), channel_id=1, source_target_pairs={{0,8},{8,16},{16,24},{24,28},{28,20},{20,12},{12,4},{4,0},{1,9},{9... | collective-permute-start | bytes 700424 | tf_op jit(solution)/shard_map/ppermute | solution.py:397
  4.9 8.6 %collective-permute-start.1 = (bf16[912,128]{1,0:T(8,128)(2,1)S(1)}, bf16[912,128]{1,0:T(8,128)(2,1)S(1)}, u32[]{:S(2)}, u32[]{:S(2)}) collective-permute-start(bf16[912,128]{1,0:T(8,128)(2,1)S(1)} %get-tuple-element.43.refs_1_), channel_id=1, source_target_pairs={{8,0},{16,8},{24,16},{28,24},{20,28},{12,20},{4,12},{0,4},{9,1},{1... | collective-permute-start | bytes 700424 | tf_op jit(solution)/shard_map/ppermute | solution.py:398
  4.9 13.6 %collective-permute-start.3 = (bf16[912,128]{1,0:T(8,128)(2,1)S(1)}, bf16[912,128]{1,0:T(8,128)(2,1)S(1)}, u32[]{:S(2)}, u32[]{:S(2)}) collective-permute-start(bf16[912,128]{1,0:T(8,128)(2,1)S(1)} %get-tuple-element.42.refs_0_), channel_id=1, source_target_pairs={{8,0},{16,8},{24,16},{28,24},{20,28},{12,20},{4,12},{0,4},{9,1},{1... | collective-permute-start | bytes 700424 | tf_op jit(solution)/shard_map/ppermute | solution.py:398
  6.9 11.7 %collective-permute-start.2 = (bf16[912,128]{1,0:T(8,128)(2,1)S(1)}, bf16[912,128]{1,0:T(8,128)(2,1)S(1)}, u32[]{:S(2)}, u32[]{:S(2)}) collective-permute-start(bf16[912,128]{1,0:T(8,128)(2,1)S(1)} %get-tuple-element.43.refs_1_), channel_id=1, source_target_pairs={{0,8},{8,16},{16,24},{24,28},{28,20},{20,12},{12,4},{4,0},{1,9},{9... | collective-permute-start | bytes 700424 | tf_op jit(solution)/shard_map/ppermute | solution.py:397
  9.5 17.8 %collective-permute-start.11 = (bf16[1024,256]{1,0:T(8,128)(2,1)S(1)}, bf16[1024,256]{1,0:T(8,128)(2,1)S(1)}, u32[]{:S(2)}, u32[]{:S(2)}) collective-permute-start(bf16[1024,256]{1,0:T(8,128)(2,1)S(1)} %get-tuple-element.48.refs_0_), channel_id=1, source_target_pairs={{0,2},{1,3},{2,0},{3,1},{4,6},{5,7},{6,4},{7,5},{8,10},{9,11},{10,... | collective-permute-start | bytes 1572872 | tf_op jit(solution)/shard_map/ppermute | solution.py:406
  13.5 8.6 %collective-permute-start.4 = (bf16[912,128]{1,0:T(8,128)(2,1)S(1)}, bf16[912,128]{1,0:T(8,128)(2,1)S(1)}, u32[]{:S(2)}, u32[]{:S(2)}) collective-permute-start(bf16[912,128]{1,0:T(8,128)(2,1)S(1)} %collective-permute-done.refs_2_), channel_id=1, source_target_pairs={{0,8},{8,16},{16,24},{24,28},{28,20},{20,12},{12,4},{4,0},{1,9},{9... | collective-permute-start | bytes 700424 | tf_op jit(solution)/shard_map/ppermute | solution.py:397
  15.1 8.6 %collective-permute-start.7 = (bf16[912,128]{1,0:T(8,128)(2,1)S(1)}, bf16[912,128]{1,0:T(8,128)(2,1)S(1)}, u32[]{:S(2)}, u32[]{:S(2)}) collective-permute-start(bf16[912,128]{1,0:T(8,128)(2,1)S(1)} %collective-permute-done.1.refs_5_), channel_id=1, source_target_pairs={{8,0},{16,8},{24,16},{28,24},{20,28},{12,20},{4,12},{0,4},{9,1},{1... | collective-permute-start | bytes 700424 | tf_op jit(solution)/shard_map/ppermute | solution.py:398
  18.5 8.5 %collective-permute-start.6 = (bf16[912,128]{1,0:T(8,128)(2,1)S(1)}, bf16[912,128]{1,0:T(8,128)(2,1)S(1)}, u32[]{:S(2)}, u32[]{:S(2)}) collective-permute-start(bf16[912,128]{1,0:T(8,128)(2,1)S(1)} %collective-permute-done.3.refs_4_), channel_id=1, source_target_pairs={{8,0},{16,8},{24,16},{28,24},{20,28},{12,20},{4,12},{0,4},{9,1},{1... | collective-permute-start | bytes 700424 | tf_op jit(solution)/shard_map/ppermute | solution.py:398
  18.5 8.8 %collective-permute-start.5 = (bf16[912,128]{1,0:T(8,128)(2,1)S(1)}, bf16[912,128]{1,0:T(8,128)(2,1)S(1)}, u32[]{:S(2)}, u32[]{:S(2)}) collective-permute-start(bf16[912,128]{1,0:T(8,128)(2,1)S(1)} %collective-permute-done.2.refs_3_), channel_id=1, source_target_pairs={{0,8},{8,16},{16,24},{24,28},{28,20},{20,12},{12,4},{4,0},{1,9},{9... | collective-permute-start | bytes 700424 | tf_op jit(solution)/shard_map/ppermute | solution.py:397
  22.2 7.9 %collective-permute-start.10 = (bf16[1024,256]{1,0:T(8,128)(2,1)S(1)}, bf16[1024,256]{1,0:T(8,128)(2,1)S(1)}, u32[]{:S(2)}, u32[]{:S(2)}) collective-permute-start(bf16[1024,256]{1,0:T(8,128)(2,1)S(1)} %get-tuple-element.48.refs_0_), channel_id=1, source_target_pairs={{0,1},{1,0},{2,3},{3,2},{4,5},{5,4},{6,7},{7,6},{8,9},{9,8},{10,11... | collective-permute-start | bytes 1572872 | tf_op jit(solution)/shard_map/ppermute | solution.py:407
  23.7 9.9 %collective-permute-start.8 = (bf16[912,128]{1,0:T(8,128)(2,1)S(1)}, bf16[912,128]{1,0:T(8,128)(2,1)S(1)}, u32[]{:S(2)}, u32[]{:S(2)}) collective-permute-start(bf16[912,128]{1,0:T(8,128)(2,1)S(1)} %collective-permute-done.4.refs_0_.refs_6_), channel_id=1, source_target_pairs={{0,8},{8,16},{16,24},{24,28},{28,20},{20,12},{12,4},{4,0},{1,9},{9... | collective-permute-start | bytes 700424 | tf_op jit(solution)/shard_map/ppermute | solution.py:397
  27.1 6.6 %collective-permute-start.9 = (bf16[912,128]{1,0:T(8,128)(2,1)S(1)}, bf16[912,128]{1,0:T(8,128)(2,1)S(1)}, u32[]{:S(2)}, u32[]{:S(2)}) collective-permute-start(bf16[912,128]{1,0:T(8,128)(2,1)S(1)} %collective-permute-done.7.refs_3_.refs_9_), channel_id=1, source_target_pairs={{8,0},{16,8},{24,16},{28,24},{20,28},{12,20},{4,12},{0,4},{9,1},{1... | collective-permute-start | bytes 700424 | tf_op jit(solution)/shard_map/ppermute | solution.py:398
  27.4 3.0 %collective-permute-start.12 = (bf16[1024,256]{1,0:T(8,128)(2,1)S(1)}, bf16[1024,256]{1,0:T(8,128)(2,1)S(1)}, u32[]{:S(2)}, u32[]{:S(2)}) collective-permute-start(bf16[1024,256]{1,0:T(8,128)(2,1)S(1)} %collective-permute-done.11.refs_2_), channel_id=1, source_target_pairs={{0,1},{1,0},{2,3},{3,2},{4,5},{5,4},{6,7},{7,6},{8,9},{9,8},{10,11... | collective-permute-start | bytes 1572872 | tf_op jit(solution)/shard_map/ppermute | solution.py:407
  28.3 10.1 %collective-permute-start.13 = (bf16[912,128]{1,0:T(8,128)(2,1)S(1)}, bf16[912,128]{1,0:T(8,128)(2,1)S(1)}, u32[]{:S(2)}, u32[]{:S(2)}) collective-permute-start(bf16[912,128]{1,0:T(8,128)(2,1)S(1)} %collective-permute-done.5.refs_1_.refs_7_), channel_id=1, source_target_pairs={{0,8},{8,16},{16,24},{24,28},{28,20},{20,12},{12,4},{4,0},{1,9},{9... | collective-permute-start | bytes 700424 | tf_op jit(solution)/shard_map/ppermute | solution.py:397
  30.1 8.3 %collective-permute-start.14 = (bf16[912,128]{1,0:T(8,128)(2,1)S(1)}, bf16[912,128]{1,0:T(8,128)(2,1)S(1)}, u32[]{:S(2)}, u32[]{:S(2)}) collective-permute-start(bf16[912,128]{1,0:T(8,128)(2,1)S(1)} %collective-permute-done.6.refs_2_.refs_8_), channel_id=1, source_target_pairs={{8,0},{16,8},{24,16},{28,24},{20,28},{12,20},{4,12},{0,4},{9,1},{1... | collective-permute-start | bytes 700424 | tf_op jit(solution)/shard_map/ppermute | solution.py:398
  34.5 7.6 %collective-permute-start.15 = (bf16[912,128]{1,0:T(8,128)(2,1)S(1)}, bf16[912,128]{1,0:T(8,128)(2,1)S(1)}, u32[]{:S(2)}, u32[]{:S(2)}) collective-permute-start(bf16[912,128]{1,0:T(8,128)(2,1)S(1)} %collective-permute-done.8.refs_10_.refs_0_), channel_id=1, source_target_pairs={{0,8},{8,16},{16,24},{24,28},{28,20},{20,12},{12,4},{4,0},{1,9},{9... | collective-permute-start | bytes 700424 | tf_op jit(solution)/shard_map/ppermute | solution.py:397
  36.3 7.2 %collective-permute-start.16 = (bf16[912,128]{1,0:T(8,128)(2,1)S(1)}, bf16[912,128]{1,0:T(8,128)(2,1)S(1)}, u32[]{:S(2)}, u32[]{:S(2)}) collective-permute-start(bf16[912,128]{1,0:T(8,128)(2,1)S(1)} %collective-permute-done.9.refs_13_.refs_1_), channel_id=1, source_target_pairs={{8,0},{16,8},{24,16},{28,24},{20,28},{12,20},{4,12},{0,4},{9,1},{1... | collective-permute-start | bytes 700424 | tf_op jit(solution)/shard_map/ppermute | solution.py:398
  44.4 12.0 %all-to-all-start = ((f32[32,1,128]{2,1,0:T(1,128)}), f32[32,1,128]{2,1,0:T(1,128)S(1)}, u32[]{:S(2)}, u32[]{:S(2)}) async-start(f32[32,1,128]{2,1,0:T(1,128)} %bitcast.9), calls=%async_computation | async-start | bytes 32768 | tf_op jit(solution)/shard_map/all_to_all | solution.py:434
  49.3 7.2 %copy-start = (s32[128,8]{0,1:T(8,128)S(1)}, s32[128,8]{0,1:T(8,128)}, u32[]{:S(2)}) copy-start(s32[128,8]{0,1:T(8,128)} %param.8) | copy-start | bytes 12292

commit v7 on v5

--- a/solution.py
+++ b/solution.py
@@ -298,7 +298,7 @@
     )(*chunks, *expert_out, sums, mask)
 
 
-def weight_grad(own, early, early_places, late, late_places, last_chunks, hidden_t):
+def weight_grad(own, early, early_places, late, late_places, chunks, chunk_places, hidden_t):
     units, slots = hidden_t.shape
     feats = late[0].shape[1]
     half = late[0].shape[0] // len(late_places[0])
@@ -307,7 +307,8 @@
 
     def body(own_ref, early_ref, *refs):
         late_refs, refs = refs[: len(late)], refs[len(late) :]
-        top_ref, bottom_ref, ht_ref, out_ref, rows_scr, held, in_sems, out_sems = refs
+        chunk_refs, refs = refs[: len(chunks)], refs[len(chunks) :]
+        ht_ref, out_ref, rows_scr, held, in_sems, out_sems = refs
         copies = [
             pltpu.make_async_copy(
                 early_ref.at[pl.ds(i * half, half)], rows_scr.at[pl.ds(place, half)], in_sems.at[i]
@@ -319,10 +320,10 @@
         for ref, at in zip(late_refs, late_places):
             for i, place in enumerate(at):
                 rows_scr[place : place + half, :] = ref[i * half : (i + 1) * half, :]
-        for c, ref in enumerate((top_ref, bottom_ref)):
+        for ref, (place, lower) in zip(chunk_refs, chunk_places):
             by = ref[ref.shape[0] - 16 :, :].astype(F32)
-            gate = column(jnp.sum(by * own_ref[...], axis=0, keepdims=True))[c * half : (c + 1) * half]
-            put_scaled(ref, rows_scr, slots - (2 - c) * half, gate, half)
+            gate = column(jnp.sum(by * own_ref[...], axis=0, keepdims=True))[lower * half : (lower + 1) * half]
+            put_scaled(ref, rows_scr, place, gate, half)
         for copy in copies:
             copy.wait()
         copies = []
@@ -337,7 +338,7 @@
 
     return pl.pallas_call(
         body,
-        in_specs=[vmem_spec(), any_spec()] + [vmem_spec()] * (3 + len(late)),
+        in_specs=[vmem_spec(), any_spec()] + [vmem_spec()] * (1 + len(late) + len(chunks)),
         out_specs=any_spec(),
         out_shape=jax.ShapeDtypeStruct((units, feats), BF16),
         scratch_shapes=[
@@ -349,7 +350,7 @@
         compiler_params=params(12),
         cost_estimate=declared(),
         name="weight_grad",
-    )(own, in_hbm(early), *late, *last_chunks, hidden_t)
+    )(own, in_hbm(early), *late, *chunks, hidden_t)
 
 
 def pick(returned, routes_t):
@@ -427,16 +428,15 @@
     rest, early = expert_out_rest(hidden, weight, [scaled_a, scaled_b], cut)
     expert_out = [start, rest]
     third, early = barrier((third, early))
-    scaled_d = scale([third[1], third[2]], [1, 0])
-    third, scaled_d = barrier((third, scaled_d))
     sums, mask, own = absorb(info, [top, bottom] + first + second + third, expert_out, tokens, steps)
     outgoing = absorb_last([up[0], down[0]], expert_out, sums, mask, groups)
     returned = lax.all_to_all(
         outgoing.reshape(experts * groups, tokens), ("ep", "et"), split_axis=0, concat_axis=0, tiled=True
     )
-    late_places = [[10 * half, 13 * half], [11 * half, 12 * half]]
+    chunks = [third[1], third[2], up[0], down[0]]
+    chunk_places = [(11 * half, 1), (12 * half, 0), (14 * half, 0), (15 * half, 1)]
     grad = weight_grad(
-        own, early, [i * half for i in range(10)], [scaled_c, scaled_d], late_places, [up[0], down[0]], hidden_t
+        own, early, [i * half for i in range(10)], [scaled_c], [[10 * half, 13 * half]], chunks, chunk_places, hidden_t
     )
     d_gate = pick(returned.reshape(experts, groups, tokens), routes.T).T
     return grad[None], d_gate

time: 57.3 us -> 57.3 us (level)
  Pallas kernels: 22 us -> 21.2 us
  waiting for transfers between devices: 8.72 us -> 9.51 us
    ppermute x7, waiting for transfers between devices: 4.6 us -> 5.39 us  [hop(): up[c] = lax.ppermute(up[c], 'ep', forth)]
    pallas_call x4 -> x3, Pallas kernels: 3.45 us -> 2.67 us  [scaled_rows(): pl.pallas_call(body, in_specs=[smem_spec()] + [vmem_spec()] * count, out_...]
  transfers between devices with their start and end apart: 18 -> 18, of which waited for: 8 -> 8; matrix products, arithmetic and copies ran while one was open for 0% -> 0% of each run, Pallas kernels for 34% -> 33%
where the time goes in v7:
time: 57.3 us; the launch traced here: 57.1 us
  starting transfers between devices  25.5 us (45%)
  Pallas kernels  21.2 us (37%)
  waiting for transfers between devices  9.51 us (17%)
  between operations  0.76 us (1%)
    ppermute x7, starting transfers between devices, hop(): up[c] = lax.ppermute(up[c], 'ep', forth)  11.9 us
    pallas_call x1, Pallas kernels, weight_grad(): pl.pallas_call(body, in_specs=[vmem_spec(), any_spec()] + [vmem_spec()] *...  6.71 us
    all_to_all x1, starting transfers between devices, dense(): lax.all_to_all(outgoing.reshape(experts * groups, tokens), ('ep', 'et'),...  6.2 us
    ppermute x7, waiting for transfers between devices, hop(): up[c] = lax.ppermute(up[c], 'ep', forth)  5.39 us
    ppermute x7, starting transfers between devices, hop(): down[c] = lax.ppermute(down[c], 'ep', back)  5.35 us
    ppermute x7, waiting for transfers between devices, hop(): down[c] = lax.ppermute(down[c], 'ep', back)  3.69 us
    pallas_call x1, Pallas kernels, assemble(): pl.pallas_call(body, in_specs=[smem_spec()] + [vmem_spec()] * (groups + 1...  2.76 us
    pallas_call x3, Pallas kernels, scaled_rows(): pl.pallas_call(body, in_specs=[smem_spec()] + [vmem_spec()] * count, out_...  2.67 us
  transfers between devices with their start and end apart: 18, of which 8 were waited for; matrix products, arithmetic and copies ran while one was open for 0% of the time, Pallas kernels for 33%

profile of v7, /device:TPU:0, one launch (start us, length us, event | category | flops | bytes accessed | tf_op | source)
XLA Modules:
  0.0 57.1 jit_solution(1578912219107316698)
XLA Ops:
  0.6 0.1 pad_add_fusion.info_ref
  0.7 1.1 %chunks.1 = (bf16[912,128]{1,0:T(8,128)(2,1)S(1)}, bf16[912,128]{1,0:T(8,128)(2,1)S(1)}) custom-call(bf16[128,1792]{1,0:T(8,128)(2,1)} %rows_ref, bf16[8,128]{1,0:T(8,128)(2,1)} %bitcast.21, s32[8,128]{1,0:T(8,128)} %bitcast.14), custom_call_target="tpu_custom_call" | custom-call | bytes 1000 | tf_op jit(solution)/shard_map/chunks/pallas_call | solution.py:69
  1.8 3.1 %collective-permute-start = (bf16[912,128]{1,0:T(8,128)(2,1)S(1)}, bf16[912,128]{1,0:T(8,128)(2,1)S(1)}, u32[]{:S(2)}, u32[]{:S(2)}) collective-permute-start(bf16[912,128]{1,0:T(8,128)(2,1)S(1)} %get-tuple-element.37.refs_0_), channel_id=1, source_target_pairs={{0,8},{8,16},{16,24},{24,28},{28,20},{20,12},{12,4},{4,0},{1,9},{9... | collective-permute-start | bytes 700424 | tf_op jit(solution)/shard_map/ppermute | solution.py:398
  4.9 0.0 collective-permute-start.1
  4.9 2.0 %collective-permute-start.2 = (bf16[912,128]{1,0:T(8,128)(2,1)S(1)}, bf16[912,128]{1,0:T(8,128)(2,1)S(1)}, u32[]{:S(2)}, u32[]{:S(2)}) collective-permute-start(bf16[912,128]{1,0:T(8,128)(2,1)S(1)} %get-tuple-element.38.refs_1_), channel_id=1, source_target_pairs={{0,8},{8,16},{16,24},{24,28},{28,20},{20,12},{12,4},{4,0},{1,9},{9... | collective-permute-start | bytes 700424 | tf_op jit(solution)/shard_map/ppermute | solution.py:398
  6.9 0.0 collective-permute-start.3
  6.9 2.5 %hidden.1 = (bf16[1024,256]{1,0:T(8,128)(2,1)S(1)}, bf16[1024,1792]{1,0:T(8,128)(2,1)S(1)}) custom-call(bf16[1024,256]{1,0:T(8,128)(2,1)} %bitcast.18, bf16[1024,256]{1,0:T(8,128)(2,1)} %bitcast.19, bf16[1024,1792]{1,0:T(8,128)(2,1)} %bitcast.16), custom_call_target="tpu_custom_call" | custom-call | bytes 1000 | tf_op jit(solution)/shard_map/hidden/pallas_call | solution.py:108
  9.5 2.0 %collective-permute-start.11 = (bf16[1024,256]{1,0:T(8,128)(2,1)S(1)}, bf16[1024,256]{1,0:T(8,128)(2,1)S(1)}, u32[]{:S(2)}, u32[]{:S(2)}) collective-permute-start(bf16[1024,256]{1,0:T(8,128)(2,1)S(1)} %get-tuple-element.43.refs_0_), channel_id=1, source_target_pairs={{0,2},{1,3},{2,0},{3,1},{4,6},{5,7},{6,4},{7,5},{8,10},{9,11},{10,... | collective-permute-start | bytes 1572872 | tf_op jit(solution)/shard_map/ppermute | solution.py:407
  11.5 0.0 collective-permute-done.refs_2_
  11.5 2.0 %collective-permute-done.1.refs_5_ = bf16[912,128]{1,0:T(8,128)(2,1)S(1)} collective-permute-done((bf16[912,128]{1,0:T(8,128)(2,1)S(1)}, bf16[912,128]{1,0:T(8,128)(2,1)S(1)}, u32[]{:S(2)}, u32[]{:S(2)}) %collective-permute-start.1) | collective-permute-done | bytes 233504 | tf_op jit(solution)/shard_map/ppermute | solution.py:399
  13.5 1.6 %collective-permute-start.4 = (bf16[912,128]{1,0:T(8,128)(2,1)S(1)}, bf16[912,128]{1,0:T(8,128)(2,1)S(1)}, u32[]{:S(2)}, u32[]{:S(2)}) collective-permute-start(bf16[912,128]{1,0:T(8,128)(2,1)S(1)} %collective-permute-done.refs_2_), channel_id=1, source_target_pairs={{0,8},{8,16},{16,24},{24,28},{28,20},{20,12},{12,4},{4,0},{1,9},{9... | collective-permute-start | bytes 700424 | tf_op jit(solution)/shard_map/ppermute | solution.py:398
  15.1 0.4 collective-permute-start.7
  15.6 0.8 %collective-permute-done.2.refs_3_ = bf16[912,128]{1,0:T(8,128)(2,1)S(1)} collective-permute-done((bf16[912,128]{1,0:T(8,128)(2,1)S(1)}, bf16[912,128]{1,0:T(8,128)(2,1)S(1)}, u32[]{:S(2)}, u32[]{:S(2)}) %collective-permute-start.2) | collective-permute-done | bytes 233504 | tf_op jit(solution)/shard_map/ppermute | solution.py:398
  16.3 2.1 %collective-permute-start.5 = (bf16[912,128]{1,0:T(8,128)(2,1)S(1)}, bf16[912,128]{1,0:T(8,128)(2,1)S(1)}, u32[]{:S(2)}, u32[]{:S(2)}) collective-permute-start(bf16[912,128]{1,0:T(8,128)(2,1)S(1)} %collective-permute-done.2.refs_3_), channel_id=1, source_target_pairs={{0,8},{8,16},{16,24},{24,28},{28,20},{20,12},{12,4},{4,0},{1,9},{9... | collective-permute-start | bytes 700424 | tf_op jit(solution)/shard_map/ppermute | solution.py:398
  18.5 0.0 collective-permute-done.3.refs_4_
  18.5 0.0 collective-permute-start.6
  18.5 1.0 %scaled_rows.3.refs_0_ = bf16[384,1792]{1,0:T(8,128)(2,1)S(1)} custom-call(s32[2]{0:T(128)S(1)} %pad_add_fusion.info_ref, bf16[912,128]{1,0:T(8,128)(2,1)S(1)} %get-tuple-element.37.refs_0_, bf16[912,128]{1,0:T(8,128)(2,1)S(1)} %get-tuple-element.38.refs_1_, bf16[912,128]{1,0:T(8,128)(2,1)S(1)} %collective-permute-done.refs_2_, ...), custom_call_target="tpu_custom_call" | custom-call | flops 4000000000 | bytes 1000 | tf_op jit(solution)/shard_map/scaled_rows/pallas_call | solution.py:229
  19.6 2.6 %collective-permute-done.4.refs_0_.refs_6_ = bf16[912,128]{1,0:T(8,128)(2,1)S(1)} collective-permute-done((bf16[912,128]{1,0:T(8,128)(2,1)S(1)}, bf16[912,128]{1,0:T(8,128)(2,1)S(1)}, u32[]{:S(2)}, u32[]{:S(2)}) %collective-permute-start.4) | collective-permute-done | bytes 233504 | tf_op jit(solution)/shard_map/ppermute | solution.py:398
  22.2 0.0 collective-permute-start.10
  22.2 1.6 %collective-permute-done.7.refs_3_.refs_9_ = bf16[912,128]{1,0:T(8,128)(2,1)S(1)} collective-permute-done((bf16[912,128]{1,0:T(8,128)(2,1)S(1)}, bf16[912,128]{1,0:T(8,128)(2,1)S(1)}, u32[]{:S(2)}, u32[]{:S(2)}) %collective-permute-start.7) | collective-permute-done | bytes 233504 | tf_op jit(solution)/shard_map/ppermute | solution.py:399
  23.7 1.6 %collective-permute-start.8 = (bf16[912,128]{1,0:T(8,128)(2,1)S(1)}, bf16[912,128]{1,0:T(8,128)(2,1)S(1)}, u32[]{:S(2)}, u32[]{:S(2)}) collective-permute-start(bf16[912,128]{1,0:T(8,128)(2,1)S(1)} %collective-permute-done.4.refs_0_.refs_6_), channel_id=1, source_target_pairs={{0,8},{8,16},{16,24},{24,28},{28,20},{20,12},{12,4},{4,0},{1,9},{9... | collective-permute-start | bytes 700424 | tf_op jit(solution)/shard_map/ppermute | solution.py:398
  25.3 0.4 collective-permute-done.5.refs_1_.refs_7_
  25.7 2.2 %collective-permute-start.9 = (bf16[912,128]{1,0:T(8,128)(2,1)S(1)}, bf16[912,128]{1,0:T(8,128)(2,1)S(1)}, u32[]{:S(2)}, u32[]{:S(2)}) collective-permute-start(bf16[912,128]{1,0:T(8,128)(2,1)S(1)} %collective-permute-done.7.refs_3_.refs_9_), channel_id=1, source_target_pairs={{8,0},{16,8},{24,16},{28,24},{20,28},{12,20},{4,12},{0,4},{9,1},{1... | collective-permute-start | bytes 700424 | tf_op jit(solution)/shard_map/ppermute | solution.py:399
  27.9 0.0 collective-permute-done.11.refs_2_
  27.9 0.0 collective-permute-start.12
  28.0 0.0 collective-permute-done.6.refs_2_.refs_8_
  28.0 0.9 %scaled_rows.4.refs_1_ = bf16[256,1792]{1,0:T(8,128)(2,1)S(1)} custom-call(s32[2]{0:T(128)S(1)} %pad_add_fusion.info_ref, bf16[912,128]{1,0:T(8,128)(2,1)S(1)} %collective-permute-done.4.refs_0_.refs_6_, bf16[912,128]{1,0:T(8,128)(2,1)S(1)} %collective-permute-done.5.refs_1_.refs_7_, bf16[912,128]{1,0:T(8,128)(2,1)S(1)} %collective-permute-done.6.refs_2_.refs_8_, ...), custom_call_target="tpu_custom_call" | custom-call | flops 8000000000 | bytes 1000 | tf_op jit(solution)/shard_map/scaled_rows/pallas_call | solution.py:229
  28.9 0.7 %collective-permute-start.13 = (bf16[912,128]{1,0:T(8,128)(2,1)S(1)}, bf16[912,128]{1,0:T(8,128)(2,1)S(1)}, u32[]{:S(2)}, u32[]{:S(2)}) collective-permute-start(bf16[912,128]{1,0:T(8,128)(2,1)S(1)} %collective-permute-done.5.refs_1_.refs_7_), channel_id=1, source_target_pairs={{0,8},{8,16},{16,24},{24,28},{28,20},{20,12},{12,4},{4,0},{1,9},{9... | collective-permute-start | bytes 700424 | tf_op jit(solution)/shard_map/ppermute | solution.py:398
  29.6 0.0 collective-permute-done.10.refs_1_
  29.6 1.3 %collective-permute-start.14 = (bf16[912,128]{1,0:T(8,128)(2,1)S(1)}, bf16[912,128]{1,0:T(8,128)(2,1)S(1)}, u32[]{:S(2)}, u32[]{:S(2)}) collective-permute-start(bf16[912,128]{1,0:T(8,128)(2,1)S(1)} %collective-permute-done.6.refs_2_.refs_8_), channel_id=1, source_target_pairs={{8,0},{16,8},{24,16},{28,24},{20,28},{12,20},{4,12},{0,4},{9,1},{1... | collective-permute-start | bytes 700424 | tf_op jit(solution)/shard_map/ppermute | solution.py:399
  30.9 0.0 collective-permute-done.12.refs_3_
  30.9 2.8 %expert_out_first.1 = (bf16[1024,1024]{1,0:T(8,128)(2,1)S(1)}, bf16[1024,1024]{1,0:T(8,128)(2,1)S(1)}, f32[1024,768]{1,0:T(8,128)S(1)}) custom-call(s32[2]{0:T(128)S(1)} %pad_add_fusion.info_ref, bf16[1024,256]{1,0:T(8,128)(2,1)S(1)} %get-tuple-element.43.refs_0_, bf16[1024,256]{1,0:T(8,128)(2,1)S(1)} %collective-permute-done.10.refs_1_, ...), custom_call_target="tpu_custom_call" | custom-call | bytes 1000 | tf_op jit(solution)/shard_map/expert_out_first/pallas_call | solution.py:144
  33.7 0.0 collective-permute-done.8.refs_10_.refs_0_
  33.7 0.0 collective-permute-done.9.refs_13_.refs_1_
  33.7 0.8 %scaled_rows.5.refs_0_ = bf16[128,1792]{1,0:T(8,128)(2,1)S(1)} custom-call(s32[2]{0:T(128)S(1)} %pad_add_fusion.info_ref, bf16[912,128]{1,0:T(8,128)(2,1)S(1)} %collective-permute-done.8.refs_10_.refs_0_, bf16[912,128]{1,0:T(8,128)(2,1)S(1)} %collective-permute-done.9.refs_13_.refs_1_), custom_call_target="tpu_custom_call" | custom-call | flops 12000000000 | bytes 1000 | tf_op jit(solution)/shard_map/scaled_rows/pallas_call | solution.py:229
  34.5 0.8 %collective-permute-start.15 = (bf16[912,128]{1,0:T(8,128)(2,1)S(1)}, bf16[912,128]{1,0:T(8,128)(2,1)S(1)}, u32[]{:S(2)}, u32[]{:S(2)}) collective-permute-start(bf16[912,128]{1,0:T(8,128)(2,1)S(1)} %collective-permute-done.8.refs_10_.refs_0_), channel_id=1, source_target_pairs={{0,8},{8,16},{16,24},{24,28},{28,20},{20,12},{12,4},{4,0},{1,9},{9... | collective-permute-start | bytes 700424 | tf_op jit(solution)/shard_map/ppermute | solution.py:398
  35.3 1.3 %collective-permute-start.16 = (bf16[912,128]{1,0:T(8,128)(2,1)S(1)}, bf16[912,128]{1,0:T(8,128)(2,1)S(1)}, u32[]{:S(2)}, u32[]{:S(2)}) collective-permute-start(bf16[912,128]{1,0:T(8,128)(2,1)S(1)} %collective-permute-done.9.refs_13_.refs_1_), channel_id=1, source_target_pairs={{8,0},{16,8},{24,16},{28,24},{20,28},{12,20},{4,12},{0,4},{9,1},{1... | collective-permute-start | bytes 700424 | tf_op jit(solution)/shard_map/ppermute | solution.py:399
  36.6 2.4 %expert_out_rest.1 = (f32[1024,1024]{1,0:T(8,128)S(1)}, bf16[640,1792]{1,0:T(8,128)(2,1)}) custom-call(bf16[1024,1024]{1,0:T(8,128)(2,1)S(1)} %get-tuple-element.50.h_ref, bf16[1024,1792]{1,0:T(8,128)(2,1)S(1)} %get-tuple-element.44.refs_4_.w_ref, bf16[384,1792]{1,0:T(8,128)(2,1)S(1)} %scaled_rows.3.refs_0_, bf16[256,1792]{1,0:T(8,128)(2,1)S(1)} %scaled_rows.4.refs_1_), custom_call_target="tpu_custom_call" | custom-call | bytes 1000 | tf_op jit(solution)/shard_map/expert_out_rest/pallas_call | solution.py:180
  39.0 0.0 collective-permute-done.13.refs_11_.refs_1_
  39.0 0.0 collective-permute-done.14.refs_12_.refs_2_
  39.0 1.5 %absorb.1 = (f32[8,128]{1,0:T(8,128)S(1)}, f32[8,128]{1,0:T(8,128)S(1)}, f32[16,128]{1,0:T(8,128)S(1)}) custom-call(s32[2]{0:T(128)S(1)} %pad_add_fusion.info_ref, bf16[912,128]{1,0:T(8,128)(2,1)S(1)} %get-tuple-element.37.refs_0_, bf16[912,128]{1,0:T(8,128)(2,1)S(1)} %get-tuple-element.38.refs_1_, bf16[912,128]{1,0:T(8,128)(2,1)S(1)} %collective-permute-done.refs_2_, ...), custom_call_target="tpu_custom_call" | custom-call | bytes 1000 | tf_op jit(solution)/shard_map/absorb/pallas_call | solution.py:264
  40.5 1.6 %collective-permute-done.15.refs_3_.top_ref = bf16[912,128]{1,0:T(8,128)(2,1)S(1)} collective-permute-done((bf16[912,128]{1,0:T(8,128)(2,1)S(1)}, bf16[912,128]{1,0:T(8,128)(2,1)S(1)}, u32[]{:S(2)}, u32[]{:S(2)}) %collective-permute-start.15) | collective-permute-done | bytes 233504 | tf_op jit(solution)/shard_map/ppermute | solution.py:398
  42.1 0.1 collective-permute-done.16.refs_4_.bottom_ref
  42.2 0.9 %absorb_last.1 = f32[8,4,128]{2,1,0:T(4,128)} custom-call(bf16[912,128]{1,0:T(8,128)(2,1)S(1)} %collective-permute-done.15.refs_3_.top_ref, bf16[912,128]{1,0:T(8,128)(2,1)S(1)} %collective-permute-done.16.refs_4_.bottom_ref, f32[1024,768]{1,0:T(8,128)S(1)} %get-tuple-element.58.refs_14_.eo_ref, f32[1024,1024]{1,0:T(8,128)S(1)} %get-tuple-element.59.refs_15_.rest_ref, ...), custom_call_target="tpu_custom_call" | custom-call | bytes 1000 | tf_op jit(solution)/shard_map/absorb_last/pallas_call | solution.py:290
  43.1 6.2 %all-to-all-start = ((f32[32,1,128]{2,1,0:T(1,128)}), f32[32,1,128]{2,1,0:T(1,128)S(1)}, u32[]{:S(2)}, u32[]{:S(2)}) async-start(f32[32,1,128]{2,1,0:T(1,128)} %bitcast.9), calls=%async_computation | async-start | bytes 32768 | tf_op jit(solution)/shard_map/all_to_all | solution.py:433
  49.3 0.0 copy-start
  49.3 6.7 %weight_grad.1 = bf16[1024,1792]{1,0:T(8,128)(2,1)} custom-call(f32[16,128]{1,0:T(8,128)S(1)} %get-tuple-element.60.own_ref, bf16[640,1792]{1,0:T(8,128)(2,1)} %get-tuple-element.61.early_ref, bf16[128,1792]{1,0:T(8,128)(2,1)S(1)} %scaled_rows.5.refs_0_, bf16[912,128]{1,0:T(8,128)(2,1)S(1)} %collective-permute-done.13.refs_11_.refs_1_, ...), custom_call_target="tpu_custom_call" | custom-call | bytes 1000 | tf_op jit(solution)/shard_map/weight_grad/pallas_call | solution.py:339
  56.0 0.4 all-to-all-done
  56.5 0.0 copy-done
  56.5 0.6 %pick_gate_grad.1 = f32[8,128]{1,0:T(8,128)} custom-call(f32[8,4,128]{2,1,0:T(4,128)S(1)} %bitcast.13, s32[8,128]{1,0:T(8,128)S(1)} %bitcast.15), custom_call_target="tpu_custom_call" | custom-call | tf_op jit(solution)/shard_map/pick_gate_grad/pallas_call | solution.py:368
Async XLA Ops:
  1.8 9.7 %collective-permute-start = (bf16[912,128]{1,0:T(8,128)(2,1)S(1)}, bf16[912,128]{1,0:T(8,128)(2,1)S(1)}, u32[]{:S(2)}, u32[]{:S(2)}) collective-permute-start(bf16[912,128]{1,0:T(8,128)(2,1)S(1)} %get-tuple-element.37.refs_0_), channel_id=1, source_target_pairs={{0,8},{8,16},{16,24},{24,28},{28,20},{20,12},{12,4},{4,0},{1,9},{9... | collective-permute-start | bytes 700424 | tf_op jit(solution)/shard_map/ppermute | solution.py:398
  4.9 8.6 %collective-permute-start.1 = (bf16[912,128]{1,0:T(8,128)(2,1)S(1)}, bf16[912,128]{1,0:T(8,128)(2,1)S(1)}, u32[]{:S(2)}, u32[]{:S(2)}) collective-permute-start(bf16[912,128]{1,0:T(8,128)(2,1)S(1)} %get-tuple-element.38.refs_1_), channel_id=1, source_target_pairs={{8,0},{16,8},{24,16},{28,24},{20,28},{12,20},{4,12},{0,4},{9,1},{1... | collective-permute-start | bytes 700424 | tf_op jit(solution)/shard_map/ppermute | solution.py:399
  4.9 11.4 %collective-permute-start.2 = (bf16[912,128]{1,0:T(8,128)(2,1)S(1)}, bf16[912,128]{1,0:T(8,128)(2,1)S(1)}, u32[]{:S(2)}, u32[]{:S(2)}) collective-permute-start(bf16[912,128]{1,0:T(8,128)(2,1)S(1)} %get-tuple-element.38.refs_1_), channel_id=1, source_target_pairs={{0,8},{8,16},{16,24},{24,28},{28,20},{20,12},{12,4},{4,0},{1,9},{9... | collective-permute-start | bytes 700424 | tf_op jit(solution)/shard_map/ppermute | solution.py:398
  6.9 11.6 %collective-permute-start.3 = (bf16[912,128]{1,0:T(8,128)(2,1)S(1)}, bf16[912,128]{1,0:T(8,128)(2,1)S(1)}, u32[]{:S(2)}, u32[]{:S(2)}) collective-permute-start(bf16[912,128]{1,0:T(8,128)(2,1)S(1)} %get-tuple-element.37.refs_0_), channel_id=1, source_target_pairs={{8,0},{16,8},{24,16},{28,24},{20,28},{12,20},{4,12},{0,4},{9,1},{1... | collective-permute-start | bytes 700424 | tf_op jit(solution)/shard_map/ppermute | solution.py:399
  9.5 18.5 %collective-permute-start.11 = (bf16[1024,256]{1,0:T(8,128)(2,1)S(1)}, bf16[1024,256]{1,0:T(8,128)(2,1)S(1)}, u32[]{:S(2)}, u32[]{:S(2)}) collective-permute-start(bf16[1024,256]{1,0:T(8,128)(2,1)S(1)} %get-tuple-element.43.refs_0_), channel_id=1, source_target_pairs={{0,2},{1,3},{2,0},{3,1},{4,6},{5,7},{6,4},{7,5},{8,10},{9,11},{10,... | collective-permute-start | bytes 1572872 | tf_op jit(solution)/shard_map/ppermute | solution.py:407
  13.5 8.6 %collective-permute-start.4 = (bf16[912,128]{1,0:T(8,128)(2,1)S(1)}, bf16[912,128]{1,0:T(8,128)(2,1)S(1)}, u32[]{:S(2)}, u32[]{:S(2)}) collective-permute-start(bf16[912,128]{1,0:T(8,128)(2,1)S(1)} %collective-permute-done.refs_2_), channel_id=1, source_target_pairs={{0,8},{8,16},{16,24},{24,28},{28,20},{20,12},{12,4},{4,0},{1,9},{9... | collective-permute-start | bytes 700424 | tf_op jit(solution)/shard_map/ppermute | solution.py:398
  15.1 8.6 %collective-permute-start.7 = (bf16[912,128]{1,0:T(8,128)(2,1)S(1)}, bf16[912,128]{1,0:T(8,128)(2,1)S(1)}, u32[]{:S(2)}, u32[]{:S(2)}) collective-permute-start(bf16[912,128]{1,0:T(8,128)(2,1)S(1)} %collective-permute-done.1.refs_5_), channel_id=1, source_target_pairs={{8,0},{16,8},{24,16},{28,24},{20,28},{12,20},{4,12},{0,4},{9,1},{1... | collective-permute-start | bytes 700424 | tf_op jit(solution)/shard_map/ppermute | solution.py:399
  16.3 9.4 %collective-permute-start.5 = (bf16[912,128]{1,0:T(8,128)(2,1)S(1)}, bf16[912,128]{1,0:T(8,128)(2,1)S(1)}, u32[]{:S(2)}, u32[]{:S(2)}) collective-permute-start(bf16[912,128]{1,0:T(8,128)(2,1)S(1)} %collective-permute-done.2.refs_3_), channel_id=1, source_target_pairs={{0,8},{8,16},{16,24},{24,28},{28,20},{20,12},{12,4},{4,0},{1,9},{9... | collective-permute-start | bytes 700424 | tf_op jit(solution)/shard_map/ppermute | solution.py:398
  18.5 9.4 %collective-permute-start.6 = (bf16[912,128]{1,0:T(8,128)(2,1)S(1)}, bf16[912,128]{1,0:T(8,128)(2,1)S(1)}, u32[]{:S(2)}, u32[]{:S(2)}) collective-permute-start(bf16[912,128]{1,0:T(8,128)(2,1)S(1)} %collective-permute-done.3.refs_4_), channel_id=1, source_target_pairs={{8,0},{16,8},{24,16},{28,24},{20,28},{12,20},{4,12},{0,4},{9,1},{1... | collective-permute-start | bytes 700424 | tf_op jit(solution)/shard_map/ppermute | solution.py:399
  22.2 7.4 %collective-permute-start.10 = (bf16[1024,256]{1,0:T(8,128)(2,1)S(1)}, bf16[1024,256]{1,0:T(8,128)(2,1)S(1)}, u32[]{:S(2)}, u32[]{:S(2)}) collective-permute-start(bf16[1024,256]{1,0:T(8,128)(2,1)S(1)} %get-tuple-element.43.refs_0_), channel_id=1, source_target_pairs={{0,1},{1,0},{2,3},{3,2},{4,5},{5,4},{6,7},{7,6},{8,9},{9,8},{10,11... | collective-permute-start | bytes 1572872 | tf_op jit(solution)/shard_map/ppermute | solution.py:408
  23.7 10.0 %collective-permute-start.8 = (bf16[912,128]{1,0:T(8,128)(2,1)S(1)}, bf16[912,128]{1,0:T(8,128)(2,1)S(1)}, u32[]{:S(2)}, u32[]{:S(2)}) collective-permute-start(bf16[912,128]{1,0:T(8,128)(2,1)S(1)} %collective-permute-done.4.refs_0_.refs_6_), channel_id=1, source_target_pairs={{0,8},{8,16},{16,24},{24,28},{28,20},{20,12},{12,4},{4,0},{1,9},{9... | collective-permute-start | bytes 700424 | tf_op jit(solution)/shard_map/ppermute | solution.py:398
  25.7 8.0 %collective-permute-start.9 = (bf16[912,128]{1,0:T(8,128)(2,1)S(1)}, bf16[912,128]{1,0:T(8,128)(2,1)S(1)}, u32[]{:S(2)}, u32[]{:S(2)}) collective-permute-start(bf16[912,128]{1,0:T(8,128)(2,1)S(1)} %collective-permute-done.7.refs_3_.refs_9_), channel_id=1, source_target_pairs={{8,0},{16,8},{24,16},{28,24},{20,28},{12,20},{4,12},{0,4},{9,1},{1... | collective-permute-start | bytes 700424 | tf_op jit(solution)/shard_map/ppermute | solution.py:399
  27.9 3.0 %collective-permute-start.12 = (bf16[1024,256]{1,0:T(8,128)(2,1)S(1)}, bf16[1024,256]{1,0:T(8,128)(2,1)S(1)}, u32[]{:S(2)}, u32[]{:S(2)}) collective-permute-start(bf16[1024,256]{1,0:T(8,128)(2,1)S(1)} %collective-permute-done.11.refs_2_), channel_id=1, source_target_pairs={{0,1},{1,0},{2,3},{3,2},{4,5},{5,4},{6,7},{7,6},{8,9},{9,8},{10,11... | collective-permute-start | bytes 1572872 | tf_op jit(solution)/shard_map/ppermute | solution.py:408
  28.9 10.1 %collective-permute-start.13 = (bf16[912,128]{1,0:T(8,128)(2,1)S(1)}, bf16[912,128]{1,0:T(8,128)(2,1)S(1)}, u32[]{:S(2)}, u32[]{:S(2)}) collective-permute-start(bf16[912,128]{1,0:T(8,128)(2,1)S(1)} %collective-permute-done.5.refs_1_.refs_7_), channel_id=1, source_target_pairs={{0,8},{8,16},{16,24},{24,28},{28,20},{20,12},{12,4},{4,0},{1,9},{9... | collective-permute-start | bytes 700424 | tf_op jit(solution)/shard_map/ppermute | solution.py:398
  29.6 9.4 %collective-permute-start.14 = (bf16[912,128]{1,0:T(8,128)(2,1)S(1)}, bf16[912,128]{1,0:T(8,128)(2,1)S(1)}, u32[]{:S(2)}, u32[]{:S(2)}) collective-permute-start(bf16[912,128]{1,0:T(8,128)(2,1)S(1)} %collective-permute-done.6.refs_2_.refs_8_), channel_id=1, source_target_pairs={{8,0},{16,8},{24,16},{28,24},{20,28},{12,20},{4,12},{0,4},{9,1},{1... | collective-permute-start | bytes 700424 | tf_op jit(solution)/shard_map/ppermute | solution.py:399
  34.5 7.6 %collective-permute-start.15 = (bf16[912,128]{1,0:T(8,128)(2,1)S(1)}, bf16[912,128]{1,0:T(8,128)(2,1)S(1)}, u32[]{:S(2)}, u32[]{:S(2)}) collective-permute-start(bf16[912,128]{1,0:T(8,128)(2,1)S(1)} %collective-permute-done.8.refs_10_.refs_0_), channel_id=1, source_target_pairs={{0,8},{8,16},{16,24},{24,28},{28,20},{20,12},{12,4},{4,0},{1,9},{9... | collective-permute-start | bytes 700424 | tf_op jit(solution)/shard_map/ppermute | solution.py:398
  35.3 6.9 %collective-permute-start.16 = (bf16[912,128]{1,0:T(8,128)(2,1)S(1)}, bf16[912,128]{1,0:T(8,128)(2,1)S(1)}, u32[]{:S(2)}, u32[]{:S(2)}) collective-permute-start(bf16[912,128]{1,0:T(8,128)(2,1)S(1)} %collective-permute-done.9.refs_13_.refs_1_), channel_id=1, source_target_pairs={{8,0},{16,8},{24,16},{28,24},{20,28},{12,20},{4,12},{0,4},{9,1},{1... | collective-permute-start | bytes 700424 | tf_op jit(solution)/shard_map/ppermute | solution.py:399
  43.1 13.4 %all-to-all-start = ((f32[32,1,128]{2,1,0:T(1,128)}), f32[32,1,128]{2,1,0:T(1,128)S(1)}, u32[]{:S(2)}, u32[]{:S(2)}) async-start(f32[32,1,128]{2,1,0:T(1,128)} %bitcast.9), calls=%async_computation | async-start | bytes 32768 | tf_op jit(solution)/shard_map/all_to_all | solution.py:433
  49.3 7.2 %copy-start = (s32[128,8]{0,1:T(8,128)S(1)}, s32[128,8]{0,1:T(8,128)}, u32[]{:S(2)}) copy-start(s32[128,8]{0,1:T(8,128)} %param.8) | copy-start | bytes 12292
